TPU v7x, 512 devices: a whole 4x8x8 slice. The times are simulated.
512 devices in a mesh: pb: 128 (over z, y, core), ka: 4 (over x).
Axes of the slice: x: 4, y: 8, z: 8, core: 2. Of those that a mesh axis runs over, the one named last changes fastest.
Arguments:
- queries: bfloat16 [32768, 1024], P('pb'), may hold values from -6 to 6
- keys: bfloat16 [32768, 128], P(('pb', 'ka')), may hold values from -6 to 6
- values: bfloat16 [32768, 128], P(('pb', 'ka')), may hold values from -6 to 6
- doc_lengths: int32 [8], replicated, may hold values from 1 to 24576, 32768 in all
Outputs:
- attended: bfloat16 [32768, 1024], P(('pb', 'ka'))
All inputs are finite; a program needn't handle non-finite values.
Results may differ from a plain program's by a relative error of at most 0.009.
Values may be sent and summed in bfloat16 or wider, within the bound.
A program may use at most 64 MiB of HBM per device.

v0:
```python
import jax
import jax.numpy as jnp
from jax import lax
from jax.sharding import PartitionSpec as P

QHEADS = 8
HEAD_DIM = 128


def joined(x, axis, combine):
    everything = jax.tree.map(lambda part: lax.all_gather(part, axis), x)
    leading = jax.tree.map(lambda part: part[0], everything)

    def step(k, so_far):
        return combine(so_far, jax.tree.map(lambda part: part[k], everything))

    return lax.fori_loop(1, lax.axis_size(axis), step, leading)


def per_device(queries, keys, values, doc_lengths):
    q_rows = queries.shape[0]
    tok_rows = keys.shape[0]
    lanes = lax.axis_size("ka")
    group_index = lax.axis_index("pb")
    lane_index = lax.axis_index("ka")
    head_count = QHEADS
    head_width = HEAD_DIM
    scaling = head_width ** (-0.5)
    doc_ends = jnp.cumsum(doc_lengths)

    def segment_of(where_at):
        return jnp.sum((where_at[:, None] >= doc_ends[None, :]).astype(jnp.int32), axis=1)

    q_pos = group_index * q_rows + jnp.arange(q_rows, dtype=jnp.int32)
    q_seg = segment_of(q_pos)
    q_heads = queries.reshape(q_rows, head_count, head_width)

    def attend(q_part, visible, key_block, value_block, state):
        running_max, totals, accumulated = state
        scores = (
            jnp.einsum("qhd,kd->qhk", q_part, key_block, preferred_element_type=jnp.float32)
            * scaling
        )
        scores = jnp.where(visible[:, None, :], scores, -1e30)
        new_max = jnp.maximum(running_max, jnp.max(scores, axis=-1))
        weights = jnp.where(visible[:, None, :], jnp.exp(scores - new_max[..., None]), 0.0)
        factor = jnp.exp(running_max - new_max)
        totals = totals * factor + jnp.sum(weights, axis=-1)
        accumulated = accumulated * factor[..., None] + jnp.einsum(
            "qhk,kd->qhd",
            weights.astype(jnp.bfloat16),
            value_block,
            preferred_element_type=jnp.float32,
        )
        return (new_max, totals, accumulated)

    def block_update(carried, key_block, value_block, key_pos):
        visible = (key_pos[None, :] <= q_pos[:, None]) & (
            segment_of(key_pos)[None, :] == q_seg[:, None]
        )
        return attend(q_heads, visible, key_block, value_block, carried)

    initial = (
        jnp.full((q_rows, head_count), -1e30, jnp.float32),
        jnp.zeros((q_rows, head_count), jnp.float32),
        jnp.zeros((q_rows, head_count, head_width), jnp.float32),
    )
    carried = initial
    key_piece = lax.all_gather(keys, "pb", axis=0, tiled=True)
    value_piece = lax.all_gather(values, "pb", axis=0, tiled=True)
    count_keys = key_piece.shape[0]
    gathered_index = jnp.arange(count_keys, dtype=jnp.int32)
    key_pos = (
        gathered_index // tok_rows * lanes + lane_index
    ) * tok_rows + gathered_index % tok_rows
    block_len = 128
    pieces = count_keys // block_len
    key_blocks = key_piece.reshape(pieces, block_len, head_width)
    value_blocks = value_piece.reshape(pieces, block_len, head_width)
    pos_blocks = key_pos.reshape(pieces, block_len)

    def scan_step(state, inputs):
        return (block_update(state, inputs[0], inputs[1], inputs[2]), None)

    carried, _ = lax.scan(scan_step, carried, (key_blocks, value_blocks, pos_blocks))
    running_max, totals, accumulated = carried

    def combine_pair(first, second):
        max_a, totals_a, acc_a = first
        max_b, totals_b, acc_b = second
        top_max = jnp.maximum(max_a, max_b)
        weight_a = jnp.exp(max_a - top_max)
        weight_b = jnp.exp(max_b - top_max)
        merged_acc = acc_a * weight_a[..., None] + acc_b * weight_b[..., None]
        return (top_max, totals_a * weight_a + totals_b * weight_b, merged_acc)

    whole_max, whole_totals, whole_acc = joined(
        (running_max, totals, accumulated), "ka", combine_pair
    )
    result = whole_acc / whole_totals[..., None]
    result = lax.dynamic_slice_in_dim(result, lane_index * tok_rows, tok_rows, 0)
    lane_rows = result.reshape(tok_rows, head_count * head_width).astype(jnp.bfloat16)
    return lane_rows


def solution(mesh):
    in_specs = (P("pb", None), P(("pb", "ka"), None), P(("pb", "ka"), None), P())
    out_specs = P(("pb", "ka"), None)
    return jax.shard_map(
        per_device, mesh=mesh, in_specs=in_specs, out_specs=out_specs, check_vma=False
    )
```

profile of v0, /device:TPU:1, one launch (start us, length us, event | category | flops | bytes accessed | tf_op | source)
XLA Modules:
  0.0 446.6 jit_solution(1175606188870625030)
XLA Ops:
  10.6 88.7 %all-gather.7.cloned.1.call-done = bf16[8192,128]{1,0:T(8,128)(2,1)} async-done(((bf16[64,128]{1,0:T(8,128)(2,1)}), bf16[8192,128]{1,0:T(8,128)(2,1)}) %all-gather.7.cloned.1.call-update) | async-done | bytes 2097168 | tf_op jit(solution)/shard_map/all_gather | solution.py:69
  99.3 83.0 %all-gather.9.cloned.1.call-done = bf16[8192,128]{1,0:T(8,128)(2,1)} async-done(((bf16[64,128]{1,0:T(8,128)(2,1)}), bf16[8192,128]{1,0:T(8,128)(2,1)}) %all-gather.9.cloned.1.call-update) | async-done | bytes 2097168 | tf_op jit(solution)/shard_map/all_gather | solution.py:70
  182.3 194.0 %while.35 = (s32[]{:T(128)}, f32[256,8]{0,1:T(8,128)S(1)}, f32[256,8]{0,1:T(8,128)S(1)}, f32[256,8,128]{2,0,1:T(8,128)S(1)}, s32[64,128]{1,0:T(8,128)S(1)}, /*in...) while((s32[]{:T(128)}, f32[256,8]{0,1:T(8,128)S(1)}, ...), condition=%wide.region_6.7_spmd.clone, body=%wide.region_2.6_spmd.clone.sunk | while | flops 137475200 | bytes 6102193 | solution.py:85
  183.8 1.5 convolution_add_fusion.2
  186.8 1.5 convolution_add_fusion.2
  189.9 1.5 convolution_add_fusion.2
  192.9 1.5 convolution_add_fusion.2
  195.9 1.5 convolution_add_fusion.2
  199.0 1.5 convolution_add_fusion.2
  202.0 1.5 convolution_add_fusion.2
  205.0 1.5 convolution_add_fusion.2
  208.1 1.5 convolution_add_fusion.2
  211.1 1.5 convolution_add_fusion.2
  214.1 1.5 convolution_add_fusion.2
  217.2 1.5 convolution_add_fusion.2
  223.2 1.5 convolution_add_fusion.2
  229.3 1.5 convolution_add_fusion.2
  235.3 1.5 convolution_add_fusion.2
  241.4 1.5 convolution_add_fusion.2
  247.5 1.5 convolution_add_fusion.2
  253.5 1.5 convolution_add_fusion.2
  259.6 1.5 convolution_add_fusion.2
  265.7 1.5 convolution_add_fusion.2
  271.7 1.5 convolution_add_fusion.2
  277.8 1.5 convolution_add_fusion.2
  283.8 1.5 convolution_add_fusion.2
  289.9 1.5 convolution_add_fusion.2
  296.0 1.5 convolution_add_fusion.2
  302.0 1.5 convolution_add_fusion.2
  308.1 1.5 convolution_add_fusion.2
  314.2 1.5 convolution_add_fusion.2
  320.2 1.5 convolution_add_fusion.2
  326.3 1.5 convolution_add_fusion.2
  332.4 1.5 convolution_add_fusion.2
  338.4 1.5 convolution_add_fusion.2
  344.5 1.5 convolution_add_fusion.2
  350.5 1.5 convolution_add_fusion.2
  356.6 1.5 convolution_add_fusion.2
  362.7 1.5 convolution_add_fusion.2
  368.7 1.5 convolution_add_fusion.2
  374.8 1.5 convolution_add_fusion.2
  377.3 9.6 %all-gather = f32[1024,8]{0,1:T(8,128)S(1)} all-gather(f32[256,8]{0,1:T(8,128)S(1)} %get-tuple-element.241), channel_id=2, replica_groups=mesh['pb'=128,'ka'=4] {'ka'}, dimensions={0}, use_global_device_ids=true | all-gather | bytes 40960 | tf_op jit(solution)/shard_map/all_gather | solution.py:11
  386.9 9.4 %all-gather.1 = f32[1024,8]{0,1:T(8,128)S(1)} all-gather(f32[256,8]{0,1:T(8,128)S(1)} %get-tuple-element.242), channel_id=3, replica_groups=mesh['pb'=128,'ka'=4] {'ka'}, dimensions={0}, use_global_device_ids=true | all-gather | bytes 40960 | tf_op jit(solution)/shard_map/all_gather | solution.py:11
  396.3 31.5 %all-gather.11.cloned.1.call-done = f32[1024,8,128]{2,0,1:T(8,128)} async-done(((f32[256,8,128]{2,0,1:T(8,128)}), f32[1024,8,128]{2,0,1:T(8,128)}) %all-gather.11.cloned.1.call-update) | async-done | bytes 4194320 | tf_op jit(solution)/shard_map/all_gather | solution.py:11
  429.6 9.5 %while.34 = (s32[]{:T(128)}, f32[256,8]{0,1:T(8,128)S(1)}, f32[256,8]{0,1:T(8,128)S(1)}, f32[256,8,128]{2,1,0:T(8,128)S(1)}, f32[4,256,8]{1,2,0:T(8,128)S(1)}, /...) while((s32[]{:T(128)}, f32[256,8]{0,1:T(8,128)S(1)}, ...), condition=%wide.region_8.9_spmd, body=%wide.region_7.8_spmd.sunk | while | flops 798725 | bytes 5357719 | solution.py:17
  431.2 1.5 fusion.46
  434.4 1.5 fusion.46
  437.6 1.5 fusion.46
  (640 shorter events, 146.1 us)
Async XLA Ops:
  6.5 92.8 %all-gather.7.cloned.1.call-start = ((), (), s32[]{:S(2)}) async-start(), calls=%async_computation | async-start | bytes 2113536 | tf_op jit(solution)/shard_map/all_gather | solution.py:69
  7.3 175.0 %all-gather.9.cloned.1.call-start = ((), (), s32[]{:S(2)}) async-start(), calls=%async_computation.1 | async-start | bytes 2113536 | tf_op jit(solution)/shard_map/all_gather | solution.py:70
  8.0 419.7 %all-gather.11.cloned.1.call-start = ((), (), s32[]{:S(2)}) async-start(), calls=%async_computation.2 | async-start | bytes 5242880 | tf_op jit(solution)/shard_map/all_gather | solution.py:11
  376.3 1.0 copy-start
  427.7 1.2 slice-start
Sparse Core Ops, SparseCore 0:
  10.5 88.7 all-gather.6
  102.4 79.8 all-gather.8
  377.4 50.2 all-gather.10
where the time goes:
time: 456 us; the launch traced here: 447 us
  waiting for transfers between devices  205 us (45%)
  matrix products  162 us (36%)
  other arithmetic  32.1 us (7%)
  blocking collectives  19 us (4%)
  between operations  13.2 us (3%)
  local copies, waits for them, and re-layouts  10.6 us (2%)
  loops' own time  5.31 us (1%)
    dot_general x64, matrix products, attend(): jnp.einsum('qhk,kd->qhd', weights.astype(jnp.bfloat16), value_block, pref...  93 us
    all_gather x1, waiting for transfers between devices, per_device(): key_piece = lax.all_gather(keys, 'pb', axis=0, tiled=True)  88.7 us
    all_gather x1, waiting for transfers between devices, per_device(): value_piece = lax.all_gather(values, 'pb', axis=0, tiled=True)  83 us
    dot_general x64, matrix products, attend(): jnp.einsum('qhd,kd->qhk', q_part, key_block, preferred_element_type=jnp.f...  68.8 us
    all_gather x1, waiting for transfers between devices, joined(): everything = jax.tree.map(lambda part: lax.all_gather(part, axis), x)  31.5 us
    all_gather x2, blocking collectives, joined(): everything = jax.tree.map(lambda part: lax.all_gather(part, axis), x)  19 us
    reduce_sum x64, other arithmetic, attend(): totals = totals * factor + jnp.sum(weights, axis=-1)  12.7 us
  transfers between devices with their start and end apart: 3, of which 3 were waited for; matrix products, arithmetic and copies ran while one was open for 1% of the time, Pallas kernels for 0%

commit v1 on v0

v1 whole, which is shorter than its diff:
```python
import functools
import math

import jax
import jax.numpy as jnp
from jax import lax
from jax.experimental import pallas as pl
from jax.experimental.pallas import tpu as pltpu
from jax.sharding import PartitionSpec as P

HEADS = 8
DIM = 128
DOCS = 8
MOST = 24576
LANES = 128
FACTOR = math.log2(math.e) / math.sqrt(DIM)
MASK = 131072.0
EMPTY = -65536.0
NOTHING = -1e30


def place(c, first, second):
    z = second * (1 - c) + first * c
    y = first * (1 - c) + second * c
    return z, y


def kernel(
    ring, lanes, q_ref, k_ref, v_ref, len_ref, out_ref,
    kv, kfeat, qcat, acc, tot, top, obuf, lbuf, rbuf, rlse,
    s_one, r_one, s_fwd, r_fwd, s_bwd, r_bwd, s_sib, r_sib, s_out, r_out, s_lse, r_lse,
):
    half = ring // 2
    rows = q_ref.shape[0]
    own = k_ref.shape[0]
    chunk = ring * own
    plane = ring * 2 * rows
    me = lax.axis_index("pb")
    x = lax.axis_index("ka")
    c = lax.rem(me, 2)
    z = me // (2 * ring)
    y = lax.rem(me // 2, ring)
    p1 = y * (1 - c) + z * c
    p2 = z * (1 - c) + y * c

    def wrap(value):
        return lax.rem(value + 2 * ring, ring)

    def device(first, second):
        zz, yy = place(c, wrap(first), wrap(second))
        return {"pb": (zz * ring + yy) * 2 + c}

    sibling = {"pb": me + 1 - 2 * c}

    barrier = pltpu.get_barrier_semaphore()
    partners = [device(p1 + d, p2) for d in range(1, ring)]
    partners += [device(p1, p2 + d) for d in ((1, ring - 1) if ring > 2 else (1,))]
    partners += [sibling]
    partners += [{"ka": lax.rem(x + d, lanes)} for d in range(1, lanes)]
    for partner in partners:
        pl.semaphore_signal(barrier, inc=1, device_id=partner, device_id_type=pl.DeviceIdType.MESH)
    kv[c, p2, p1, :, :DIM] = k_ref[...]
    kv[c, p2, p1, :, DIM:] = v_ref[...]
    pl.semaphore_wait(barrier, len(partners))

    def copy(ref, send, recv, where):
        return pltpu.make_async_remote_copy(
            src_ref=ref, dst_ref=ref, send_sem=send, recv_sem=recv,
            device_id=where, device_id_type=pl.DeviceIdType.MESH,
        )

    def one_copy(d, b1):
        return copy(kv.at[c, p2, wrap(b1)], s_one.at[d - 1], r_one.at[d - 1], device(p1 + d, p2))

    def piece(cc, b, part):
        if part is None:
            return kv.at[cc, wrap(b)]
        return kv.at[cc, wrap(b), pl.ds(part * half, half)]

    def fwd_copy(s, b, last):
        return copy(piece(c, b, 0 if last else None), s_fwd.at[s - 1], r_fwd.at[s - 1], device(p1, p2 + 1))

    def bwd_copy(s, b, last):
        return copy(piece(c, b, 1 if last else None), s_bwd.at[s - 1], r_bwd.at[s - 1], device(p1, p2 - 1))

    def sib_copy(n, cc, b, part):
        return copy(piece(cc, b, part), s_sib.at[n], r_sib.at[n], sibling)

    def ring_start(s, last):
        fwd_copy(s, p2 - s + 1, last).start()
        bwd_copy(s, p2 + s - 1, last).start()

    def ring_arrived(s, last):
        fwd_copy(s, p2 - s, last).wait_recv()
        sib_copy(2 * s - 1, c, p2 - s, 0 if last else None).start()
        bwd_copy(s, p2 + s, last).wait_recv()
        sib_copy(2 * s, c, p2 + s, 1 if last else None).start()

    def sib_arrived(s, last):
        sib_copy(2 * s - 1, 1 - c, p1 - s, 0 if last else None).wait_recv()
        sib_copy(2 * s, 1 - c, p1 + s, 1 if last else None).wait_recv()

    for d in range(1, ring):
        one_copy(d, p1).start()

    lane = lax.broadcasted_iota(jnp.int32, (1, LANES), 1)
    ends = jnp.zeros((1, LANES), jnp.int32)
    begins = jnp.zeros((1, LANES), jnp.int32)
    for j in range(DOCS):
        length = len_ref[j]
        ends += jnp.where(lane >= j, length, 0)
        begins += jnp.where(lane > j, length, 0)
    tok = lax.broadcasted_iota(jnp.int32, (rows, LANES), 0)
    col = lax.broadcasted_iota(jnp.int32, (rows, LANES), 1)
    pos = me * rows + tok
    hidden = jnp.where((col < DOCS) & ((pos < begins) | (pos >= ends)), -MASK, 0.0)
    hidden = jnp.where(col == DOCS, -MASK, hidden)
    first = col - 2 * DOCS
    later = (first >= 0) & (first < own) & (tok < x * own + first)
    hidden = jnp.where(later, -MASK, hidden).astype(jnp.bfloat16)
    for h in range(HEADS):
        qcat[h * rows : (h + 1) * rows, :DIM] = q_ref[:, h * DIM : (h + 1) * DIM]
        qcat[h * rows : (h + 1) * rows, DIM:] = hidden
    acc[...] = jnp.zeros_like(acc)
    tot[...] = jnp.zeros_like(tot)
    top[...] = jnp.full_like(top, EMPTY)

    def features(n, carry):
        cc, b = n // ring, lax.rem(n, ring)
        inner = lax.broadcasted_iota(jnp.int32, (own, LANES), 0)
        lanes_of = lax.broadcasted_iota(jnp.int32, (own, LANES), 1)
        for a in range(ring):
            zz, yy = place(cc, a, b)
            block = (zz * ring + yy) * 2 + cc
            at = block * rows + x * own + inner
            mark = ((at >= begins) & (at < ends)).astype(jnp.float32)
            mark = jnp.where((lanes_of == DOCS) & (block > me), 1.0, mark)
            mark = jnp.where((lanes_of == inner + 2 * DOCS) & (block == me), 1.0, mark)
            kfeat[cc, b, a * own : (a + 1) * own, :] = mark.astype(jnp.bfloat16)
        return carry

    lax.fori_loop(0, 2 * ring, features, 0)

    ones = jnp.ones((chunk, LANES), jnp.bfloat16)

    def scores(h, cc, b):
        q = qcat[h * rows : (h + 1) * rows, :]
        keys = jnp.concatenate([kv[cc, b, :, :, :DIM].reshape(chunk, DIM), kfeat[cc, b]], axis=1)
        return lax.dot_general(q, keys, (((1,), (1,)), ((), ())), preferred_element_type=jnp.float32)

    def fold(h, cc, b, s):
        at = slice(h * rows, (h + 1) * rows)
        old = top[at, :]
        new = jnp.maximum(old, jnp.max(s, axis=1, keepdims=True))
        wide = jnp.concatenate([new] * (chunk // LANES), axis=1)
        p = jnp.exp2((s - wide) * FACTOR).astype(jnp.bfloat16)
        vals = jnp.concatenate([kv[cc, b, :, :, DIM:].reshape(chunk, DIM), ones], axis=1)
        both = jnp.dot(p, vals, preferred_element_type=jnp.float32)
        alpha = jnp.exp2((old - new) * FACTOR)
        acc[at, :] = acc[at, :] * alpha + both[:, :DIM]
        tot[at, :] = tot[at, :] * alpha + both[:, DIM:]
        top[at, :] = new

    def needed(cc, b):
        seen = (b <= z) & ((b + 1) * plane > me * rows - (MOST - 1))
        return (cc == 1) | seen

    def unit(cc, b):
        @pl.when(needed(cc, b))
        def _():
            s = scores(0, cc, b)
            for h in range(HEADS):
                after = scores(h + 1, cc, b) if h + 1 < HEADS else None
                fold(h, cc, b, s)
                s = after

    def pair(cc, base, s):
        def body(i, carry):
            unit(cc, wrap(base + (2 * i - 1) * s))
            return carry

        lax.fori_loop(0, 2, body, 0)

    for d in range(1, ring):
        one_copy(d, p1 - d).wait_recv()
    ring_start(1, half == 1)
    sib_copy(0, c, p2, None).start()
    unit(c, p2)
    ring_arrived(1, half == 1)
    if half > 1:
        ring_start(2, half == 2)
    sib_copy(0, 1 - c, p1, None).wait_recv()
    unit(1 - c, p1)

    def step(s, carry):
        pair(c, p2, s)

        @pl.when(s + 1 < half)
        def _():
            ring_arrived(s + 1, False)

        @pl.when(s + 1 == half)
        def _():
            ring_arrived(s + 1, True)

        @pl.when(s + 2 < half)
        def _():
            ring_start(s + 2, False)

        @pl.when(s + 2 == half)
        def _():
            ring_start(s + 2, True)

        sib_arrived(s, False)
        pair(1 - c, p1, s)
        return carry

    lax.fori_loop(1, half, step, 0)
    sib_arrived(half, True)

    def out_copy(d, g):
        cols = pl.ds(g * 2 * DIM, 2 * DIM)
        return pltpu.make_async_remote_copy(
            src_ref=obuf.at[lax.rem(x + d, lanes), :, cols], dst_ref=rbuf.at[d, :, cols],
            send_sem=s_out.at[d, g], recv_sem=r_out.at[d, g],
            device_id={"ka": lax.rem(x + d, lanes)}, device_id_type=pl.DeviceIdType.MESH,
        )

    def lse_copy(d):
        return pltpu.make_async_remote_copy(
            src_ref=lbuf.at[lax.rem(x + d, lanes)], dst_ref=rlse.at[d],
            send_sem=s_lse.at[d], recv_sem=r_lse.at[d],
            device_id={"ka": lax.rem(x + d, lanes)}, device_id_type=pl.DeviceIdType.MESH,
        )

    last = ((c, wrap(p2 + half)), (1 - c, wrap(p1 + half)))
    logs = jnp.zeros((rows, LANES), jnp.float32)
    work = [(h, cc, b) for h in range(HEADS) for cc, b in last]
    s = scores(*work[0])
    for n, (h, cc, b) in enumerate(work):
        after = scores(*work[n + 1]) if n + 1 < len(work) else None
        fold(h, cc, b, s)
        s = after
        if n % 2 == 1:
            at = slice(h * rows, (h + 1) * rows)
            total = tot[at, :]
            some = total > 0.0
            safe = jnp.where(some, total, 1.0)
            part = (acc[at, :] / safe).astype(jnp.bfloat16)
            size = jnp.where(some, top[at, :] * FACTOR + jnp.log2(safe), NOTHING)
            logs = jnp.where(col == h, size, logs)
            for j in range(lanes):
                obuf[j, :, h * DIM : (h + 1) * DIM] = part[j * own : (j + 1) * own, :]
            if h % 2 == 1:
                for d in range(1, lanes):
                    out_copy(d, h // 2).start()
    for j in range(lanes):
        lbuf[j] = logs[j * own : (j + 1) * own, :]
    for d in range(1, lanes):
        lse_copy(d).start()
    for d in range(1, lanes):
        lse_copy(d).wait_recv()
    sizes = [lbuf[x]] + [rlse[d] for d in range(1, lanes)]
    highest = functools.reduce(jnp.maximum, sizes)
    shares = [jnp.exp2(size - highest) for size in sizes]
    whole = functools.reduce(jnp.add, shares)
    shares = [share / whole for share in shares]
    for g in range(HEADS // 2):
        for d in range(1, lanes):
            out_copy(d, g).wait_recv()
        for h in (2 * g, 2 * g + 1):
            cols = slice(h * DIM, (h + 1) * DIM)
            mixed = shares[0][:, h : h + 1] * obuf[x, :, cols].astype(jnp.float32)
            for d in range(1, lanes):
                mixed += shares[d][:, h : h + 1] * rbuf[d, :, cols].astype(jnp.float32)
            out_ref[:, cols] = mixed.astype(out_ref.dtype)

    for d in range(1, ring):
        one_copy(d, p1).wait_send()
    for s in range(1, half + 1):
        fwd_copy(s, p2 - s + 1, s == half).wait_send()
        bwd_copy(s, p2 + s - 1, s == half).wait_send()
        sib_copy(2 * s - 1, c, p2 - s, 0 if s == half else None).wait_send()
        sib_copy(2 * s, c, p2 + s, 1 if s == half else None).wait_send()
    sib_copy(0, c, p2, None).wait_send()
    for d in range(1, lanes):
        lse_copy(d).wait_send()
        for g in range(HEADS // 2):
            out_copy(d, g).wait_send()


def per_device(ring, lanes, queries, keys, values, doc_lengths):
    rows, own = queries.shape[0], keys.shape[0]
    half = ring // 2
    chunk = ring * own
    vmem = pl.BlockSpec(memory_space=pltpu.VMEM)
    sems = pltpu.SemaphoreType.DMA
    return pl.pallas_call(
        functools.partial(kernel, ring, lanes),
        out_shape=jax.ShapeDtypeStruct((own, HEADS * DIM), jnp.bfloat16),
        in_specs=[vmem, vmem, vmem, pl.BlockSpec(memory_space=pltpu.SMEM)],
        out_specs=vmem,
        scratch_shapes=[
            pltpu.VMEM((2, ring, ring, own, 2 * DIM), jnp.bfloat16),
            pltpu.VMEM((2, ring, chunk, LANES), jnp.bfloat16),
            pltpu.VMEM((HEADS * rows, 2 * DIM), jnp.bfloat16),
            pltpu.VMEM((HEADS * rows, LANES), jnp.float32),
            pltpu.VMEM((HEADS * rows, LANES), jnp.float32),
            pltpu.VMEM((HEADS * rows, LANES), jnp.float32),
            pltpu.VMEM((lanes, own, HEADS * DIM), jnp.bfloat16),
            pltpu.VMEM((lanes, own, LANES), jnp.float32),
            pltpu.VMEM((lanes, own, HEADS * DIM), jnp.bfloat16),
            pltpu.VMEM((lanes, own, LANES), jnp.float32),
            sems((ring - 1,)), sems((ring - 1,)),
            sems((half,)), sems((half,)), sems((half,)), sems((half,)),
            sems((2 * half + 1,)), sems((2 * half + 1,)),
            sems((lanes, HEADS // 2)), sems((lanes, HEADS // 2)),
            sems((lanes,)), sems((lanes,)),
        ],
        compiler_params=pltpu.CompilerParams(
            collective_id=0, has_side_effects=True, vmem_limit_bytes=48 * 1024 * 1024
        ),
        cost_estimate=pl.CostEstimate(flops=10**10, bytes_accessed=10**7, transcendentals=10**7),
        name="attend",
    )(queries, keys, values, doc_lengths)


def solution(mesh):
    ring = math.isqrt(mesh.shape["pb"] // 2)
    return jax.shard_map(
        functools.partial(per_device, ring, mesh.shape["ka"]),
        mesh=mesh,
        in_specs=(P("pb", None), P(("pb", "ka"), None), P(("pb", "ka"), None), P()),
        out_specs=P(("pb", "ka"), None),
        check_vma=False,
    )
```

time: 456 us -> 62.6 us (0.14)
  the two profiles are of different devices: /device:TPU:1 before, /device:TPU:32 now
where the time goes in v1:
time: 62.6 us; the launch traced here: 62.3 us
  Pallas kernels  58.5 us (93%)
  local copies, waits for them, and re-layouts  3.79 us (6%)
    pallas_call x1, Pallas kernels, per_device(): pl.pallas_call(functools.partial(kernel, ring, lanes), out_shape=jax.Shap...  58.5 us
    unnamed x9, local copies, waits for them, and re-layouts  3.79 us

profile of v1, /device:TPU:32, one launch (start us, length us, event | category | flops | bytes accessed | tf_op | source)
XLA Modules:
  0.0 62.3 jit_solution(3575238375525332694)
XLA Ops:
  0.0 0.0 copy-start
  0.0 1.0 %copy-done = bf16[256,1024]{1,0:T(8,128)(2,1)S(1)} copy-done((bf16[256,1024]{1,0:T(8,128)(2,1)S(1)}, bf16[256,1024]{1,0:T(8,128)(2,1)}, u32[]{:S(2)}) %copy-start) | copy-done | bytes 524312
  1.0 0.0 copy-start.1
  1.0 0.7 %copy-done.1 = bf16[64,128]{1,0:T(8,128)(2,1)S(1)} copy-done((bf16[64,128]{1,0:T(8,128)(2,1)S(1)}, bf16[64,128]{1,0:T(8,128)(2,1)}, u32[]{:S(2)}) %copy-start.1) | copy-done | bytes 16408
  1.8 0.0 copy-start.2
  1.8 0.7 %copy-done.2 = bf16[64,128]{1,0:T(8,128)(2,1)S(1)} copy-done((bf16[64,128]{1,0:T(8,128)(2,1)S(1)}, bf16[64,128]{1,0:T(8,128)(2,1)}, u32[]{:S(2)}) %copy-start.2) | copy-done | bytes 16408
  2.5 0.0 copy-start.3
  2.5 0.7 %copy-done.3 = s32[8]{0:T(128)S(1)} copy-done((s32[8]{0:T(128)S(1)}, s32[8]{0:T(128)}, u32[]{:S(2)}) %copy-start.3) | copy-done | bytes 56
  3.1 58.5 %attend.1 = bf16[64,1024]{1,0:T(8,128)(2,1)S(1)} custom-call(bf16[256,1024]{1,0:T(8,128)(2,1)S(1)} %copy-done, bf16[64,128]{1,0:T(8,128)(2,1)S(1)} %copy-done.1, bf16[64,128]{1,0:T(8,128)(2,1)S(1)} %copy-done.2, s32[8]{0:T(128)S(1)} %copy-done.3), custom_call_target="tpu_custom_call" | custom-call | flops 10000000000 | bytes 10000000 | tf_op jit(solution)/shard_map/attend/pallas_call | solution.py:298
  61.7 0.7 %copy.6 = bf16[64,1024]{1,0:T(8,128)(2,1)} copy(bf16[64,1024]{1,0:T(8,128)(2,1)S(1)} %attend.1) | data formatting | bytes 262144
Async XLA Ops:
  0.0 1.0 %copy-start = (bf16[256,1024]{1,0:T(8,128)(2,1)S(1)}, bf16[256,1024]{1,0:T(8,128)(2,1)}, u32[]{:S(2)}) copy-start(bf16[256,1024]{1,0:T(8,128)(2,1)} %q_ref.1) | copy-start | bytes 1572868
  1.0 0.7 %copy-start.1 = (bf16[64,128]{1,0:T(8,128)(2,1)S(1)}, bf16[64,128]{1,0:T(8,128)(2,1)}, u32[]{:S(2)}) copy-start(bf16[64,128]{1,0:T(8,128)(2,1)} %k_ref.1) | copy-start | bytes 49156
  1.8 0.7 %copy-start.2 = (bf16[64,128]{1,0:T(8,128)(2,1)S(1)}, bf16[64,128]{1,0:T(8,128)(2,1)}, u32[]{:S(2)}) copy-start(bf16[64,128]{1,0:T(8,128)(2,1)} %v_ref.1) | copy-start | bytes 49156
  2.5 0.7 %copy-start.3 = (s32[8]{0:T(128)S(1)}, s32[8]{0:T(128)}, u32[]{:S(2)}) copy-start(s32[8]{0:T(128)} %len_ref.1) | copy-start | bytes 100

commit v2 on v1

--- a/solution.py
+++ b/solution.py
@@ -26,13 +26,13 @@
 
 
 def kernel(
-    ring, lanes, q_ref, k_ref, v_ref, len_ref, out_ref,
-    kv, kfeat, qcat, acc, tot, top, obuf, lbuf, rbuf, rlse,
-    s_one, r_one, s_fwd, r_fwd, s_bwd, r_bwd, s_sib, r_sib, s_out, r_out, s_lse, r_lse,
+    ring, lanes, q_hbm, k_hbm, v_hbm, len_hbm, out_ref,
+    q_in, k_in, v_in, lens, stage, kv, kfeat, qcat, acc, tot, top, obuf, lbuf, rbuf, rlse,
+    s_in, s_one, r_one, s_fwd, r_fwd, s_bwd, r_bwd, s_sib, r_sib, s_out, r_out, s_lse, r_lse,
 ):
     half = ring // 2
-    rows = q_ref.shape[0]
-    own = k_ref.shape[0]
+    rows = q_in.shape[0]
+    own = k_in.shape[0]
     chunk = ring * own
     plane = ring * 2 * rows
     me = lax.axis_index("pb")
@@ -59,8 +59,16 @@
     partners += [{"ka": lax.rem(x + d, lanes)} for d in range(1, lanes)]
     for partner in partners:
         pl.semaphore_signal(barrier, inc=1, device_id=partner, device_id_type=pl.DeviceIdType.MESH)
-    kv[c, p2, p1, :, :DIM] = k_ref[...]
-    kv[c, p2, p1, :, DIM:] = v_ref[...]
+    moves = [
+        pltpu.make_async_copy(src, dst, s_in.at[n])
+        for n, (src, dst) in enumerate(((k_hbm, k_in), (v_hbm, v_in), (len_hbm, lens), (q_hbm, q_in)))
+    ]
+    for move in moves:
+        move.start()
+    moves[0].wait()
+    moves[1].wait()
+    stage[p1, :, :DIM] = k_in[...]
+    stage[p1, :, DIM:] = v_in[...]
     pl.semaphore_wait(barrier, len(partners))
 
     def copy(ref, send, recv, where):
@@ -70,12 +78,12 @@
         )
 
     def one_copy(d, b1):
-        return copy(kv.at[c, p2, wrap(b1)], s_one.at[d - 1], r_one.at[d - 1], device(p1 + d, p2))
+        return copy(stage.at[wrap(b1)], s_one.at[d - 1], r_one.at[d - 1], device(p1 + d, p2))
 
     def piece(cc, b, part):
         if part is None:
             return kv.at[cc, wrap(b)]
-        return kv.at[cc, wrap(b), pl.ds(part * half, half)]
+        return kv.at[cc, wrap(b), part]
 
     def fwd_copy(s, b, last):
         return copy(piece(c, b, 0 if last else None), s_fwd.at[s - 1], r_fwd.at[s - 1], device(p1, p2 + 1))
@@ -102,25 +110,32 @@
 
     for d in range(1, ring):
         one_copy(d, p1).start()
+    moves[2].wait()
+    moves[3].wait()
 
     lane = lax.broadcasted_iota(jnp.int32, (1, LANES), 1)
+    line = lax.broadcasted_iota(jnp.int32, (LANES, 1), 0)
     ends = jnp.zeros((1, LANES), jnp.int32)
     begins = jnp.zeros((1, LANES), jnp.int32)
+    ends_down = jnp.zeros((LANES, 1), jnp.int32)
+    begins_down = jnp.zeros((LANES, 1), jnp.int32)
     for j in range(DOCS):
-        length = len_ref[j]
+        length = lens[j]
         ends += jnp.where(lane >= j, length, 0)
         begins += jnp.where(lane > j, length, 0)
-    tok = lax.broadcasted_iota(jnp.int32, (rows, LANES), 0)
-    col = lax.broadcasted_iota(jnp.int32, (rows, LANES), 1)
+        ends_down += jnp.where(line >= j, length, 0)
+        begins_down += jnp.where(line > j, length, 0)
+    tok = lax.broadcasted_iota(jnp.int32, (LANES, rows), 1)
+    col = lax.broadcasted_iota(jnp.int32, (LANES, rows), 0)
     pos = me * rows + tok
-    hidden = jnp.where((col < DOCS) & ((pos < begins) | (pos >= ends)), -MASK, 0.0)
+    hidden = jnp.where((col < DOCS) & ((pos < begins_down) | (pos >= ends_down)), -MASK, 0.0)
     hidden = jnp.where(col == DOCS, -MASK, hidden)
     first = col - 2 * DOCS
     later = (first >= 0) & (first < own) & (tok < x * own + first)
     hidden = jnp.where(later, -MASK, hidden).astype(jnp.bfloat16)
     for h in range(HEADS):
-        qcat[h * rows : (h + 1) * rows, :DIM] = q_ref[:, h * DIM : (h + 1) * DIM]
-        qcat[h * rows : (h + 1) * rows, DIM:] = hidden
+        qcat[:DIM, h * rows : (h + 1) * rows] = q_in[:, h * DIM : (h + 1) * DIM].T
+        qcat[DIM:, h * rows : (h + 1) * rows] = hidden
     acc[...] = jnp.zeros_like(acc)
     tot[...] = jnp.zeros_like(tot)
     top[...] = jnp.full_like(top, EMPTY)
@@ -141,25 +156,22 @@
 
     lax.fori_loop(0, 2 * ring, features, 0)
 
-    ones = jnp.ones((chunk, LANES), jnp.bfloat16)
+    ones = jnp.ones((16, chunk), jnp.bfloat16)
 
     def scores(h, cc, b):
-        q = qcat[h * rows : (h + 1) * rows, :]
-        keys = jnp.concatenate([kv[cc, b, :, :, :DIM].reshape(chunk, DIM), kfeat[cc, b]], axis=1)
-        return lax.dot_general(q, keys, (((1,), (1,)), ((), ())), preferred_element_type=jnp.float32)
+        keys = jnp.concatenate([kv[cc, b, 0], kfeat[cc, b]], axis=1)
+        return jnp.dot(keys, qcat[:, h * rows : (h + 1) * rows], preferred_element_type=jnp.float32)
 
     def fold(h, cc, b, s):
-        at = slice(h * rows, (h + 1) * rows)
-        old = top[at, :]
-        new = jnp.maximum(old, jnp.max(s, axis=1, keepdims=True))
-        wide = jnp.concatenate([new] * (chunk // LANES), axis=1)
-        p = jnp.exp2((s - wide) * FACTOR).astype(jnp.bfloat16)
-        vals = jnp.concatenate([kv[cc, b, :, :, DIM:].reshape(chunk, DIM), ones], axis=1)
-        both = jnp.dot(p, vals, preferred_element_type=jnp.float32)
+        old = top[h : h + 1, :]
+        new = jnp.maximum(old, jnp.max(s, axis=0, keepdims=True))
+        p = jnp.exp2((s - new) * FACTOR).astype(jnp.bfloat16)
+        vals = jnp.concatenate([kv[cc, b, 1, n : n + LANES] for n in range(0, chunk, LANES)], axis=1)
+        both = jnp.dot(jnp.concatenate([vals, ones], axis=0), p, preferred_element_type=jnp.float32)
         alpha = jnp.exp2((old - new) * FACTOR)
-        acc[at, :] = acc[at, :] * alpha + both[:, :DIM]
-        tot[at, :] = tot[at, :] * alpha + both[:, DIM:]
-        top[at, :] = new
+        acc[h] = acc[h] * alpha + both[:DIM]
+        tot[h : h + 1, :] = tot[h : h + 1, :] * alpha + both[DIM : DIM + 1]
+        top[h : h + 1, :] = new
 
     def needed(cc, b):
         seen = (b <= z) & ((b + 1) * plane > me * rows - (MOST - 1))
@@ -183,6 +195,12 @@
 
     for d in range(1, ring):
         one_copy(d, p1 - d).wait_recv()
+    for n in range(ring):
+        kv[c, p2, 0, n * own : (n + 1) * own] = stage[n, :, :DIM]
+    side = LANES // own
+    for n in range(ring // side):
+        block = stage[n * side : (n + 1) * side, :, DIM:].reshape(LANES, DIM)
+        kv[c, p2, 1, n * LANES : (n + 1) * LANES] = block.T
     ring_start(1, half == 1)
     sib_copy(0, c, p2, None).start()
     unit(c, p2)
@@ -234,7 +252,7 @@
         )
 
     last = ((c, wrap(p2 + half)), (1 - c, wrap(p1 + half)))
-    logs = jnp.zeros((rows, LANES), jnp.float32)
+    logs = []
     work = [(h, cc, b) for h in range(HEADS) for cc, b in last]
     s = scores(*work[0])
     for n, (h, cc, b) in enumerate(work):
@@ -242,18 +260,18 @@
         fold(h, cc, b, s)
         s = after
         if n % 2 == 1:
-            at = slice(h * rows, (h + 1) * rows)
-            total = tot[at, :]
+            total = tot[h : h + 1, :]
             some = total > 0.0
             safe = jnp.where(some, total, 1.0)
-            part = (acc[at, :] / safe).astype(jnp.bfloat16)
-            size = jnp.where(some, top[at, :] * FACTOR + jnp.log2(safe), NOTHING)
-            logs = jnp.where(col == h, size, logs)
+            part = (acc[h] / safe).T.astype(jnp.bfloat16)
+            logs.append(jnp.where(some, top[h : h + 1, :] * FACTOR + jnp.log2(safe), NOTHING))
             for j in range(lanes):
                 obuf[j, :, h * DIM : (h + 1) * DIM] = part[j * own : (j + 1) * own, :]
             if h % 2 == 1:
                 for d in range(1, lanes):
                     out_copy(d, h // 2).start()
+    logs.append(jnp.zeros((LANES - HEADS, rows), jnp.float32))
+    logs = jnp.concatenate(logs, axis=0).T
     for j in range(lanes):
         lbuf[j] = logs[j * own : (j + 1) * own, :]
     for d in range(1, lanes):
@@ -298,19 +316,25 @@
     return pl.pallas_call(
         functools.partial(kernel, ring, lanes),
         out_shape=jax.ShapeDtypeStruct((own, HEADS * DIM), jnp.bfloat16),
-        in_specs=[vmem, vmem, vmem, pl.BlockSpec(memory_space=pltpu.SMEM)],
+        in_specs=[pl.BlockSpec(memory_space=pl.ANY)] * 4,
         out_specs=vmem,
         scratch_shapes=[
-            pltpu.VMEM((2, ring, ring, own, 2 * DIM), jnp.bfloat16),
+            pltpu.VMEM(queries.shape, jnp.bfloat16),
+            pltpu.VMEM(keys.shape, jnp.bfloat16),
+            pltpu.VMEM(values.shape, jnp.bfloat16),
+            pltpu.SMEM(doc_lengths.shape, jnp.int32),
+            pltpu.VMEM((ring, own, 2 * DIM), jnp.bfloat16),
+            pltpu.VMEM((2, ring, 2, chunk, DIM), jnp.bfloat16),
             pltpu.VMEM((2, ring, chunk, LANES), jnp.bfloat16),
-            pltpu.VMEM((HEADS * rows, 2 * DIM), jnp.bfloat16),
-            pltpu.VMEM((HEADS * rows, LANES), jnp.float32),
-            pltpu.VMEM((HEADS * rows, LANES), jnp.float32),
-            pltpu.VMEM((HEADS * rows, LANES), jnp.float32),
+            pltpu.VMEM((2 * DIM, HEADS * rows), jnp.bfloat16),
+            pltpu.VMEM((HEADS, DIM, rows), jnp.float32),
+            pltpu.VMEM((HEADS, rows), jnp.float32),
+            pltpu.VMEM((HEADS, rows), jnp.float32),
             pltpu.VMEM((lanes, own, HEADS * DIM), jnp.bfloat16),
             pltpu.VMEM((lanes, own, LANES), jnp.float32),
             pltpu.VMEM((lanes, own, HEADS * DIM), jnp.bfloat16),
             pltpu.VMEM((lanes, own, LANES), jnp.float32),
+            sems((4,)),
             sems((ring - 1,)), sems((ring - 1,)),
             sems((half,)), sems((half,)), sems((half,)), sems((half,)),
             sems((2 * half + 1,)), sems((2 * half + 1,)),

time: 62.6 us -> 63.8 us (1.019)
  Pallas kernels: 58.5 us -> 59.8 us
    pallas_call x1, Pallas kernels: 58.5 us -> 59.8 us  [per_device(): pl.pallas_call(functools.partial(kernel, ring, lanes), out_shape=jax.Shap...]
where the time goes in v2:
time: 63.8 us; the launch traced here: 63.6 us
  Pallas kernels  59.8 us (94%)
  local copies, waits for them, and re-layouts  3.79 us (6%)
    pallas_call x1, Pallas kernels, per_device(): pl.pallas_call(functools.partial(kernel, ring, lanes), out_shape=jax.Shap...  59.8 us
    unnamed x9, local copies, waits for them, and re-layouts  3.79 us

profile of v2, /device:TPU:32, one launch (start us, length us, event | category | flops | bytes accessed | tf_op | source)
XLA Modules:
  0.0 63.6 jit_solution(4658646344382657250)
XLA Ops:
  0.0 0.0 copy-start
  0.0 1.0 %copy-done = bf16[256,1024]{1,0:T(8,128)(2,1)S(1)} copy-done((bf16[256,1024]{1,0:T(8,128)(2,1)S(1)}, bf16[256,1024]{1,0:T(8,128)(2,1)}, u32[]{:S(2)}) %copy-start) | copy-done | bytes 524312
  1.0 0.0 copy-start.1
  1.0 0.7 %copy-done.1 = bf16[64,128]{1,0:T(8,128)(2,1)S(1)} copy-done((bf16[64,128]{1,0:T(8,128)(2,1)S(1)}, bf16[64,128]{1,0:T(8,128)(2,1)}, u32[]{:S(2)}) %copy-start.1) | copy-done | bytes 16408
  1.8 0.0 copy-start.2
  1.8 0.7 %copy-done.2 = bf16[64,128]{1,0:T(8,128)(2,1)S(1)} copy-done((bf16[64,128]{1,0:T(8,128)(2,1)S(1)}, bf16[64,128]{1,0:T(8,128)(2,1)}, u32[]{:S(2)}) %copy-start.2) | copy-done | bytes 16408
  2.5 0.0 copy-start.3
  2.5 0.7 %copy-done.3 = s32[8]{0:T(128)S(1)} copy-done((s32[8]{0:T(128)S(1)}, s32[8]{0:T(128)}, u32[]{:S(2)}) %copy-start.3) | copy-done | bytes 56
  3.1 59.8 %attend.1 = bf16[64,1024]{1,0:T(8,128)(2,1)S(1)} custom-call(bf16[256,1024]{1,0:T(8,128)(2,1)S(1)} %copy-done, bf16[64,128]{1,0:T(8,128)(2,1)S(1)} %copy-done.1, bf16[64,128]{1,0:T(8,128)(2,1)S(1)} %copy-done.2, s32[8]{0:T(128)S(1)} %copy-done.3), custom_call_target="tpu_custom_call" | custom-call | flops 10000000000 | bytes 10000000 | tf_op jit(solution)/shard_map/attend/pallas_call | solution.py:316
  62.9 0.7 %copy.6 = bf16[64,1024]{1,0:T(8,128)(2,1)} copy(bf16[64,1024]{1,0:T(8,128)(2,1)S(1)} %attend.1) | data formatting | bytes 262144
Async XLA Ops:
  0.0 1.0 %copy-start = (bf16[256,1024]{1,0:T(8,128)(2,1)S(1)}, bf16[256,1024]{1,0:T(8,128)(2,1)}, u32[]{:S(2)}) copy-start(bf16[256,1024]{1,0:T(8,128)(2,1)} %q_hbm.1) | copy-start | bytes 1572868
  1.0 0.7 %copy-start.1 = (bf16[64,128]{1,0:T(8,128)(2,1)S(1)}, bf16[64,128]{1,0:T(8,128)(2,1)}, u32[]{:S(2)}) copy-start(bf16[64,128]{1,0:T(8,128)(2,1)} %k_hbm.1) | copy-start | bytes 49156
  1.8 0.7 %copy-start.2 = (bf16[64,128]{1,0:T(8,128)(2,1)S(1)}, bf16[64,128]{1,0:T(8,128)(2,1)}, u32[]{:S(2)}) copy-start(bf16[64,128]{1,0:T(8,128)(2,1)} %v_hbm.1) | copy-start | bytes 49156
  2.5 0.7 %copy-start.3 = (s32[8]{0:T(128)S(1)}, s32[8]{0:T(128)}, u32[]{:S(2)}) copy-start(s32[8]{0:T(128)} %len_hbm.1) | copy-start | bytes 100

commit v3 on v2

v3 whole, which is shorter than its diff:
```python
import functools
import math

import jax
import jax.numpy as jnp
from jax import lax
from jax.experimental import pallas as pl
from jax.experimental.pallas import tpu as pltpu
from jax.sharding import PartitionSpec as P

HEADS = 8
DIM = 128
DOCS = 8
MOST = 24576
LANES = 128
FACTOR = math.log2(math.e) / math.sqrt(DIM)
MASK = 131072.0
EMPTY = -65536.0
NOTHING = -1e30
MESH = pl.DeviceIdType.MESH


def place(c, first, second):
    z = second * (1 - c) + first * c
    y = first * (1 - c) + second * c
    return z, y


def kernel(
    ring, lanes, q_hbm, k_hbm, v_hbm, len_hbm, out_ref,
    q_in, k_in, v_in, lens, stage, kv, kfeat, qcat, acc, tot, top, obuf, rbuf, logs, mixing,
    s_in, s_one, r_one, s_fwd, r_fwd, s_bwd, r_bwd, s_sib, r_sib, s_out, r_out, s_log, r_log,
):
    half = ring // 2
    rows = q_in.shape[0]
    own = k_in.shape[0]
    chunk = ring * own
    plane = ring * 2 * rows
    me = lax.axis_index("pb")
    x = lax.axis_index("ka")
    c = lax.rem(me, 2)
    z = me // (2 * ring)
    y = lax.rem(me // 2, ring)
    p1 = y * (1 - c) + z * c
    p2 = z * (1 - c) + y * c

    def wrap(value):
        return lax.rem(value + 2 * ring, ring)

    def device(first, second):
        zz, yy = place(c, wrap(first), wrap(second))
        return {"pb": (zz * ring + yy) * 2 + c}

    sibling = {"pb": me + 1 - 2 * c}

    barrier = pltpu.get_barrier_semaphore()
    partners = [device(p1 + d, p2) for d in range(1, ring)]
    partners += [device(p1, p2 + d) for d in ((1, ring - 1) if ring > 2 else (1,))]
    partners += [sibling]
    partners += [{"ka": lax.rem(x + d, lanes)} for d in range(1, lanes)]
    for partner in partners:
        pl.semaphore_signal(barrier, inc=1, device_id=partner, device_id_type=MESH)
    moves = [
        pltpu.make_async_copy(src, dst, s_in.at[n])
        for n, (src, dst) in enumerate(((k_hbm, k_in), (v_hbm, v_in), (len_hbm, lens), (q_hbm, q_in)))
    ]
    for move in moves:
        move.start()
    moves[0].wait()
    moves[1].wait()
    stage[p1, :, :DIM] = k_in[...]
    stage[p1, :, DIM:] = v_in[...]
    pl.semaphore_wait(barrier, len(partners))

    def copy(ref, send, recv, where):
        return pltpu.make_async_remote_copy(
            src_ref=ref, dst_ref=ref, send_sem=send, recv_sem=recv, device_id=where, device_id_type=MESH
        )

    def one_copy(d, b1):
        return copy(stage.at[wrap(b1)], s_one.at[d - 1], r_one.at[d - 1], device(p1 + d, p2))

    def piece(cc, b, p):
        return kv.at[cc, wrap(b), p // 2, pl.ds((p % 2) * (chunk // 2), chunk // 2)]

    def fwd_copy(s, b, p):
        return copy(piece(c, b, p), s_fwd.at[s - 1, p], r_fwd.at[s - 1, p], device(p1, p2 + 1))

    def bwd_copy(s, b, p):
        return copy(piece(c, b, p), s_bwd.at[s - 1, p], r_bwd.at[s - 1, p], device(p1, p2 - 1))

    def sib_copy(n, cc, b, p):
        return copy(piece(cc, b, p), s_sib.at[n, p], r_sib.at[n, p], sibling)

    def ring_arrived(s):
        for p in range(4):
            fwd_copy(s, p2 - s, p).wait_recv()
            onward = functools.partial(fwd_copy, s + 1, p2 - s, p)
            if p < 2:
                onward().start()
            else:
                pl.when(s + 1 < half)(lambda onward=onward: onward().start())
            sib_copy(2 * s - 1, c, p2 - s, p).start()
            bwd_copy(s, p2 + s, p).wait_recv()
            onward = functools.partial(bwd_copy, s + 1, p2 + s, p)
            if p >= 2:
                onward().start()
            else:
                pl.when(s + 1 < half)(lambda onward=onward: onward().start())
            sib_copy(2 * s, c, p2 + s, p).start()

    def ring_last():
        for p in range(2):
            fwd_copy(half, p2 - half, p).wait_recv()
            sib_copy(2 * half - 1, c, p2 - half, p).start()
            bwd_copy(half, p2 + half, p + 2).wait_recv()
            sib_copy(2 * half, c, p2 + half, p + 2).start()

    def sib_arrived(s):
        for p in range(4):
            sib_copy(2 * s - 1, 1 - c, p1 - s, p).wait_recv()
            sib_copy(2 * s, 1 - c, p1 + s, p).wait_recv()

    for d in range(1, ring):
        one_copy(d, p1).start()
    moves[2].wait()
    moves[3].wait()

    lane = lax.broadcasted_iota(jnp.int32, (1, LANES), 1)
    line = lax.broadcasted_iota(jnp.int32, (LANES, 1), 0)
    ends = jnp.zeros((1, LANES), jnp.int32)
    begins = jnp.zeros((1, LANES), jnp.int32)
    ends_down = jnp.zeros((LANES, 1), jnp.int32)
    begins_down = jnp.zeros((LANES, 1), jnp.int32)
    for j in range(DOCS):
        length = lens[j]
        ends += jnp.where(lane >= j, length, 0)
        begins += jnp.where(lane > j, length, 0)
        ends_down += jnp.where(line >= j, length, 0)
        begins_down += jnp.where(line > j, length, 0)
    tok = lax.broadcasted_iota(jnp.int32, (LANES, rows), 1)
    col = lax.broadcasted_iota(jnp.int32, (LANES, rows), 0)
    pos = me * rows + tok
    hidden = jnp.where((col < DOCS) & ((pos < begins_down) | (pos >= ends_down)), -MASK, 0.0)
    hidden = jnp.where(col == DOCS, -MASK, hidden)
    first = col - 2 * DOCS
    later = (first >= 0) & (first < own) & (tok < x * own + first)
    hidden = jnp.where(later, -MASK, hidden).astype(jnp.bfloat16)
    for h in range(HEADS):
        qcat[h, :DIM, :] = q_in[:, h * DIM : (h + 1) * DIM].T
        qcat[h, DIM:, :] = hidden
    acc[...] = jnp.zeros_like(acc)
    tot[...] = jnp.zeros_like(tot)
    top[...] = jnp.full_like(top, EMPTY)

    def features(n, carry):
        cc, b = n // ring, lax.rem(n, ring)
        inner = lax.broadcasted_iota(jnp.int32, (own, LANES), 0)
        lanes_of = lax.broadcasted_iota(jnp.int32, (own, LANES), 1)
        for a in range(ring):
            zz, yy = place(cc, a, b)
            block = (zz * ring + yy) * 2 + cc
            at = block * rows + x * own + inner
            mark = ((at >= begins) & (at < ends)).astype(jnp.float32)
            mark = jnp.where((lanes_of == DOCS) & (block > me), 1.0, mark)
            mark = jnp.where((lanes_of == inner + 2 * DOCS) & (block == me), 1.0, mark)
            kfeat[cc, b, a * own : (a + 1) * own, :] = mark.astype(jnp.bfloat16)
        return carry

    lax.fori_loop(0, 2 * ring, features, 0)

    ones = jnp.ones((16, chunk), jnp.bfloat16)

    def scores(h, cc, b):
        keys = jnp.concatenate([kv[cc, b, 0], kfeat[cc, b]], axis=1)
        return jnp.dot(keys, qcat[h], preferred_element_type=jnp.float32)

    def fold(h, cc, b, s):
        old = top[h]
        new = jnp.maximum(old, jnp.max(s, axis=0, keepdims=True))
        p = jnp.exp2((s - new) * FACTOR).astype(jnp.bfloat16)
        vals = jnp.concatenate([kv[cc, b, 1, n : n + LANES] for n in range(0, chunk, LANES)], axis=1)
        both = jnp.dot(jnp.concatenate([vals, ones], axis=0), p, preferred_element_type=jnp.float32)
        alpha = jnp.exp2((old - new) * FACTOR)
        acc[h] = acc[h] * alpha + both[:DIM]
        tot[h] = tot[h] * alpha + both[DIM : DIM + 1]
        top[h] = new

    def run(work):
        s = scores(*work[0])
        for n, item in enumerate(work):
            after = scores(*work[n + 1]) if n + 1 < len(work) else None
            fold(*item, s)
            s = after

    def needed(cc, b):
        seen = (b <= z) & ((b + 1) * plane > me * rows - (MOST - 1))
        return (cc == 1) | seen

    def unit(cc, b):
        @pl.when(needed(cc, b))
        def _():
            run([(h, cc, b) for h in range(HEADS)])

    for d in range(1, ring):
        one_copy(d, p1 - d).wait_recv()
    for n in range(ring):
        kv[c, p2, 0, n * own : (n + 1) * own] = stage[n, :, :DIM]
    for p in range(2):
        fwd_copy(1, p2, p).start()
        bwd_copy(1, p2, p).start()
        sib_copy(0, c, p2, p).start()
    side = LANES // own
    for n in range(ring // side):
        block = stage[n * side : (n + 1) * side, :, DIM:].reshape(LANES, DIM)
        kv[c, p2, 1, n * LANES : (n + 1) * LANES] = block.T
    for p in range(2, 4):
        fwd_copy(1, p2, p).start()
        bwd_copy(1, p2, p).start()
        sib_copy(0, c, p2, p).start()
    unit(c, p2)
    for p in range(4):
        sib_copy(0, 1 - c, p1, p).wait_recv()
    unit(1 - c, p1)
    ring_arrived(1)

    def step(s, carry):
        def mine(i, carry):
            unit(c, wrap(p2 + (2 * i - 1) * s))
            return carry

        def other(i, carry):
            unit(1 - c, wrap(p1 + (2 * i - 1) * s))

            @pl.when((s == half - 2) & (i == 0))
            def _():
                ring_last()

            return carry

        lax.fori_loop(0, 2, mine, 0)
        ring_arrived(s + 1)
        sib_arrived(s)
        lax.fori_loop(0, 2, other, 0)
        return carry

    lax.fori_loop(1, half - 1, step, 0)
    if half == 2:
        ring_last()
    sib_arrived(half - 1)
    for p in range(2):
        sib_copy(2 * half - 1, 1 - c, p1 - half, p).wait_recv()
        sib_copy(2 * half, 1 - c, p1 + half, p + 2).wait_recv()

    def peer(d):
        return lax.rem(x + d, lanes)

    def out_copy(d, h):
        cols = pl.ds(pl.multiple_of(h * DIM, DIM), DIM)
        return pltpu.make_async_remote_copy(
            src_ref=obuf.at[peer(d), :, cols], dst_ref=rbuf.at[d, :, cols],
            send_sem=s_out.at[d, h], recv_sem=r_out.at[d, h], device_id={"ka": peer(d)}, device_id_type=MESH,
        )

    def log_copy(d):
        return pltpu.make_async_remote_copy(
            src_ref=logs.at[0], dst_ref=logs.at[d],
            send_sem=s_log.at[d], recv_sem=r_log.at[d], device_id={"ka": peer(d)}, device_id_type=MESH,
        )

    late = [(c, p2 - half + 1), (c, p2 + half - 1), (1 - c, p1 - half + 1), (1 - c, p1 + half - 1)]
    late += [(c, p2 + half), (1 - c, p1 + half)]

    def finish(h, carry):
        run([(h, cc, wrap(b)) for cc, b in late])
        total = tot[h]
        some = total > 0.0
        safe = jnp.where(some, total, 1.0)
        part = (acc[h] / safe).T.astype(jnp.bfloat16)
        logs[0, h] = jnp.where(some, top[h] * FACTOR + jnp.log2(safe), NOTHING)
        cols = pl.ds(pl.multiple_of(h * DIM, DIM), DIM)
        for j in range(lanes):
            obuf[j, :, cols] = part[j * own : (j + 1) * own, :]
        for d in range(1, lanes):
            out_copy(d, h).start()
        return carry

    lax.fori_loop(0, HEADS, finish, 0)
    for d in range(1, lanes):
        log_copy(d).start()
    for d in range(1, lanes):
        log_copy(d).wait_recv()
    sizes = [jnp.concatenate([logs[d, h] for h in range(HEADS)], axis=0) for d in range(lanes)]
    highest = functools.reduce(jnp.maximum, sizes)
    shares = [jnp.exp2(size - highest) for size in sizes]
    whole = functools.reduce(jnp.add, shares)
    shares = [share / whole for share in shares]
    shares.append(jnp.zeros((LANES - HEADS * lanes, rows), jnp.float32))
    mixing[...] = jnp.concatenate(shares, axis=0).T
    mix = mixing[pl.ds(pl.multiple_of(x * own, own), own), :]
    for h in range(HEADS):
        cols = slice(h * DIM, (h + 1) * DIM)
        mixed = mix[:, h : h + 1] * obuf[x, :, cols].astype(jnp.float32)
        for d in range(1, lanes):
            out_copy(d, h).wait_recv()
            at = d * HEADS + h
            mixed += mix[:, at : at + 1] * rbuf[d, :, cols].astype(jnp.float32)
        out_ref[:, cols] = mixed.astype(out_ref.dtype)

    for d in range(1, ring):
        one_copy(d, p1).wait_send()
    for p in range(4):
        sib_copy(0, c, p2, p).wait_send()
    for s in range(1, half + 1):
        for p in range(4):
            if s < half or p < 2:
                fwd_copy(s, p2 - s + 1, p).wait_send()
                sib_copy(2 * s - 1, c, p2 - s, p).wait_send()
            if s < half or p >= 2:
                bwd_copy(s, p2 + s - 1, p).wait_send()
                sib_copy(2 * s, c, p2 + s, p).wait_send()
    for d in range(1, lanes):
        log_copy(d).wait_send()
        for h in range(HEADS):
            out_copy(d, h).wait_send()


def per_device(ring, lanes, queries, keys, values, doc_lengths):
    rows, own = queries.shape[0], keys.shape[0]
    half = ring // 2
    chunk = ring * own
    vmem = pl.BlockSpec(memory_space=pltpu.VMEM)
    sems = pltpu.SemaphoreType.DMA
    return pl.pallas_call(
        functools.partial(kernel, ring, lanes),
        out_shape=jax.ShapeDtypeStruct((own, HEADS * DIM), jnp.bfloat16),
        in_specs=[pl.BlockSpec(memory_space=pl.ANY)] * 4,
        out_specs=vmem,
        scratch_shapes=[
            pltpu.VMEM(queries.shape, jnp.bfloat16),
            pltpu.VMEM(keys.shape, jnp.bfloat16),
            pltpu.VMEM(values.shape, jnp.bfloat16),
            pltpu.SMEM(doc_lengths.shape, jnp.int32),
            pltpu.VMEM((ring, own, 2 * DIM), jnp.bfloat16),
            pltpu.VMEM((2, ring, 2, chunk, DIM), jnp.bfloat16),
            pltpu.VMEM((2, ring, chunk, LANES), jnp.bfloat16),
            pltpu.VMEM((HEADS, 2 * DIM, rows), jnp.bfloat16),
            pltpu.VMEM((HEADS, DIM, rows), jnp.float32),
            pltpu.VMEM((HEADS, 1, rows), jnp.float32),
            pltpu.VMEM((HEADS, 1, rows), jnp.float32),
            pltpu.VMEM((lanes, own, HEADS * DIM), jnp.bfloat16),
            pltpu.VMEM((lanes, own, HEADS * DIM), jnp.bfloat16),
            pltpu.VMEM((lanes, HEADS, 1, rows), jnp.float32),
            pltpu.VMEM((rows, LANES), jnp.float32),
            sems((4,)),
            sems((ring - 1,)), sems((ring - 1,)),
            sems((half, 4)), sems((half, 4)), sems((half, 4)), sems((half, 4)),
            sems((2 * half + 1, 4)), sems((2 * half + 1, 4)),
            sems((lanes, HEADS)), sems((lanes, HEADS)),
            sems((lanes,)), sems((lanes,)),
        ],
        compiler_params=pltpu.CompilerParams(
            collective_id=0, has_side_effects=True, vmem_limit_bytes=63 * 1024 * 1024
        ),
        cost_estimate=pl.CostEstimate(flops=10**10, bytes_accessed=10**7, transcendentals=10**7),
        name="attend",
    )(queries, keys, values, doc_lengths)


def solution(mesh):
    ring = math.isqrt(mesh.shape["pb"] // 2)
    return jax.shard_map(
        functools.partial(per_device, ring, mesh.shape["ka"]),
        mesh=mesh,
        in_specs=(P("pb", None), P(("pb", "ka"), None), P(("pb", "ka"), None), P()),
        out_specs=P(("pb", "ka"), None),
        check_vma=False,
    )
```

time: 63.8 us -> 67.8 us (1.063)
  the two profiles are of different devices: /device:TPU:32 before, /device:TPU:1 now
where the time goes in v3:
time: 67.8 us; the launch traced here: 67.6 us
  Pallas kernels  66.1 us (97%)
  local copies, waits for them, and re-layouts  1.57 us (2%)
    pallas_call x1, Pallas kernels, per_device(): pl.pallas_call(functools.partial(kernel, ring, lanes), out_shape=jax.Shap...  66.1 us
    unnamed x1, local copies, waits for them, and re-layouts  1.57 us

profile of v3, /device:TPU:1, one launch (start us, length us, event | category | flops | bytes accessed | tf_op | source)
XLA Modules:
  0.0 67.6 jit_solution(2358930709650002429)
XLA Ops:
  0.0 66.1 %attend.1 = bf16[64,1024]{1,0:T(8,128)(2,1)} custom-call(bf16[256,1024]{1,0:T(8,128)(2,1)} %q_hbm.1, bf16[64,128]{1,0:T(8,128)(2,1)} %k_hbm.1, bf16[64,128]{1,0:T(8,128)(2,1)} %v_hbm.1, s32[8]{0:T(128)} %len_hbm.1), custom_call_target="tpu_custom_call" | custom-call | flops 10000000000 | bytes 10000000 | tf_op jit(solution)/shard_map/attend/pallas_call | solution.py:334
  66.1 1.6 %copy.6 = bf16[64,1024]{1,0:T(8,128)(2,1)} copy(bf16[64,1024]{1,0:T(8,128)(2,1)} %attend.1) | data formatting | bytes 262144

commit v4 on v3

v4 whole, which is shorter than its diff:
```python
import functools
import math

import jax
import jax.numpy as jnp
from jax import lax
from jax.experimental import pallas as pl
from jax.experimental.pallas import tpu as pltpu
from jax.sharding import PartitionSpec as P

HEADS = 8
DIM = 128
DOCS = 8
MOST = 24576
LANES = 128
FACTOR = math.log2(math.e) / math.sqrt(DIM)
MASK = 131072.0
EMPTY = -65536.0
NOTHING = -1e30
EXTRA = 16
SAFE = 100.0
MESH = pl.DeviceIdType.MESH


def place(c, first, second):
    z = second * (1 - c) + first * c
    y = first * (1 - c) + second * c
    return z, y


def swift_kernel(
    ring, lanes, q_hbm, k_hbm, v_hbm, len_hbm, out_ref, bound_ref,
    q_in, k_in, v_in, lens, stage, kv, kfeat, qcat, acc, tot, obuf, rbuf, sums, mixing,
    s_in, s_one, r_one, s_fwd, r_fwd, s_bwd, r_bwd, s_sib, r_sib, s_out, r_out, s_sum, r_sum,
):
    half = ring // 2
    rows = q_in.shape[0]
    own = k_in.shape[0]
    chunk = ring * own
    plane = ring * 2 * rows
    me = lax.axis_index("pb")
    x = lax.axis_index("ka")
    c = lax.rem(me, 2)
    z = me // (2 * ring)
    y = lax.rem(me // 2, ring)
    p1 = y * (1 - c) + z * c
    p2 = z * (1 - c) + y * c

    def wrap(value):
        return lax.rem(value + 2 * ring, ring)

    def device(first, second):
        zz, yy = place(c, wrap(first), wrap(second))
        return {"pb": (zz * ring + yy) * 2 + c}

    sibling = {"pb": me + 1 - 2 * c}

    barrier = pltpu.get_barrier_semaphore()
    partners = [device(p1 + d, p2) for d in range(1, ring)]
    partners += [device(p1, p2 + d) for d in ((1, ring - 1) if ring > 2 else (1,))]
    partners += [sibling]
    partners += [{"ka": lax.rem(x + d, lanes)} for d in range(1, lanes)]
    for partner in partners:
        pl.semaphore_signal(barrier, inc=1, device_id=partner, device_id_type=MESH)
    moves = [
        pltpu.make_async_copy(src, dst, s_in.at[n])
        for n, (src, dst) in enumerate(((k_hbm, k_in), (v_hbm, v_in), (len_hbm, lens), (q_hbm, q_in)))
    ]
    for move in moves:
        move.start()
    moves[0].wait()
    moves[1].wait()
    stage[p1, :own, :DIM] = k_in[...]
    stage[p1, :own, DIM:] = v_in[...]
    wide = k_in[...].astype(jnp.float32)
    longest = jnp.max(jnp.sum(wide * wide, axis=1, keepdims=True), axis=0, keepdims=True)
    stage[p1, own:, :DIM] = jnp.broadcast_to(longest * 1.01, (EXTRA, DIM)).astype(jnp.bfloat16)
    moves[3].wait()
    longest = jnp.zeros((rows, 1), jnp.float32)
    for h in range(HEADS):
        wide = q_in[:, h * DIM : (h + 1) * DIM].astype(jnp.float32)
        longest = jnp.maximum(longest, jnp.sum(wide * wide, axis=1, keepdims=True))
    longest = jnp.max(longest, axis=0, keepdims=True)
    stage[p1, own:, DIM:] = jnp.broadcast_to(longest * 1.01, (EXTRA, DIM)).astype(jnp.bfloat16)
    pl.semaphore_wait(barrier, len(partners))

    def copy(ref, send, recv, where):
        return pltpu.make_async_remote_copy(
            src_ref=ref, dst_ref=ref, send_sem=send, recv_sem=recv, device_id=where, device_id_type=MESH
        )

    def one_copy(d, b1):
        return copy(stage.at[wrap(b1)], s_one.at[d - 1], r_one.at[d - 1], device(p1 + d, p2))

    def piece(cc, b, i, q):
        return kv.at[cc, wrap(b), i, pl.ds(q * (chunk // 2), chunk // 2 + q * EXTRA)]

    def fwd_copy(s, b, i, q):
        n = 2 * i + q
        return copy(piece(c, b, i, q), s_fwd.at[s - 1, n], r_fwd.at[s - 1, n], device(p1, p2 + 1))

    def bwd_copy(s, b, i, q):
        n = 2 * i + q
        return copy(piece(c, b, i, q), s_bwd.at[s - 1, n], r_bwd.at[s - 1, n], device(p1, p2 - 1))

    def sib_copy(k, cc, b, i, q):
        n = 2 * i + q
        return copy(piece(cc, b, i, q), s_sib.at[k, n], r_sib.at[k, n], sibling)

    def pass_on(s, i):
        both = s + 1 < half
        for q in range(2):
            fwd_copy(s, p2 - s, i, q).wait_recv()
            pl.when(both | (i == 0))(lambda q=q: fwd_copy(s + 1, p2 - s, i, q).start())
            bwd_copy(s, p2 + s, i, q).wait_recv()
            pl.when(both | (i == 1))(lambda q=q: bwd_copy(s + 1, p2 + s, i, q).start())
        for q in range(2):
            sib_copy(2 * s - 1, c, p2 - s, i, q).start()
            sib_copy(2 * s, c, p2 + s, i, q).start()

    def pass_last():
        for q in range(2):
            fwd_copy(half, p2 - half, 0, q).wait_recv()
            sib_copy(2 * half - 1, c, p2 - half, 0, q).start()
            bwd_copy(half, p2 + half, 1, q).wait_recv()
            sib_copy(2 * half, c, p2 + half, 1, q).start()

    def sib_arrived(s):
        for i in range(2):
            for q in range(2):
                sib_copy(2 * s - 1, 1 - c, p1 - s, i, q).wait_recv()
                sib_copy(2 * s, 1 - c, p1 + s, i, q).wait_recv()

    for d in range(1, ring):
        one_copy(d, p1).start()
    moves[2].wait()

    lane = lax.broadcasted_iota(jnp.int32, (1, LANES), 1)
    line = lax.broadcasted_iota(jnp.int32, (LANES, 1), 0)
    ends = jnp.zeros((1, LANES), jnp.int32)
    begins = jnp.zeros((1, LANES), jnp.int32)
    ends_down = jnp.zeros((LANES, 1), jnp.int32)
    begins_down = jnp.zeros((LANES, 1), jnp.int32)
    for j in range(DOCS):
        length = lens[j]
        ends += jnp.where(lane >= j, length, 0)
        begins += jnp.where(lane > j, length, 0)
        ends_down += jnp.where(line >= j, length, 0)
        begins_down += jnp.where(line > j, length, 0)
    tok = lax.broadcasted_iota(jnp.int32, (LANES, rows), 1)
    col = lax.broadcasted_iota(jnp.int32, (LANES, rows), 0)
    pos = me * rows + tok
    hidden = jnp.where((col < DOCS) & ((pos < begins_down) | (pos >= ends_down)), -MASK, 0.0)
    hidden = jnp.where(col == DOCS, -MASK, hidden)
    first = col - 2 * DOCS
    later = (first >= 0) & (first < own) & (tok < x * own + first)
    hidden = jnp.where(later, -MASK, hidden).astype(jnp.bfloat16)
    for h in range(HEADS):
        qcat[h, :DIM, :] = q_in[:, h * DIM : (h + 1) * DIM].T
        qcat[h, DIM:, :] = hidden
    acc[...] = jnp.zeros_like(acc)
    tot[...] = jnp.zeros_like(tot)

    def features(n, carry):
        cc, b = n // ring, lax.rem(n, ring)
        inner = lax.broadcasted_iota(jnp.int32, (own, LANES), 0)
        lanes_of = lax.broadcasted_iota(jnp.int32, (own, LANES), 1)
        for a in range(ring):
            zz, yy = place(cc, a, b)
            block = (zz * ring + yy) * 2 + cc
            at = block * rows + x * own + inner
            mark = ((at >= begins) & (at < ends)).astype(jnp.float32)
            mark = jnp.where((lanes_of == DOCS) & (block > me), 1.0, mark)
            mark = jnp.where((lanes_of == inner + 2 * DOCS) & (block == me), 1.0, mark)
            kfeat[cc, b, a * own : (a + 1) * own, :] = mark.astype(jnp.bfloat16)
        return carry

    lax.fori_loop(0, 2 * ring, features, 0)

    ones = jnp.ones((16, chunk), jnp.bfloat16)

    def scores(h, cc, b):
        keys = jnp.concatenate([kv[cc, b, 0, :chunk], kfeat[cc, b]], axis=1)
        return jnp.dot(keys, qcat[h], preferred_element_type=jnp.float32)

    def fold(h, cc, b, s):
        p = jnp.exp2(s * FACTOR).astype(jnp.bfloat16)
        vals = jnp.concatenate([kv[cc, b, 1, n : n + LANES] for n in range(0, chunk, LANES)], axis=1)
        both = jnp.dot(jnp.concatenate([vals, ones], axis=0), p, preferred_element_type=jnp.float32)
        acc[h] += both[:DIM]
        tot[h] += both[DIM : DIM + 1]

    def run(work):
        s = scores(*work[0])
        for n, item in enumerate(work):
            after = scores(*work[n + 1]) if n + 1 < len(work) else None
            fold(*item, s)
            s = after

    for d in range(1, ring):
        one_copy(d, p1 - d).wait_recv()
    for n in range(ring):
        kv[c, p2, 0, n * own : (n + 1) * own] = stage[n, :own, :DIM]
    largest = functools.reduce(jnp.maximum, [stage[n, own:, :] for n in range(ring)])
    kv[c, p2, 0, chunk:] = largest[:, :DIM]
    kv[c, p2, 1, chunk:] = largest[:, DIM:]
    for q in range(2):
        fwd_copy(1, p2, 0, q).start()
        bwd_copy(1, p2, 0, q).start()
    side = LANES // own
    for n in range(ring // side):
        block = stage[n * side : (n + 1) * side, :own, DIM:].reshape(LANES, DIM)
        kv[c, p2, 1, n * LANES : (n + 1) * LANES] = block.T
    for q in range(2):
        fwd_copy(1, p2, 1, q).start()
        bwd_copy(1, p2, 1, q).start()
    for i in range(2):
        for q in range(2):
            sib_copy(0, c, p2, i, q).start()

    def unit(u, carry):
        v = jnp.maximum(u - 2, 0)
        s = v // 4 + 1
        r = lax.rem(v, 4)
        early = u < 2
        mine = jnp.where(early, u == 0, r < 2)
        cc = jnp.where(mine, c, 1 - c)
        shift = jnp.where(early, 0, (2 * lax.rem(r, 2) - 1) * s)
        b = wrap(jnp.where(mine, p2, p1) + shift)

        @pl.when(u == 1)
        def _():
            for i in range(2):
                for q in range(2):
                    sib_copy(0, 1 - c, p1, i, q).wait_recv()

        @pl.when((u >= 2) & (r == 2))
        def _():
            sib_arrived(s)

        seen = (b <= z) & ((b + 1) * plane > me * rows - (MOST - 1))

        @pl.when((cc == 1) | seen)
        def _():
            run([(h, cc, b) for h in range(HEADS)])

        @pl.when(u < 2 * (half - 1))
        def _():
            pass_on(u // 2 + 1, lax.rem(u, 2))

        @pl.when(u == 2 * (half - 1))
        def _():
            pass_last()

        return carry

    units = 2 + 4 * (half - 2)
    lax.fori_loop(0, units, unit, 0)
    if units <= 2 * (half - 1):
        pass_last()
    sib_arrived(half - 1)
    for q in range(2):
        sib_copy(2 * half - 1, 1 - c, p1 - half, 0, q).wait_recv()
        sib_copy(2 * half, 1 - c, p1 + half, 1, q).wait_recv()

    def peer(d):
        return lax.rem(x + d, lanes)

    def out_copy(d, h):
        cols = pl.ds(pl.multiple_of(h * DIM, DIM), DIM)
        return pltpu.make_async_remote_copy(
            src_ref=obuf.at[peer(d), :, cols], dst_ref=rbuf.at[d, :, cols],
            send_sem=s_out.at[d, h], recv_sem=r_out.at[d, h], device_id={"ka": peer(d)}, device_id_type=MESH,
        )

    def sum_copy(d):
        return pltpu.make_async_remote_copy(
            src_ref=sums.at[0], dst_ref=sums.at[d],
            send_sem=s_sum.at[d], recv_sem=r_sum.at[d], device_id={"ka": peer(d)}, device_id_type=MESH,
        )

    late = [(c, p2 - half + 1), (c, p2 + half - 1), (1 - c, p1 - half + 1), (1 - c, p1 + half - 1)]
    late += [(c, p2 + half), (1 - c, p1 + half)]

    def finish(h, carry):
        run([(h, cc, wrap(b)) for cc, b in late])
        part = acc[h].T.astype(jnp.bfloat16)
        sums[0, h] = tot[h]
        cols = pl.ds(pl.multiple_of(h * DIM, DIM), DIM)
        for j in range(lanes):
            obuf[j, :, cols] = part[j * own : (j + 1) * own, :]
        for d in range(1, lanes):
            out_copy(d, h).start()
        return carry

    lax.fori_loop(0, HEADS, finish, 0)
    for i in range(2):
        met = [kv[cc, b, i, chunk:] for cc in range(2) for b in range(ring)]
        met = functools.reduce(jnp.maximum, met)[:1, :].astype(jnp.float32)
        sums[0, HEADS + i] = jnp.concatenate([met] * (rows // LANES), axis=1)
    for d in range(1, lanes):
        sum_copy(d).start()
    for d in range(1, lanes):
        sum_copy(d).wait_recv()
    whole = functools.reduce(jnp.add, [sums[d] for d in range(lanes)])
    share = [1.0 / whole[h] for h in range(HEADS)] + [jnp.zeros((LANES - HEADS, rows), jnp.float32)]
    mixing[...] = jnp.concatenate(share, axis=0).T
    met = functools.reduce(jnp.maximum, [sums[d] for d in range(lanes)])
    bound_ref[...] = jnp.broadcast_to((met[HEADS] * met[HEADS + 1])[:, :LANES], bound_ref.shape)
    mix = mixing[pl.ds(pl.multiple_of(x * own, own), own), :]
    for h in range(HEADS):
        cols = slice(h * DIM, (h + 1) * DIM)
        mixed = obuf[x, :, cols].astype(jnp.float32)
        for d in range(1, lanes):
            out_copy(d, h).wait_recv()
            mixed += rbuf[d, :, cols].astype(jnp.float32)
        out_ref[:, cols] = (mixed * mix[:, h : h + 1]).astype(out_ref.dtype)

    for d in range(1, ring):
        one_copy(d, p1).wait_send()
    for i in range(2):
        for q in range(2):
            sib_copy(0, c, p2, i, q).wait_send()
    for s in range(1, half + 1):
        for i in range(2):
            for q in range(2):
                if s < half or i == 0:
                    fwd_copy(s, p2 - s + 1, i, q).wait_send()
                    sib_copy(2 * s - 1, c, p2 - s, i, q).wait_send()
                if s < half or i == 1:
                    bwd_copy(s, p2 + s - 1, i, q).wait_send()
                    sib_copy(2 * s, c, p2 + s, i, q).wait_send()
    for d in range(1, lanes):
        sum_copy(d).wait_send()
        for h in range(HEADS):
            out_copy(d, h).wait_send()


def swift(ring, lanes, queries, keys, values, doc_lengths):
    rows, own = queries.shape[0], keys.shape[0]
    half = ring // 2
    chunk = ring * own
    vmem = pl.BlockSpec(memory_space=pltpu.VMEM)
    sems = pltpu.SemaphoreType.DMA
    parts = (lanes, own, HEADS * DIM)
    return pl.pallas_call(
        functools.partial(swift_kernel, ring, lanes),
        out_shape=(
            jax.ShapeDtypeStruct((own, HEADS * DIM), jnp.bfloat16),
            jax.ShapeDtypeStruct((8, LANES), jnp.float32),
        ),
        in_specs=[pl.BlockSpec(memory_space=pltpu.HBM)] * 4,
        out_specs=(vmem, vmem),
        scratch_shapes=[
            pltpu.VMEM(queries.shape, jnp.bfloat16),
            pltpu.VMEM(keys.shape, jnp.bfloat16),
            pltpu.VMEM(values.shape, jnp.bfloat16),
            pltpu.SMEM(doc_lengths.shape, jnp.int32),
            pltpu.VMEM((ring, own + EXTRA, 2 * DIM), jnp.bfloat16),
            pltpu.VMEM((2, ring, 2, chunk + EXTRA, DIM), jnp.bfloat16),
            pltpu.VMEM((2, ring, chunk, LANES), jnp.bfloat16),
            pltpu.VMEM((HEADS, 2 * DIM, rows), jnp.bfloat16),
            pltpu.VMEM((HEADS, DIM, rows), jnp.float32),
            pltpu.VMEM((HEADS, 1, rows), jnp.float32),
            pltpu.VMEM(parts, jnp.bfloat16),
            pltpu.VMEM(parts, jnp.bfloat16),
            pltpu.VMEM((lanes, HEADS + 2, 1, rows), jnp.float32),
            pltpu.VMEM((rows, LANES), jnp.float32),
            sems((4,)),
            sems((ring - 1,)), sems((ring - 1,)),
            sems((half, 4)), sems((half, 4)), sems((half, 4)), sems((half, 4)),
            sems((2 * half + 1, 4)), sems((2 * half + 1, 4)),
            sems((lanes, HEADS)), sems((lanes, HEADS)),
            sems((lanes,)), sems((lanes,)),
        ],
        compiler_params=pltpu.CompilerParams(
            collective_id=0, has_side_effects=True, vmem_limit_bytes=63 * 1024 * 1024
        ),
        cost_estimate=pl.CostEstimate(flops=10**10, bytes_accessed=10**7, transcendentals=10**7),
        name="swift",
    )(queries, keys, values, doc_lengths)


def where(ring):
    me = lax.axis_index("pb")
    x = lax.axis_index("ka")
    c = lax.rem(me, 2)
    z = me // (2 * ring)
    y = lax.rem(me // 2, ring)
    return me, x, c, z, y


def greet(partners):
    barrier = pltpu.get_barrier_semaphore()
    for partner in partners:
        pl.semaphore_signal(barrier, inc=1, device_id=partner, device_id_type=MESH)
    return lambda: pl.semaphore_wait(barrier, len(partners))


def gather_kernel(
    ring, k_ref, v_ref, kv, stage,
    s_one, r_one, s_fwd, r_fwd, s_bwd, r_bwd, s_sib, r_sib,
):
    half = ring // 2
    own = k_ref.shape[0]
    me, x, c, z, y = where(ring)
    p1 = y * (1 - c) + z * c
    p2 = z * (1 - c) + y * c

    def wrap(value):
        return lax.rem(value + 2 * ring, ring)

    def device(first, second):
        zz, yy = place(c, wrap(first), wrap(second))
        return {"pb": (zz * ring + yy) * 2 + c}

    sibling = {"pb": me + 1 - 2 * c}
    partners = [device(p1 + d, p2) for d in range(1, ring)]
    partners += [device(p1, p2 + d) for d in ((1, ring - 1) if ring > 2 else (1,))]
    ready = greet(partners + [sibling])
    stage[p1, :, :DIM] = k_ref[...]
    stage[p1, :, DIM:] = v_ref[...]
    ready()

    def copy(ref, send, recv, to):
        return pltpu.make_async_remote_copy(
            src_ref=ref, dst_ref=ref, send_sem=send, recv_sem=recv, device_id=to, device_id_type=MESH
        )

    def one_copy(d, b1):
        return copy(stage.at[wrap(b1)], s_one.at[d - 1], r_one.at[d - 1], device(p1 + d, p2))

    def piece(cc, b, p):
        size = ring * own // 2
        return kv.at[cc, wrap(b), p // 2, pl.ds((p % 2) * size, size)]

    def fwd_copy(s, b, p):
        return copy(piece(c, b, p), s_fwd.at[s - 1, p], r_fwd.at[s - 1, p], device(p1, p2 + 1))

    def bwd_copy(s, b, p):
        return copy(piece(c, b, p), s_bwd.at[s - 1, p], r_bwd.at[s - 1, p], device(p1, p2 - 1))

    def sib_copy(n, cc, b, p):
        return copy(piece(cc, b, p), s_sib.at[n, p], r_sib.at[n, p], sibling)

    def travels(s, p):
        return s < half or (s == half and p < 2), s < half or (s == half and p >= 2)

    for d in range(1, ring):
        one_copy(d, p1).start()
    for d in range(1, ring):
        one_copy(d, p1 - d).wait_recv()
    for n in range(ring):
        kv[c, p2, 0, n * own : (n + 1) * own] = stage[n, :, :DIM]
    side = LANES // own
    for n in range(ring // side):
        block = stage[n * side : (n + 1) * side, :, DIM:].reshape(LANES, DIM)
        kv[c, p2, 1, n * LANES : (n + 1) * LANES] = block.T
    for p in range(4):
        if travels(1, p)[0]:
            fwd_copy(1, p2, p).start()
        if travels(1, p)[1]:
            bwd_copy(1, p2, p).start()
    for p in range(4):
        sib_copy(0, c, p2, p).start()
    for s in range(1, half + 1):
        for p in range(4):
            if travels(s, p)[0]:
                fwd_copy(s, p2 - s, p).wait_recv()
                if travels(s + 1, p)[0]:
                    fwd_copy(s + 1, p2 - s, p).start()
            if travels(s, p)[1]:
                bwd_copy(s, p2 + s, p).wait_recv()
                if travels(s + 1, p)[1]:
                    bwd_copy(s + 1, p2 + s, p).start()
        for p in range(4):
            if travels(s, p)[0]:
                sib_copy(2 * s - 1, c, p2 - s, p).start()
            if travels(s, p)[1]:
                sib_copy(2 * s, c, p2 + s, p).start()
    for p in range(4):
        sib_copy(0, 1 - c, p1, p).wait_recv()
    for s in range(1, half + 1):
        for p in range(4):
            if travels(s, p)[0]:
                sib_copy(2 * s - 1, 1 - c, p1 - s, p).wait_recv()
            if travels(s, p)[1]:
                sib_copy(2 * s, 1 - c, p1 + s, p).wait_recv()
    for d in range(1, ring):
        one_copy(d, p1).wait_send()
    for p in range(4):
        sib_copy(0, c, p2, p).wait_send()
    for s in range(1, half + 1):
        for p in range(4):
            if travels(s, p)[0]:
                fwd_copy(s, p2 - s + 1, p).wait_send()
                sib_copy(2 * s - 1, c, p2 - s, p).wait_send()
            if travels(s, p)[1]:
                bwd_copy(s, p2 + s - 1, p).wait_send()
                sib_copy(2 * s, c, p2 + s, p).wait_send()


def attend_kernel(ring, lanes, q_ref, kv, lens, obuf, lbuf, kfeat, qcat, acc, tot, top):
    rows = q_ref.shape[0]
    own = rows // lanes
    chunk = ring * own
    plane = ring * 2 * rows
    me, x, c, z, y = where(ring)

    lane = lax.broadcasted_iota(jnp.int32, (1, LANES), 1)
    line = lax.broadcasted_iota(jnp.int32, (LANES, 1), 0)
    ends = jnp.zeros((1, LANES), jnp.int32)
    begins = jnp.zeros((1, LANES), jnp.int32)
    ends_down = jnp.zeros((LANES, 1), jnp.int32)
    begins_down = jnp.zeros((LANES, 1), jnp.int32)
    for j in range(DOCS):
        length = lens[j]
        ends += jnp.where(lane >= j, length, 0)
        begins += jnp.where(lane > j, length, 0)
        ends_down += jnp.where(line >= j, length, 0)
        begins_down += jnp.where(line > j, length, 0)
    tok = lax.broadcasted_iota(jnp.int32, (LANES, rows), 1)
    col = lax.broadcasted_iota(jnp.int32, (LANES, rows), 0)
    pos = me * rows + tok
    hidden = jnp.where((col < DOCS) & ((pos < begins_down) | (pos >= ends_down)), -MASK, 0.0)
    hidden = jnp.where(col == DOCS, -MASK, hidden)
    first = col - 2 * DOCS
    later = (first >= 0) & (first < own) & (tok < x * own + first)
    hidden = jnp.where(later, -MASK, hidden).astype(jnp.bfloat16)
    for h in range(HEADS):
        turned = q_ref[:, h * DIM : (h + 1) * DIM].T
        qcat[:DIM, h * rows : (h + 1) * rows] = turned
        qcat[DIM:, h * rows : (h + 1) * rows] = hidden
    acc[...] = jnp.zeros_like(acc)
    tot[...] = jnp.zeros_like(tot)
    top[...] = jnp.full_like(top, EMPTY)

    def features(n, carry):
        cc, b = n // ring, lax.rem(n, ring)
        inner = lax.broadcasted_iota(jnp.int32, (own, LANES), 0)
        lanes_of = lax.broadcasted_iota(jnp.int32, (own, LANES), 1)
        for a in range(ring):
            zz, yy = place(cc, a, b)
            block = (zz * ring + yy) * 2 + cc
            at = block * rows + x * own + inner
            mark = ((at >= begins) & (at < ends)).astype(jnp.float32)
            mark = jnp.where((lanes_of == DOCS) & (block > me), 1.0, mark)
            mark = jnp.where((lanes_of == inner + 2 * DOCS) & (block == me), 1.0, mark)
            kfeat[cc, b, a * own : (a + 1) * own, :] = mark.astype(jnp.bfloat16)
        return carry

    lax.fori_loop(0, 2 * ring, features, 0)
    ones = jnp.ones((16, chunk), jnp.bfloat16)

    def scores(h, cc, b):
        keys = jnp.concatenate([kv[cc, b, 0], kfeat[cc, b]], axis=1)
        return jnp.dot(keys, qcat[:, h * rows : (h + 1) * rows], preferred_element_type=jnp.float32)

    def weighted(cc, b, p):
        vals = jnp.concatenate([kv[cc, b, 1, n : n + LANES] for n in range(0, chunk, LANES)], axis=1)
        return jnp.dot(jnp.concatenate([vals, ones], axis=0), p, preferred_element_type=jnp.float32)

    def fold(h, cc, b, s):
        old = top[h : h + 1, :]
        new = jnp.maximum(old, jnp.max(s, axis=0, keepdims=True))
        both = weighted(cc, b, jnp.exp2((s - new) * FACTOR).astype(jnp.bfloat16))
        alpha = jnp.exp2((old - new) * FACTOR)
        acc[h] = acc[h] * alpha + both[:DIM]
        tot[h : h + 1, :] = tot[h : h + 1, :] * alpha + both[DIM : DIM + 1]
        top[h : h + 1, :] = new

    def sweep(fold):
        def body(n, carry):
            cc, b = n // ring, lax.rem(n, ring)
            seen = (b <= z) & ((b + 1) * plane > me * rows - (MOST - 1))

            @pl.when((cc == 1) | seen)
            def _():
                s = scores(0, cc, b)
                for h in range(HEADS):
                    after = scores(h + 1, cc, b) if h + 1 < HEADS else None
                    fold(h, cc, b, s)
                    s = after

            return carry

        lax.fori_loop(0, 2 * ring, body, 0)

    sweep(fold)
    logs = []
    for h in range(HEADS):
        total = tot[h : h + 1, :]
        some = total > 0.0
        safe = jnp.where(some, total, 1.0)
        part = (acc[h] / safe).T.astype(jnp.bfloat16)
        logs.append(jnp.where(some, top[h : h + 1, :] * FACTOR + jnp.log2(safe), NOTHING))
        for j in range(lanes):
            obuf[j, :, h * DIM : (h + 1) * DIM] = part[j * own : (j + 1) * own, :]
    lbuf[...] = jnp.concatenate(logs, axis=0)


def merge_kernel(lanes, obuf, lbuf, out_ref, rbuf, logs, mixing, relay, s_out, r_out, s_log, r_log, s_rel, r_rel):
    x = lax.axis_index("ka")
    own = out_ref.shape[0]
    rows = lbuf.shape[1]
    near = [d for d in range(1, lanes) if lanes != 4 or d != 2]

    def peer(d):
        return lax.rem(x + d, lanes)

    def copy(src, dst, send, recv, d):
        return pltpu.make_async_remote_copy(
            src_ref=src, dst_ref=dst, send_sem=send, recv_sem=recv, device_id={"ka": peer(d)}, device_id_type=MESH
        )

    def cols_of(g):
        return pl.ds(g * 2 * DIM, 2 * DIM)

    def out_copy(d, g):
        cols = cols_of(g)
        return copy(obuf.at[peer(d), :, cols], rbuf.at[d, :, cols], s_out.at[d, g], r_out.at[d, g], d)

    def way(g):
        return 1 if g < HEADS // 4 else 3

    def relay_copy(g):
        cols = cols_of(g)
        return copy(obuf.at[peer(2), :, cols], relay.at[:, cols], s_rel.at[g], r_rel.at[g], way(g))

    def onward_copy(g):
        cols = cols_of(g)
        return copy(relay.at[:, cols], rbuf.at[2, :, cols], s_out.at[2, g], r_out.at[2, g], way(g))

    def log_copy(d):
        return copy(lbuf, logs.at[d], s_log.at[d], r_log.at[d], d)

    greet([{"ka": peer(d)} for d in range(1, lanes)])()
    groups = range(HEADS // 2)
    for d in range(1, lanes):
        log_copy(d).start()
    if lanes == 4:
        for g in (0, 2, 1, 3):
            relay_copy(g).start()
    for g in groups:
        for d in near:
            out_copy(d, g).start()
    if lanes == 4:
        for g in (0, 2, 1, 3):
            relay_copy(g).wait_recv()
            onward_copy(g).start()
    for d in range(1, lanes):
        log_copy(d).wait_recv()
    sizes = [lbuf[...]] + [logs[d] for d in range(1, lanes)]
    highest = functools.reduce(jnp.maximum, sizes)
    shares = [jnp.exp2(size - highest) for size in sizes]
    whole = functools.reduce(jnp.add, shares)
    shares = [share / whole for share in shares]
    shares.append(jnp.zeros((LANES - HEADS * lanes, rows), jnp.float32))
    mixing[...] = jnp.concatenate(shares, axis=0).T
    mix = mixing[pl.ds(pl.multiple_of(x * own, own), own), :]
    for g in groups:
        for d in range(1, lanes):
            out_copy(d, g).wait_recv()
        for h in (2 * g, 2 * g + 1):
            cols = slice(h * DIM, (h + 1) * DIM)
            mixed = mix[:, h : h + 1] * obuf[x, :, cols].astype(jnp.float32)
            for d in range(1, lanes):
                at = d * HEADS + h
                mixed += mix[:, at : at + 1] * rbuf[d, :, cols].astype(jnp.float32)
            out_ref[:, cols] = mixed.astype(out_ref.dtype)
    for d in range(1, lanes):
        log_copy(d).wait_send()
    for g in groups:
        for d in near:
            out_copy(d, g).wait_send()
        if lanes == 4:
            relay_copy(g).wait_send()
            onward_copy(g).wait_send()


def steady(ring, lanes, queries, keys, values, doc_lengths):
    rows, own = queries.shape[0], keys.shape[0]
    half = ring // 2
    chunk = ring * own
    vmem = pl.BlockSpec(memory_space=pltpu.VMEM)
    sems = pltpu.SemaphoreType.DMA
    limit = 48 * 1024 * 1024
    kv = pl.pallas_call(
        functools.partial(gather_kernel, ring),
        out_shape=jax.ShapeDtypeStruct((2, ring, 2, chunk, DIM), jnp.bfloat16),
        in_specs=[vmem, vmem],
        out_specs=vmem,
        scratch_shapes=[
            pltpu.VMEM((ring, own, 2 * DIM), jnp.bfloat16),
            sems((ring - 1,)), sems((ring - 1,)),
            sems((half, 4)), sems((half, 4)), sems((half, 4)), sems((half, 4)),
            sems((2 * half + 1, 4)), sems((2 * half + 1, 4)),
        ],
        compiler_params=pltpu.CompilerParams(collective_id=1, has_side_effects=True, vmem_limit_bytes=limit),
        name="gather",
    )(keys, values)
    parts, logs = pl.pallas_call(
        functools.partial(attend_kernel, ring, lanes),
        out_shape=(
            jax.ShapeDtypeStruct((lanes, own, HEADS * DIM), jnp.bfloat16),
            jax.ShapeDtypeStruct((HEADS, rows), jnp.float32),
        ),
        in_specs=[vmem, vmem, pl.BlockSpec(memory_space=pltpu.SMEM)],
        out_specs=(vmem, vmem),
        scratch_shapes=[
            pltpu.VMEM((2, ring, chunk, LANES), jnp.bfloat16),
            pltpu.VMEM((2 * DIM, HEADS * rows), jnp.bfloat16),
            pltpu.VMEM((HEADS, DIM, rows), jnp.float32),
            pltpu.VMEM((HEADS, rows), jnp.float32),
            pltpu.VMEM((HEADS, rows), jnp.float32),
        ],
        compiler_params=pltpu.CompilerParams(vmem_limit_bytes=limit),
        name="attend",
    )(queries, kv, doc_lengths)
    return pl.pallas_call(
        functools.partial(merge_kernel, lanes),
        out_shape=jax.ShapeDtypeStruct((own, HEADS * DIM), jnp.bfloat16),
        in_specs=[vmem, vmem],
        out_specs=vmem,
        scratch_shapes=[
            pltpu.VMEM((lanes, own, HEADS * DIM), jnp.bfloat16),
            pltpu.VMEM((lanes, HEADS, rows), jnp.float32),
            pltpu.VMEM((rows, LANES), jnp.float32),
            pltpu.VMEM((own, HEADS * DIM), jnp.bfloat16),
            sems((lanes, HEADS // 2)), sems((lanes, HEADS // 2)),
            sems((lanes,)), sems((lanes,)),
            sems((HEADS // 2,)), sems((HEADS // 2,)),
        ],
        compiler_params=pltpu.CompilerParams(collective_id=2, has_side_effects=True, vmem_limit_bytes=limit),
        name="merge",
    )(parts, logs)


def per_device(ring, lanes, queries, keys, values, doc_lengths):
    args = (queries, keys, values, doc_lengths)
    out, bound = swift(ring, lanes, *args)
    fits = bound[0, 0] <= (SAFE / FACTOR) ** 2
    return lax.cond(fits, lambda *_: out, functools.partial(steady, ring, lanes), *args)


def solution(mesh):
    ring = math.isqrt(mesh.shape["pb"] // 2)
    return jax.shard_map(
        functools.partial(per_device, ring, mesh.shape["ka"]),
        mesh=mesh,
        in_specs=(P("pb", None), P(("pb", "ka"), None), P(("pb", "ka"), None), P()),
        out_specs=P(("pb", "ka"), None),
        check_vma=False,
    )
```

time: 67.8 us -> 130 us (1.92)
  the two profiles are of different devices: /device:TPU:1 before, /device:TPU:448 now
where the time goes in v4:
time: 130 us
  Pallas kernels  127 us (98%)
  local copies, waits for them, and re-layouts  1.86 us (1%)
    pallas_call x1, Pallas kernels, swift(): pl.pallas_call(functools.partial(swift_kernel, ring, lanes), out_shape=(j...  53.9 us
    pallas_call x1, Pallas kernels, steady(): pl.pallas_call(functools.partial(attend_kernel, ring, lanes), out_shape=(...  31 us
    pallas_call x1, Pallas kernels, steady(): pl.pallas_call(functools.partial(gather_kernel, ring), out_shape=jax.Shap...  30.6 us
    pallas_call x1, Pallas kernels, steady(): pl.pallas_call(functools.partial(merge_kernel, lanes), out_shape=jax.Shap...  11.9 us

profile of v4, /device:TPU:448, one launch (start us, length us, event | category | flops | bytes accessed | tf_op | source)
XLA Modules:
  0.0 130.0 jit_solution(1439977902220239063)
XLA Ops:
  0.0 0.0 copy-start
  0.0 0.0 copy-start.1
  0.0 0.0 copy-start.2
  0.0 0.0 copy-start.3
  0.0 53.9 %swift.1 = (bf16[64,1024]{1,0:T(8,128)(2,1)S(1)}, f32[8,128]{1,0:T(8,128)}) custom-call(bf16[256,1024]{1,0:T(8,128)(2,1)} %q_hbm.1, bf16[64,128]{1,0:T(8,128)(2,1)} %k_hbm.1, bf16[64,128]{1,0:T(8,128)(2,1)} %v_hbm.1, s32[8]{0:T(128)} %len_hbm.1), custom_call_target="tpu_custom_call" | custom-call | flops 10000000000 | bytes 10000000 | tf_op jit(solution)/shard_map/swift/pallas_call | solution.py:346
  54.0 1.2 slice.3
  55.8 0.0 copy-done
  55.8 0.0 copy-done.1
  55.8 0.0 copy-done.2
  55.8 0.0 copy-done.3
  55.8 73.5 %conditional.1 = (bf16[64,1024]{1,0:T(8,128)(2,1)S(1)}) conditional(s32[]{:T(128)} %bitcast, (bf16[64,128]{1,0:T(8,128)(2,1)S(1)}, bf16[64,128]{1,0:T(8,128)(2,1)S(1)}, bf16[256,1024]{1,0:T(8,128)(2,1)S(1)}, s32[8]{0:T(128)S(1)}) %tuple.20, bf16[64,1024]{1,0:T(8,128)(2,1)S(1)} %get-tuple-element.26), branch_computations={%region_0.0_spmd, %region_1.0_spmd} | conditional | bytes 8 | solution.py:743
  55.9 30.6 %gather.1.kv = bf16[2,8,2,512,128]{4,3,2,1,0:T(8,128)(2,1)S(1)} custom-call(bf16[64,128]{1,0:T(8,128)(2,1)S(1)} %get-tuple-element.18.k_ref, bf16[64,128]{1,0:T(8,128)(2,1)S(1)} %get-tuple-element.19.v_ref), custom_call_target="tpu_custom_call" | custom-call | tf_op jit(solution)/shard_map/cond/branch_0_fun/gather/pallas_call | solution.py:688
  86.5 31.0 %attend.1 = (bf16[4,64,1024]{2,1,0:T(8,128)(2,1)S(1)}, f32[8,256]{1,0:T(8,128)S(1)}) custom-call(bf16[256,1024]{1,0:T(8,128)(2,1)S(1)} %get-tuple-element.17.q_ref, bf16[2,8,2,512,128]{4,3,2,1,0:T(8,128)(2,1)S(1)} %gather.1.kv, s32[8]{0:T(128)S(1)} %get-tuple-element.20.lens), custom_call_target="tpu_custom_call" | custom-call | tf_op jit(solution)/shard_map/cond/branch_0_fun/attend/pallas_call | solution.py:702
  117.5 11.9 %merge.1 = bf16[64,1024]{1,0:T(8,128)(2,1)S(1)} custom-call(bf16[4,64,1024]{2,1,0:T(8,128)(2,1)S(1)} %get-tuple-element.21.obuf, f32[8,256]{1,0:T(8,128)S(1)} %get-tuple-element.22.lbuf), custom_call_target="tpu_custom_call" | custom-call | tf_op jit(solution)/shard_map/cond/branch_0_fun/merge/pallas_call | solution.py:720
  129.4 0.7 copy.10
Async XLA Ops:
  0.0 55.8 %copy-start = (bf16[256,1024]{1,0:T(8,128)(2,1)S(1)}, bf16[256,1024]{1,0:T(8,128)(2,1)}, u32[]{:S(2)}) copy-start(bf16[256,1024]{1,0:T(8,128)(2,1)} %q_hbm.1) | copy-start | bytes 1572868
  0.0 55.8 %copy-start.1 = (bf16[64,128]{1,0:T(8,128)(2,1)S(1)}, bf16[64,128]{1,0:T(8,128)(2,1)}, u32[]{:S(2)}) copy-start(bf16[64,128]{1,0:T(8,128)(2,1)} %k_hbm.1) | copy-start | bytes 49156
  0.0 55.8 %copy-start.2 = (bf16[64,128]{1,0:T(8,128)(2,1)S(1)}, bf16[64,128]{1,0:T(8,128)(2,1)}, u32[]{:S(2)}) copy-start(bf16[64,128]{1,0:T(8,128)(2,1)} %v_hbm.1) | copy-start | bytes 49156
  0.0 55.8 %copy-start.3 = (s32[8]{0:T(128)S(1)}, s32[8]{0:T(128)}, u32[]{:S(2)}) copy-start(s32[8]{0:T(128)} %len_hbm.1) | copy-start | bytes 100

commit v5 on v4

--- a/solution.py
+++ b/solution.py
@@ -36,30 +36,30 @@
     half = ring // 2
     rows = q_in.shape[0]
     own = k_in.shape[0]
-    chunk = ring * own
+    part = own // 2
+    side = ring * part
+    chunk = 2 * side
     plane = ring * 2 * rows
     me = lax.axis_index("pb")
     x = lax.axis_index("ka")
     c = lax.rem(me, 2)
     z = me // (2 * ring)
     y = lax.rem(me // 2, ring)
-    p1 = y * (1 - c) + z * c
-    p2 = z * (1 - c) + y * c
+    first, second = (y, z), (z, y)
+    classes = (0, 1)
 
     def wrap(value):
         return lax.rem(value + 2 * ring, ring)
 
-    def device(first, second):
-        zz, yy = place(c, wrap(first), wrap(second))
+    def device(cls, along_first, along_second):
+        zz, yy = place(cls, wrap(first[cls] + along_first), wrap(second[cls] + along_second))
         return {"pb": (zz * ring + yy) * 2 + c}
 
     sibling = {"pb": me + 1 - 2 * c}
 
     barrier = pltpu.get_barrier_semaphore()
-    partners = [device(p1 + d, p2) for d in range(1, ring)]
-    partners += [device(p1, p2 + d) for d in ((1, ring - 1) if ring > 2 else (1,))]
-    partners += [sibling]
-    partners += [{"ka": lax.rem(x + d, lanes)} for d in range(1, lanes)]
+    partners = [device(cls, d, 0) for cls in classes for d in range(1, ring)]
+    partners += [sibling] + [{"ka": lax.rem(x + d, lanes)} for d in range(1, lanes)]
     for partner in partners:
         pl.semaphore_signal(barrier, inc=1, device_id=partner, device_id_type=MESH)
     moves = [
@@ -70,18 +70,21 @@
         move.start()
     moves[0].wait()
     moves[1].wait()
-    stage[p1, :own, :DIM] = k_in[...]
-    stage[p1, :own, DIM:] = v_in[...]
     wide = k_in[...].astype(jnp.float32)
     longest = jnp.max(jnp.sum(wide * wide, axis=1, keepdims=True), axis=0, keepdims=True)
-    stage[p1, own:, :DIM] = jnp.broadcast_to(longest * 1.01, (EXTRA, DIM)).astype(jnp.bfloat16)
+    k_most = jnp.broadcast_to(longest * 1.01, (EXTRA, DIM)).astype(jnp.bfloat16)
     moves[3].wait()
     longest = jnp.zeros((rows, 1), jnp.float32)
     for h in range(HEADS):
         wide = q_in[:, h * DIM : (h + 1) * DIM].astype(jnp.float32)
         longest = jnp.maximum(longest, jnp.sum(wide * wide, axis=1, keepdims=True))
     longest = jnp.max(longest, axis=0, keepdims=True)
-    stage[p1, own:, DIM:] = jnp.broadcast_to(longest * 1.01, (EXTRA, DIM)).astype(jnp.bfloat16)
+    q_most = jnp.broadcast_to(longest * 1.01, (EXTRA, DIM)).astype(jnp.bfloat16)
+    for cls in classes:
+        stage[cls, first[cls], :part, :DIM] = k_in[cls * part : (cls + 1) * part]
+        stage[cls, first[cls], :part, DIM:] = v_in[cls * part : (cls + 1) * part]
+        stage[cls, first[cls], part:, :DIM] = k_most
+        stage[cls, first[cls], part:, DIM:] = q_most
     pl.semaphore_wait(barrier, len(partners))
 
     def copy(ref, send, recv, where):
@@ -89,50 +92,52 @@
             src_ref=ref, dst_ref=ref, send_sem=send, recv_sem=recv, device_id=where, device_id_type=MESH
         )
 
-    def one_copy(d, b1):
-        return copy(stage.at[wrap(b1)], s_one.at[d - 1], r_one.at[d - 1], device(p1 + d, p2))
-
-    def piece(cc, b, i, q):
-        return kv.at[cc, wrap(b), i, pl.ds(q * (chunk // 2), chunk // 2 + q * EXTRA)]
-
-    def fwd_copy(s, b, i, q):
-        n = 2 * i + q
-        return copy(piece(c, b, i, q), s_fwd.at[s - 1, n], r_fwd.at[s - 1, n], device(p1, p2 + 1))
-
-    def bwd_copy(s, b, i, q):
-        n = 2 * i + q
-        return copy(piece(c, b, i, q), s_bwd.at[s - 1, n], r_bwd.at[s - 1, n], device(p1, p2 - 1))
-
-    def sib_copy(k, cc, b, i, q):
-        n = 2 * i + q
-        return copy(piece(cc, b, i, q), s_sib.at[k, n], r_sib.at[k, n], sibling)
-
-    def pass_on(s, i):
-        both = s + 1 < half
-        for q in range(2):
-            fwd_copy(s, p2 - s, i, q).wait_recv()
-            pl.when(both | (i == 0))(lambda q=q: fwd_copy(s + 1, p2 - s, i, q).start())
-            bwd_copy(s, p2 + s, i, q).wait_recv()
-            pl.when(both | (i == 1))(lambda q=q: bwd_copy(s + 1, p2 + s, i, q).start())
-        for q in range(2):
-            sib_copy(2 * s - 1, c, p2 - s, i, q).start()
-            sib_copy(2 * s, c, p2 + s, i, q).start()
-
-    def pass_last():
-        for q in range(2):
-            fwd_copy(half, p2 - half, 0, q).wait_recv()
-            sib_copy(2 * half - 1, c, p2 - half, 0, q).start()
-            bwd_copy(half, p2 + half, 1, q).wait_recv()
-            sib_copy(2 * half, c, p2 + half, 1, q).start()
-
-    def sib_arrived(s):
-        for i in range(2):
-            for q in range(2):
-                sib_copy(2 * s - 1, 1 - c, p1 - s, i, q).wait_recv()
-                sib_copy(2 * s, 1 - c, p1 + s, i, q).wait_recv()
+    def one_copy(cls, d, at):
+        ref = stage.at[cls, wrap(at)]
+        return copy(ref, s_one.at[cls, d - 1], r_one.at[cls, d - 1], device(cls, d, 0))
+
+    def piece(cls, b, core, which):
+        if which is None:
+            return kv.at[cls, wrap(b), core]
+        return kv.at[cls, wrap(b), core, pl.ds(which * side, side + which * EXTRA)]
+
+    def fwd_copy(cls, s, b, last):
+        ref = piece(cls, b, c, 0 if last else None)
+        return copy(ref, s_fwd.at[cls, s - 1], r_fwd.at[cls, s - 1], device(cls, 0, 1))
+
+    def bwd_copy(cls, s, b, last):
+        ref = piece(cls, b, c, 1 if last else None)
+        return copy(ref, s_bwd.at[cls, s - 1], r_bwd.at[cls, s - 1], device(cls, 0, -1))
+
+    def sib_copy(cls, n, b, core, which):
+        return copy(piece(cls, b, core, which), s_sib.at[cls, n], r_sib.at[cls, n], sibling)
+
+    def pass_on(cls, s):
+        at = second[cls]
+        fwd_copy(cls, s, at - s, False).wait_recv()
+        pl.when(s + 1 < half)(lambda: fwd_copy(cls, s + 1, at - s, False).start())
+        pl.when(s + 1 == half)(lambda: fwd_copy(cls, s + 1, at - s, True).start())
+        bwd_copy(cls, s, at + s, False).wait_recv()
+        pl.when(s + 1 < half)(lambda: bwd_copy(cls, s + 1, at + s, False).start())
+        pl.when(s + 1 == half)(lambda: bwd_copy(cls, s + 1, at + s, True).start())
+        sib_copy(cls, 2 * s - 1, at - s, c, None).start()
+        sib_copy(cls, 2 * s, at + s, c, None).start()
+
+    def pass_last(cls):
+        at = second[cls]
+        fwd_copy(cls, half, at - half, True).wait_recv()
+        sib_copy(cls, 2 * half - 1, at - half, c, 0).start()
+        bwd_copy(cls, half, at + half, True).wait_recv()
+        sib_copy(cls, 2 * half, at + half, c, 1).start()
+
+    def sib_arrived(cls, s):
+        at = second[cls]
+        sib_copy(cls, 2 * s - 1, at - s, 1 - c, None).wait_recv()
+        sib_copy(cls, 2 * s, at + s, 1 - c, None).wait_recv()
 
     for d in range(1, ring):
-        one_copy(d, p1).start()
+        for cls in classes:
+            one_copy(cls, d, first[cls]).start()
     moves[2].wait()
 
     lane = lax.broadcasted_iota(jnp.int32, (1, LANES), 1)
@@ -152,8 +157,8 @@
     pos = me * rows + tok
     hidden = jnp.where((col < DOCS) & ((pos < begins_down) | (pos >= ends_down)), -MASK, 0.0)
     hidden = jnp.where(col == DOCS, -MASK, hidden)
-    first = col - 2 * DOCS
-    later = (first >= 0) & (first < own) & (tok < x * own + first)
+    inside = col - 2 * DOCS
+    later = (inside >= 0) & (inside < own) & (tok < x * own + inside)
     hidden = jnp.where(later, -MASK, hidden).astype(jnp.bfloat16)
     for h in range(HEADS):
         qcat[h, :DIM, :] = q_in[:, h * DIM : (h + 1) * DIM].T
@@ -162,31 +167,35 @@
     tot[...] = jnp.zeros_like(tot)
 
     def features(n, carry):
-        cc, b = n // ring, lax.rem(n, ring)
-        inner = lax.broadcasted_iota(jnp.int32, (own, LANES), 0)
-        lanes_of = lax.broadcasted_iota(jnp.int32, (own, LANES), 1)
-        for a in range(ring):
-            zz, yy = place(cc, a, b)
-            block = (zz * ring + yy) * 2 + cc
-            at = block * rows + x * own + inner
-            mark = ((at >= begins) & (at < ends)).astype(jnp.float32)
-            mark = jnp.where((lanes_of == DOCS) & (block > me), 1.0, mark)
-            mark = jnp.where((lanes_of == inner + 2 * DOCS) & (block == me), 1.0, mark)
-            kfeat[cc, b, a * own : (a + 1) * own, :] = mark.astype(jnp.bfloat16)
+        cls, b = n // ring, lax.rem(n, ring)
+        inner = lax.broadcasted_iota(jnp.int32, (part, LANES), 0) + cls * part
+        lanes_of = lax.broadcasted_iota(jnp.int32, (part, LANES), 1)
+        for core in range(2):
+            for a in range(ring):
+                zz, yy = place(cls, a, b)
+                block = (zz * ring + yy) * 2 + core
+                at = block * rows + x * own + inner
+                mark = ((at >= begins) & (at < ends)).astype(jnp.float32)
+                mark = jnp.where((lanes_of == DOCS) & (block > me), 1.0, mark)
+                mark = jnp.where((lanes_of == inner + 2 * DOCS) & (block == me), 1.0, mark)
+                row = core * side + a * part
+                kfeat[cls, b, row : row + part, :] = mark.astype(jnp.bfloat16)
         return carry
 
     lax.fori_loop(0, 2 * ring, features, 0)
 
     ones = jnp.ones((16, chunk), jnp.bfloat16)
 
-    def scores(h, cc, b):
-        keys = jnp.concatenate([kv[cc, b, 0, :chunk], kfeat[cc, b]], axis=1)
+    def scores(h, cls, b):
+        keys = jnp.concatenate([kv[cls, b, 0, :side], kv[cls, b, 1, :side]], axis=0)
+        keys = jnp.concatenate([keys, kfeat[cls, b]], axis=1)
         return jnp.dot(keys, qcat[h], preferred_element_type=jnp.float32)
 
-    def fold(h, cc, b, s):
+    def fold(h, cls, b, s):
         p = jnp.exp2(s * FACTOR).astype(jnp.bfloat16)
-        vals = jnp.concatenate([kv[cc, b, 1, n : n + LANES] for n in range(0, chunk, LANES)], axis=1)
-        both = jnp.dot(jnp.concatenate([vals, ones], axis=0), p, preferred_element_type=jnp.float32)
+        vals = [kv[cls, b, core, n : n + LANES] for core in range(2) for n in range(side, chunk, LANES)]
+        vals = jnp.concatenate([jnp.concatenate(vals, axis=1), ones], axis=0)
+        both = jnp.dot(vals, p, preferred_element_type=jnp.float32)
         acc[h] += both[:DIM]
         tot[h] += both[DIM : DIM + 1]
 
@@ -197,71 +206,68 @@
             fold(*item, s)
             s = after
 
-    for d in range(1, ring):
-        one_copy(d, p1 - d).wait_recv()
-    for n in range(ring):
-        kv[c, p2, 0, n * own : (n + 1) * own] = stage[n, :own, :DIM]
-    largest = functools.reduce(jnp.maximum, [stage[n, own:, :] for n in range(ring)])
-    kv[c, p2, 0, chunk:] = largest[:, :DIM]
-    kv[c, p2, 1, chunk:] = largest[:, DIM:]
-    for q in range(2):
-        fwd_copy(1, p2, 0, q).start()
-        bwd_copy(1, p2, 0, q).start()
-    side = LANES // own
-    for n in range(ring // side):
-        block = stage[n * side : (n + 1) * side, :own, DIM:].reshape(LANES, DIM)
-        kv[c, p2, 1, n * LANES : (n + 1) * LANES] = block.T
-    for q in range(2):
-        fwd_copy(1, p2, 1, q).start()
-        bwd_copy(1, p2, 1, q).start()
-    for i in range(2):
-        for q in range(2):
-            sib_copy(0, c, p2, i, q).start()
+    per = LANES // part
+    lower = lax.broadcasted_iota(jnp.int32, (EXTRA, DIM), 0) < EXTRA // 2
+    for cls in classes:
+        at = second[cls]
+        for d in range(1, ring):
+            one_copy(cls, d, first[cls] - d).wait_recv()
+        for n in range(ring):
+            kv[cls, at, c, n * part : (n + 1) * part] = stage[cls, n, :part, :DIM]
+        for n in range(ring // per):
+            block = stage[cls, n * per : (n + 1) * per, :part, DIM:].reshape(LANES, DIM)
+            kv[cls, at, c, side + n * LANES : side + (n + 1) * LANES] = block.T
+        largest = functools.reduce(jnp.maximum, [stage[cls, n, part:, :] for n in range(ring)])
+        kv[cls, at, c, chunk:] = jnp.where(lower, largest[:, :DIM], largest[:, DIM:])
+        fwd_copy(cls, 1, at, half == 1).start()
+        bwd_copy(cls, 1, at, half == 1).start()
+        sib_copy(cls, 0, at, c, None).start()
 
     def unit(u, carry):
         v = jnp.maximum(u - 2, 0)
         s = v // 4 + 1
         r = lax.rem(v, 4)
         early = u < 2
-        mine = jnp.where(early, u == 0, r < 2)
-        cc = jnp.where(mine, c, 1 - c)
+        cls = jnp.where(early, u, r // 2)
         shift = jnp.where(early, 0, (2 * lax.rem(r, 2) - 1) * s)
-        b = wrap(jnp.where(mine, p2, p1) + shift)
-
-        @pl.when(u == 1)
+        b = wrap(jnp.where(cls == 0, z, y) + shift)
+        for k in classes:
+
+            @pl.when(u == k)
+            def _(k=k):
+                sib_copy(k, 0, second[k], 1 - c, None).wait_recv()
+
+            @pl.when((u >= 2) & (r == 2 * k))
+            def _(k=k):
+                sib_arrived(k, s)
+
+        seen = (b <= z) & ((b + 1) * plane > me * rows - (MOST - 1))
+
+        @pl.when((cls == 1) | seen)
         def _():
-            for i in range(2):
-                for q in range(2):
-                    sib_copy(0, 1 - c, p1, i, q).wait_recv()
-
-        @pl.when((u >= 2) & (r == 2))
-        def _():
-            sib_arrived(s)
-
-        seen = (b <= z) & ((b + 1) * plane > me * rows - (MOST - 1))
-
-        @pl.when((cc == 1) | seen)
-        def _():
-            run([(h, cc, b) for h in range(HEADS)])
-
-        @pl.when(u < 2 * (half - 1))
-        def _():
-            pass_on(u // 2 + 1, lax.rem(u, 2))
-
-        @pl.when(u == 2 * (half - 1))
-        def _():
-            pass_last()
+            run([(h, cls, b) for h in range(HEADS)])
+
+        for k in classes:
+
+            @pl.when((u < 2 * (half - 1)) & (lax.rem(u, 2) == k))
+            def _(k=k):
+                pass_on(k, u // 2 + 1)
+
+            @pl.when(u == 2 * (half - 1) + k)
+            def _(k=k):
+                pass_last(k)
 
         return carry
 
     units = 2 + 4 * (half - 2)
     lax.fori_loop(0, units, unit, 0)
-    if units <= 2 * (half - 1):
-        pass_last()
-    sib_arrived(half - 1)
-    for q in range(2):
-        sib_copy(2 * half - 1, 1 - c, p1 - half, 0, q).wait_recv()
-        sib_copy(2 * half, 1 - c, p1 + half, 1, q).wait_recv()
+    for cls in classes:
+        if units <= 2 * (half - 1) + cls:
+            pass_last(cls)
+    for cls in classes:
+        sib_arrived(cls, half - 1)
+        sib_copy(cls, 2 * half - 1, second[cls] - half, 1 - c, 0).wait_recv()
+        sib_copy(cls, 2 * half, second[cls] + half, 1 - c, 1).wait_recv()
 
     def peer(d):
         return lax.rem(x + d, lanes)
@@ -279,27 +285,39 @@
             send_sem=s_sum.at[d], recv_sem=r_sum.at[d], device_id={"ka": peer(d)}, device_id_type=MESH,
         )
 
-    late = [(c, p2 - half + 1), (c, p2 + half - 1), (1 - c, p1 - half + 1), (1 - c, p1 + half - 1)]
-    late += [(c, p2 + half), (1 - c, p1 + half)]
+    late = [(cls, second[cls] + sign * (half - 1)) for cls in classes for sign in (-1, 1)]
+    late += [(cls, second[cls] + half) for cls in classes]
 
     def finish(h, carry):
-        run([(h, cc, wrap(b)) for cc, b in late])
-        part = acc[h].T.astype(jnp.bfloat16)
+        run([(h, cls, wrap(b)) for cls, b in late])
+        turned = acc[h].T.astype(jnp.bfloat16)
         sums[0, h] = tot[h]
         cols = pl.ds(pl.multiple_of(h * DIM, DIM), DIM)
         for j in range(lanes):
-            obuf[j, :, cols] = part[j * own : (j + 1) * own, :]
+            obuf[j, :, cols] = turned[j * own : (j + 1) * own, :]
         for d in range(1, lanes):
             out_copy(d, h).start()
         return carry
 
     lax.fori_loop(0, HEADS, finish, 0)
+    met = [kv[cls, b, core, chunk:] for cls in classes for b in range(ring) for core in range(2)]
+    met = functools.reduce(jnp.maximum, met).astype(jnp.float32)
     for i in range(2):
-        met = [kv[cc, b, i, chunk:] for cc in range(2) for b in range(ring)]
-        met = functools.reduce(jnp.maximum, met)[:1, :].astype(jnp.float32)
-        sums[0, HEADS + i] = jnp.concatenate([met] * (rows // LANES), axis=1)
+        row = met[i * EXTRA // 2 : i * EXTRA // 2 + 1, :]
+        sums[0, HEADS + i] = jnp.concatenate([row] * (rows // LANES), axis=1)
     for d in range(1, lanes):
         sum_copy(d).start()
+    for cls in classes:
+        at = second[cls]
+        for d in range(1, ring):
+            one_copy(cls, d, first[cls]).wait_send()
+        sib_copy(cls, 0, at, c, None).wait_send()
+        for s in range(1, half + 1):
+            last = s == half
+            fwd_copy(cls, s, at - s + 1, last).wait_send()
+            bwd_copy(cls, s, at + s - 1, last).wait_send()
+            sib_copy(cls, 2 * s - 1, at - s, c, 0 if last else None).wait_send()
+            sib_copy(cls, 2 * s, at + s, c, 1 if last else None).wait_send()
     for d in range(1, lanes):
         sum_copy(d).wait_recv()
     whole = functools.reduce(jnp.add, [sums[d] for d in range(lanes)])
@@ -316,20 +334,6 @@
             mixed += rbuf[d, :, cols].astype(jnp.float32)
         out_ref[:, cols] = (mixed * mix[:, h : h + 1]).astype(out_ref.dtype)
 
-    for d in range(1, ring):
-        one_copy(d, p1).wait_send()
-    for i in range(2):
-        for q in range(2):
-            sib_copy(0, c, p2, i, q).wait_send()
-    for s in range(1, half + 1):
-        for i in range(2):
-            for q in range(2):
-                if s < half or i == 0:
-                    fwd_copy(s, p2 - s + 1, i, q).wait_send()
-                    sib_copy(2 * s - 1, c, p2 - s, i, q).wait_send()
-                if s < half or i == 1:
-                    bwd_copy(s, p2 + s - 1, i, q).wait_send()
-                    sib_copy(2 * s, c, p2 + s, i, q).wait_send()
     for d in range(1, lanes):
         sum_copy(d).wait_send()
         for h in range(HEADS):
@@ -356,7 +360,7 @@
             pltpu.VMEM(keys.shape, jnp.bfloat16),
             pltpu.VMEM(values.shape, jnp.bfloat16),
             pltpu.SMEM(doc_lengths.shape, jnp.int32),
-            pltpu.VMEM((ring, own + EXTRA, 2 * DIM), jnp.bfloat16),
+            pltpu.VMEM((2, ring, own // 2 + EXTRA, 2 * DIM), jnp.bfloat16),
             pltpu.VMEM((2, ring, 2, chunk + EXTRA, DIM), jnp.bfloat16),
             pltpu.VMEM((2, ring, chunk, LANES), jnp.bfloat16),
             pltpu.VMEM((HEADS, 2 * DIM, rows), jnp.bfloat16),
@@ -367,9 +371,9 @@
             pltpu.VMEM((lanes, HEADS + 2, 1, rows), jnp.float32),
             pltpu.VMEM((rows, LANES), jnp.float32),
             sems((4,)),
-            sems((ring - 1,)), sems((ring - 1,)),
-            sems((half, 4)), sems((half, 4)), sems((half, 4)), sems((half, 4)),
-            sems((2 * half + 1, 4)), sems((2 * half + 1, 4)),
+            sems((2, ring - 1)), sems((2, ring - 1)),
+            sems((2, half)), sems((2, half)), sems((2, half)), sems((2, half)),
+            sems((2, 2 * half + 1)), sems((2, 2 * half + 1)),
             sems((lanes, HEADS)), sems((lanes, HEADS)),
             sems((lanes,)), sems((lanes,)),
         ],

time: 130 us -> 130 us (level); the launches traced: 130 us -> 128 us
    pallas_call x1, Pallas kernels: 53.9 us -> 52.2 us  [swift(): pl.pallas_call(functools.partial(swift_kernel, ring, lanes), out_shape=(j...]
where the time goes in v5:
time: 130 us; the launch traced here: 128 us
  Pallas kernels  126 us (97%)
  local copies, waits for them, and re-layouts  1.86 us (1%)
    pallas_call x1, Pallas kernels, swift(): pl.pallas_call(functools.partial(swift_kernel, ring, lanes), out_shape=(j...  52.2 us
    pallas_call x1, Pallas kernels, steady(): pl.pallas_call(functools.partial(attend_kernel, ring, lanes), out_shape=(...  31 us
    pallas_call x1, Pallas kernels, steady(): pl.pallas_call(functools.partial(gather_kernel, ring), out_shape=jax.Shap...  30.8 us
    pallas_call x1, Pallas kernels, steady(): pl.pallas_call(functools.partial(merge_kernel, lanes), out_shape=jax.Shap...  11.9 us

profile of v5, /device:TPU:448, one launch (start us, length us, event | category | flops | bytes accessed | tf_op | source)
XLA Modules:
  0.0 128.5 jit_solution(17670210064668097836)
XLA Ops:
  0.0 0.0 copy-start
  0.0 0.0 copy-start.1
  0.0 0.0 copy-start.2
  0.0 0.0 copy-start.3
  0.0 52.2 %swift.1 = (bf16[64,1024]{1,0:T(8,128)(2,1)S(1)}, f32[8,128]{1,0:T(8,128)}) custom-call(bf16[256,1024]{1,0:T(8,128)(2,1)} %q_hbm.1, bf16[64,128]{1,0:T(8,128)(2,1)} %k_hbm.1, bf16[64,128]{1,0:T(8,128)(2,1)} %v_hbm.1, s32[8]{0:T(128)} %len_hbm.1), custom_call_target="tpu_custom_call" | custom-call | flops 10000000000 | bytes 10000000 | tf_op jit(solution)/shard_map/swift/pallas_call | solution.py:350
  52.2 1.2 slice.3
  54.1 0.0 copy-done
  54.1 0.0 copy-done.1
  54.1 0.0 copy-done.2
  54.1 0.0 copy-done.3
  54.1 73.7 %conditional.1 = (bf16[64,1024]{1,0:T(8,128)(2,1)S(1)}) conditional(s32[]{:T(128)} %bitcast, (bf16[64,128]{1,0:T(8,128)(2,1)S(1)}, bf16[64,128]{1,0:T(8,128)(2,1)S(1)}, bf16[256,1024]{1,0:T(8,128)(2,1)S(1)}, s32[8]{0:T(128)S(1)}) %tuple.20, bf16[64,1024]{1,0:T(8,128)(2,1)S(1)} %get-tuple-element.26), branch_computations={%region_0.0_spmd, %region_1.0_spmd} | conditional | bytes 8 | solution.py:747
  54.1 30.8 %gather.1.kv = bf16[2,8,2,512,128]{4,3,2,1,0:T(8,128)(2,1)S(1)} custom-call(bf16[64,128]{1,0:T(8,128)(2,1)S(1)} %get-tuple-element.18.k_ref, bf16[64,128]{1,0:T(8,128)(2,1)S(1)} %get-tuple-element.19.v_ref), custom_call_target="tpu_custom_call" | custom-call | tf_op jit(solution)/shard_map/cond/branch_0_fun/gather/pallas_call | solution.py:692
  84.9 31.0 %attend.1 = (bf16[4,64,1024]{2,1,0:T(8,128)(2,1)S(1)}, f32[8,256]{1,0:T(8,128)S(1)}) custom-call(bf16[256,1024]{1,0:T(8,128)(2,1)S(1)} %get-tuple-element.17.q_ref, bf16[2,8,2,512,128]{4,3,2,1,0:T(8,128)(2,1)S(1)} %gather.1.kv, s32[8]{0:T(128)S(1)} %get-tuple-element.20.lens), custom_call_target="tpu_custom_call" | custom-call | tf_op jit(solution)/shard_map/cond/branch_0_fun/attend/pallas_call | solution.py:706
  115.9 11.9 %merge.1 = bf16[64,1024]{1,0:T(8,128)(2,1)S(1)} custom-call(bf16[4,64,1024]{2,1,0:T(8,128)(2,1)S(1)} %get-tuple-element.21.obuf, f32[8,256]{1,0:T(8,128)S(1)} %get-tuple-element.22.lbuf), custom_call_target="tpu_custom_call" | custom-call | tf_op jit(solution)/shard_map/cond/branch_0_fun/merge/pallas_call | solution.py:724
  127.8 0.7 copy.10
Async XLA Ops:
  0.0 54.1 %copy-start = (bf16[256,1024]{1,0:T(8,128)(2,1)S(1)}, bf16[256,1024]{1,0:T(8,128)(2,1)}, u32[]{:S(2)}) copy-start(bf16[256,1024]{1,0:T(8,128)(2,1)} %q_hbm.1) | copy-start | bytes 1572868
  0.0 54.1 %copy-start.1 = (bf16[64,128]{1,0:T(8,128)(2,1)S(1)}, bf16[64,128]{1,0:T(8,128)(2,1)}, u32[]{:S(2)}) copy-start(bf16[64,128]{1,0:T(8,128)(2,1)} %k_hbm.1) | copy-start | bytes 49156
  0.0 54.1 %copy-start.2 = (bf16[64,128]{1,0:T(8,128)(2,1)S(1)}, bf16[64,128]{1,0:T(8,128)(2,1)}, u32[]{:S(2)}) copy-start(bf16[64,128]{1,0:T(8,128)(2,1)} %v_hbm.1) | copy-start | bytes 49156
  0.0 54.1 %copy-start.3 = (s32[8]{0:T(128)S(1)}, s32[8]{0:T(128)}, u32[]{:S(2)}) copy-start(s32[8]{0:T(128)} %len_hbm.1) | copy-start | bytes 100

commit v6 on v4

--- a/solution.py
+++ b/solution.py
@@ -31,7 +31,7 @@
 def swift_kernel(
     ring, lanes, q_hbm, k_hbm, v_hbm, len_hbm, out_ref, bound_ref,
     q_in, k_in, v_in, lens, stage, kv, kfeat, qcat, acc, tot, obuf, rbuf, sums, mixing,
-    s_in, s_one, r_one, s_fwd, r_fwd, s_bwd, r_bwd, s_sib, r_sib, s_out, r_out, s_sum, r_sum,
+    s_in, s_one, r_one, s_fwd, r_fwd, s_bwd, r_bwd, s_sib, r_sib, s_cross, r_cross, s_out, r_out, s_sum, r_sum,
 ):
     half = ring // 2
     rows = q_in.shape[0]
@@ -49,17 +49,17 @@
     def wrap(value):
         return lax.rem(value + 2 * ring, ring)
 
-    def device(first, second):
+    def device(first, second, core=c):
         zz, yy = place(c, wrap(first), wrap(second))
-        return {"pb": (zz * ring + yy) * 2 + c}
+        return {"pb": (zz * ring + yy) * 2 + core}
 
     sibling = {"pb": me + 1 - 2 * c}
 
     barrier = pltpu.get_barrier_semaphore()
     partners = [device(p1 + d, p2) for d in range(1, ring)]
-    partners += [device(p1, p2 + d) for d in ((1, ring - 1) if ring > 2 else (1,))]
-    partners += [sibling]
-    partners += [{"ka": lax.rem(x + d, lanes)} for d in range(1, lanes)]
+    partners += [device(p1, p2 + d, core) for d in (1, -1) for core in (c, 1 - c)]
+    partners += [device(p1 + d, p2, 1 - c) for d in (1, -1)]
+    partners += [sibling] + [{"ka": lax.rem(x + d, lanes)} for d in range(1, lanes)]
     for partner in partners:
         pl.semaphore_signal(barrier, inc=1, device_id=partner, device_id_type=MESH)
     moves = [
@@ -92,44 +92,39 @@
     def one_copy(d, b1):
         return copy(stage.at[wrap(b1)], s_one.at[d - 1], r_one.at[d - 1], device(p1 + d, p2))
 
-    def piece(cc, b, i, q):
-        return kv.at[cc, wrap(b), i, pl.ds(q * (chunk // 2), chunk // 2 + q * EXTRA)]
-
-    def fwd_copy(s, b, i, q):
-        n = 2 * i + q
-        return copy(piece(c, b, i, q), s_fwd.at[s - 1, n], r_fwd.at[s - 1, n], device(p1, p2 + 1))
-
-    def bwd_copy(s, b, i, q):
-        n = 2 * i + q
-        return copy(piece(c, b, i, q), s_bwd.at[s - 1, n], r_bwd.at[s - 1, n], device(p1, p2 - 1))
-
-    def sib_copy(k, cc, b, i, q):
-        n = 2 * i + q
-        return copy(piece(cc, b, i, q), s_sib.at[k, n], r_sib.at[k, n], sibling)
-
-    def pass_on(s, i):
-        both = s + 1 < half
-        for q in range(2):
-            fwd_copy(s, p2 - s, i, q).wait_recv()
-            pl.when(both | (i == 0))(lambda q=q: fwd_copy(s + 1, p2 - s, i, q).start())
-            bwd_copy(s, p2 + s, i, q).wait_recv()
-            pl.when(both | (i == 1))(lambda q=q: bwd_copy(s + 1, p2 + s, i, q).start())
-        for q in range(2):
-            sib_copy(2 * s - 1, c, p2 - s, i, q).start()
-            sib_copy(2 * s, c, p2 + s, i, q).start()
-
-    def pass_last():
-        for q in range(2):
-            fwd_copy(half, p2 - half, 0, q).wait_recv()
-            sib_copy(2 * half - 1, c, p2 - half, 0, q).start()
-            bwd_copy(half, p2 + half, 1, q).wait_recv()
-            sib_copy(2 * half, c, p2 + half, 1, q).start()
+    def piece(cc, b, i):
+        return kv.at[cc, wrap(b), i]
+
+    def fwd_copy(s, b, i):
+        return copy(piece(c, b, i), s_fwd.at[s - 1, i], r_fwd.at[s - 1, i], device(p1, p2 + 1))
+
+    def bwd_copy(s, b, i):
+        return copy(piece(c, b, i), s_bwd.at[s - 1, i], r_bwd.at[s - 1, i], device(p1, p2 - 1))
+
+    def sib_copy(k, cc, b, i):
+        return copy(piece(cc, b, i), s_sib.at[k, i], r_sib.at[k, i], sibling)
+
+    def cross_copy(cc, b, i):
+        return copy(piece(cc, b, i), s_cross.at[i], r_cross.at[i], device(p1, p2 + 1 - 2 * i, 1 - c))
+
+    def pass_on(s):
+        for i in range(2):
+            fwd_copy(s, p2 - s, i).wait_recv()
+            if s + 1 < half or i == 0:
+                fwd_copy(s + 1, p2 - s, i).start()
+            bwd_copy(s, p2 + s, i).wait_recv()
+            if s + 1 < half or i == 1:
+                bwd_copy(s + 1, p2 + s, i).start()
+            if s + 1 == half:
+                cross_copy(c, p2 - s + 2 * i * s, i).start()
+        for i in range(2):
+            sib_copy(2 * s - 1, c, p2 - s, i).start()
+            sib_copy(2 * s, c, p2 + s, i).start()
 
     def sib_arrived(s):
         for i in range(2):
-            for q in range(2):
-                sib_copy(2 * s - 1, 1 - c, p1 - s, i, q).wait_recv()
-                sib_copy(2 * s, 1 - c, p1 + s, i, q).wait_recv()
+            sib_copy(2 * s - 1, 1 - c, p1 - s, i).wait_recv()
+            sib_copy(2 * s, 1 - c, p1 + s, i).wait_recv()
 
     for d in range(1, ring):
         one_copy(d, p1).start()
@@ -179,14 +174,14 @@
 
     ones = jnp.ones((16, chunk), jnp.bfloat16)
 
-    def scores(h, cc, b):
-        keys = jnp.concatenate([kv[cc, b, 0, :chunk], kfeat[cc, b]], axis=1)
+    def scores(h, cc, b, size):
+        keys = jnp.concatenate([kv[cc, b, 0, :size], kfeat[cc, b, :size]], axis=1)
         return jnp.dot(keys, qcat[h], preferred_element_type=jnp.float32)
 
-    def fold(h, cc, b, s):
+    def fold(h, cc, b, size, s):
         p = jnp.exp2(s * FACTOR).astype(jnp.bfloat16)
-        vals = jnp.concatenate([kv[cc, b, 1, n : n + LANES] for n in range(0, chunk, LANES)], axis=1)
-        both = jnp.dot(jnp.concatenate([vals, ones], axis=0), p, preferred_element_type=jnp.float32)
+        vals = jnp.concatenate([kv[cc, b, 1, n : n + LANES] for n in range(0, size, LANES)], axis=1)
+        both = jnp.dot(jnp.concatenate([vals, ones[:, :size]], axis=0), p, preferred_element_type=jnp.float32)
         acc[h] += both[:DIM]
         tot[h] += both[DIM : DIM + 1]
 
@@ -204,19 +199,19 @@
     largest = functools.reduce(jnp.maximum, [stage[n, own:, :] for n in range(ring)])
     kv[c, p2, 0, chunk:] = largest[:, :DIM]
     kv[c, p2, 1, chunk:] = largest[:, DIM:]
-    for q in range(2):
-        fwd_copy(1, p2, 0, q).start()
-        bwd_copy(1, p2, 0, q).start()
+    fwd_copy(1, p2, 0).start()
+    bwd_copy(1, p2, 0).start()
     side = LANES // own
     for n in range(ring // side):
         block = stage[n * side : (n + 1) * side, :own, DIM:].reshape(LANES, DIM)
         kv[c, p2, 1, n * LANES : (n + 1) * LANES] = block.T
-    for q in range(2):
-        fwd_copy(1, p2, 1, q).start()
-        bwd_copy(1, p2, 1, q).start()
+    fwd_copy(1, p2, 1).start()
+    bwd_copy(1, p2, 1).start()
     for i in range(2):
-        for q in range(2):
-            sib_copy(0, c, p2, i, q).start()
+        sib_copy(0, c, p2, i).start()
+
+    def seen(b):
+        return (b <= z) & ((b + 1) * plane > me * rows - (MOST - 1))
 
     def unit(u, carry):
         v = jnp.maximum(u - 2, 0)
@@ -231,37 +226,27 @@
         @pl.when(u == 1)
         def _():
             for i in range(2):
-                for q in range(2):
-                    sib_copy(0, 1 - c, p1, i, q).wait_recv()
+                sib_copy(0, 1 - c, p1, i).wait_recv()
 
         @pl.when((u >= 2) & (r == 2))
         def _():
             sib_arrived(s)
 
-        seen = (b <= z) & ((b + 1) * plane > me * rows - (MOST - 1))
-
-        @pl.when((cc == 1) | seen)
+        @pl.when((cc == 1) | seen(b))
         def _():
-            run([(h, cc, b) for h in range(HEADS)])
-
-        @pl.when(u < 2 * (half - 1))
-        def _():
-            pass_on(u // 2 + 1, lax.rem(u, 2))
-
-        @pl.when(u == 2 * (half - 1))
-        def _():
-            pass_last()
-
+            run([(h, cc, b, chunk) for h in range(HEADS)])
+
+        for step, after in ((1, 1), (2, 3), (3, 6)):
+            if step < half:
+                pl.when(u == after)(functools.partial(pass_on, step))
         return carry
 
-    units = 2 + 4 * (half - 2)
-    lax.fori_loop(0, units, unit, 0)
-    if units <= 2 * (half - 1):
-        pass_last()
+    lax.fori_loop(0, 2 + 4 * (half - 2), unit, 0)
     sib_arrived(half - 1)
-    for q in range(2):
-        sib_copy(2 * half - 1, 1 - c, p1 - half, 0, q).wait_recv()
-        sib_copy(2 * half, 1 - c, p1 + half, 1, q).wait_recv()
+    fwd_copy(half, p2 - half, 0).wait_recv()
+    bwd_copy(half, p2 + half, 1).wait_recv()
+    cross_copy(1 - c, p1 - half, 0).wait_recv()
+    cross_copy(1 - c, p1 + half, 1).wait_recv()
 
     def peer(d):
         return lax.rem(x + d, lanes)
@@ -279,11 +264,13 @@
             send_sem=s_sum.at[d], recv_sem=r_sum.at[d], device_id={"ka": peer(d)}, device_id_type=MESH,
         )
 
-    late = [(c, p2 - half + 1), (c, p2 + half - 1), (1 - c, p1 - half + 1), (1 - c, p1 + half - 1)]
-    late += [(c, p2 + half), (1 - c, p1 + half)]
-
-    def finish(h, carry):
-        run([(h, cc, wrap(b)) for cc, b in late])
+    shifts = (1 - half, half - 1, half)
+    early_cc = [(c, p2 + d) for d in shifts[:2]] + [(1 - c, p1 + d) for d in shifts[:2]]
+    late = early_cc + [(c, p2 + half), (1 - c, p1 + half)]
+    some = functools.reduce(jnp.logical_or, [seen(wrap(z + d)) for d in shifts])
+
+    def finish(work, h, carry):
+        run([(h, cc, wrap(b), size) for cc, b, size in work])
         part = acc[h].T.astype(jnp.bfloat16)
         sums[0, h] = tot[h]
         cols = pl.ds(pl.multiple_of(h * DIM, DIM), DIM)
@@ -293,20 +280,39 @@
             out_copy(d, h).start()
         return carry
 
-    lax.fori_loop(0, HEADS, finish, 0)
+    @pl.when(some)
+    def _():
+        lax.fori_loop(0, HEADS, functools.partial(finish, [(cc, b, chunk) for cc, b in late]), 0)
+
+    @pl.when(jnp.logical_not(some))
+    def _():
+        lax.fori_loop(0, HEADS, functools.partial(finish, [(1, y + d, chunk // 2) for d in shifts]), 0)
+
     for i in range(2):
         met = [kv[cc, b, i, chunk:] for cc in range(2) for b in range(ring)]
         met = functools.reduce(jnp.maximum, met)[:1, :].astype(jnp.float32)
         sums[0, HEADS + i] = jnp.concatenate([met] * (rows // LANES), axis=1)
     for d in range(1, lanes):
         sum_copy(d).start()
+    for d in range(1, ring):
+        one_copy(d, p1).wait_send()
+    for i in range(2):
+        sib_copy(0, c, p2, i).wait_send()
+        for s in range(1, half):
+            fwd_copy(s, p2 - s + 1, i).wait_send()
+            bwd_copy(s, p2 + s - 1, i).wait_send()
+            sib_copy(2 * s - 1, c, p2 - s, i).wait_send()
+            sib_copy(2 * s, c, p2 + s, i).wait_send()
+        cross_copy(c, p2 + (2 * i - 1) * (half - 1), i).wait_send()
+    fwd_copy(half, p2 - half + 1, 0).wait_send()
+    bwd_copy(half, p2 + half - 1, 1).wait_send()
     for d in range(1, lanes):
         sum_copy(d).wait_recv()
     whole = functools.reduce(jnp.add, [sums[d] for d in range(lanes)])
     share = [1.0 / whole[h] for h in range(HEADS)] + [jnp.zeros((LANES - HEADS, rows), jnp.float32)]
     mixing[...] = jnp.concatenate(share, axis=0).T
     met = functools.reduce(jnp.maximum, [sums[d] for d in range(lanes)])
-    bound_ref[...] = jnp.broadcast_to((met[HEADS] * met[HEADS + 1])[:, :LANES], bound_ref.shape)
+    bound_ref[0] = jnp.max(met[HEADS] * met[HEADS + 1])
     mix = mixing[pl.ds(pl.multiple_of(x * own, own), own), :]
     for h in range(HEADS):
         cols = slice(h * DIM, (h + 1) * DIM)
@@ -316,20 +322,6 @@
             mixed += rbuf[d, :, cols].astype(jnp.float32)
         out_ref[:, cols] = (mixed * mix[:, h : h + 1]).astype(out_ref.dtype)
 
-    for d in range(1, ring):
-        one_copy(d, p1).wait_send()
-    for i in range(2):
-        for q in range(2):
-            sib_copy(0, c, p2, i, q).wait_send()
-    for s in range(1, half + 1):
-        for i in range(2):
-            for q in range(2):
-                if s < half or i == 0:
-                    fwd_copy(s, p2 - s + 1, i, q).wait_send()
-                    sib_copy(2 * s - 1, c, p2 - s, i, q).wait_send()
-                if s < half or i == 1:
-                    bwd_copy(s, p2 + s - 1, i, q).wait_send()
-                    sib_copy(2 * s, c, p2 + s, i, q).wait_send()
     for d in range(1, lanes):
         sum_copy(d).wait_send()
         for h in range(HEADS):
@@ -347,10 +339,10 @@
         functools.partial(swift_kernel, ring, lanes),
         out_shape=(
             jax.ShapeDtypeStruct((own, HEADS * DIM), jnp.bfloat16),
-            jax.ShapeDtypeStruct((8, LANES), jnp.float32),
+            jax.ShapeDtypeStruct((1,), jnp.float32),
         ),
         in_specs=[pl.BlockSpec(memory_space=pltpu.HBM)] * 4,
-        out_specs=(vmem, vmem),
+        out_specs=(vmem, pl.BlockSpec(memory_space=pltpu.SMEM)),
         scratch_shapes=[
             pltpu.VMEM(queries.shape, jnp.bfloat16),
             pltpu.VMEM(keys.shape, jnp.bfloat16),
@@ -368,8 +360,8 @@
             pltpu.VMEM((rows, LANES), jnp.float32),
             sems((4,)),
             sems((ring - 1,)), sems((ring - 1,)),
-            sems((half, 4)), sems((half, 4)), sems((half, 4)), sems((half, 4)),
-            sems((2 * half + 1, 4)), sems((2 * half + 1, 4)),
+            sems((half, 2)), sems((half, 2)), sems((half, 2)), sems((half, 2)),
+            sems((2 * half - 1, 2)), sems((2 * half - 1, 2)), sems((2,)), sems((2,)),
             sems((lanes, HEADS)), sems((lanes, HEADS)),
             sems((lanes,)), sems((lanes,)),
         ],
@@ -739,7 +731,7 @@
 def per_device(ring, lanes, queries, keys, values, doc_lengths):
     args = (queries, keys, values, doc_lengths)
     out, bound = swift(ring, lanes, *args)
-    fits = bound[0, 0] <= (SAFE / FACTOR) ** 2
+    fits = bound[0] <= (SAFE / FACTOR) ** 2
     return lax.cond(fits, lambda *_: out, functools.partial(steady, ring, lanes), *args)
 
 

time: 130 us -> 127 us (0.977)
  Pallas kernels: 127 us -> 125 us
    pallas_call x1, Pallas kernels: 53.9 us -> 50.4 us  [swift(): pl.pallas_call(functools.partial(swift_kernel, ring, lanes), out_shape=(j...]
where the time goes in v6:
time: 127 us; the launch traced here: 126 us
  Pallas kernels  125 us (98%)
    pallas_call x1, Pallas kernels, swift(): pl.pallas_call(functools.partial(swift_kernel, ring, lanes), out_shape=(j...  50.4 us
    pallas_call x1, Pallas kernels, steady(): pl.pallas_call(functools.partial(gather_kernel, ring), out_shape=jax.Shap...  31.7 us
    pallas_call x1, Pallas kernels, steady(): pl.pallas_call(functools.partial(attend_kernel, ring, lanes), out_shape=(...  31 us
    pallas_call x1, Pallas kernels, steady(): pl.pallas_call(functools.partial(merge_kernel, lanes), out_shape=jax.Shap...  11.9 us

profile of v6, /device:TPU:448, one launch (start us, length us, event | category | flops | bytes accessed | tf_op | source)
XLA Modules:
  0.0 126.3 jit_solution(12580110309272062473)
XLA Ops:
  0.0 0.0 copy-start
  0.0 0.0 copy-start.1
  0.0 0.0 copy-start.2
  0.0 0.0 copy-start.3
  0.0 50.4 %swift.1 = (bf16[64,1024]{1,0:T(8,128)(2,1)S(1)}, f32[1]{0:T(128)}) custom-call(bf16[256,1024]{1,0:T(8,128)(2,1)} %q_hbm.1, bf16[64,128]{1,0:T(8,128)(2,1)} %k_hbm.1, bf16[64,128]{1,0:T(8,128)(2,1)} %v_hbm.1, s32[8]{0:T(128)} %len_hbm.1), custom_call_target="tpu_custom_call" | custom-call | flops 10000000000 | bytes 10000000 | tf_op jit(solution)/shard_map/swift/pallas_call | solution.py:338
  51.0 0.0 copy-done
  51.0 0.0 copy-done.1
  51.0 0.0 copy-done.2
  51.0 0.0 copy-done.3
  51.0 74.6 %conditional.1 = (bf16[64,1024]{1,0:T(8,128)(2,1)S(1)}) conditional(s32[]{:T(128)} %bitcast, (bf16[64,128]{1,0:T(8,128)(2,1)S(1)}, bf16[64,128]{1,0:T(8,128)(2,1)S(1)}, bf16[256,1024]{1,0:T(8,128)(2,1)S(1)}, s32[8]{0:T(128)S(1)}) %tuple.20, bf16[64,1024]{1,0:T(8,128)(2,1)S(1)} %get-tuple-element.26), branch_computations={%region_0.0_spmd, %region_1.0_spmd} | conditional | bytes 8 | solution.py:735
  51.0 31.7 %gather.1.kv = bf16[2,8,2,512,128]{4,3,2,1,0:T(8,128)(2,1)S(1)} custom-call(bf16[64,128]{1,0:T(8,128)(2,1)S(1)} %get-tuple-element.18.k_ref, bf16[64,128]{1,0:T(8,128)(2,1)S(1)} %get-tuple-element.19.v_ref), custom_call_target="tpu_custom_call" | custom-call | tf_op jit(solution)/shard_map/cond/branch_0_fun/gather/pallas_call | solution.py:680
  82.7 31.0 %attend.1 = (bf16[4,64,1024]{2,1,0:T(8,128)(2,1)S(1)}, f32[8,256]{1,0:T(8,128)S(1)}) custom-call(bf16[256,1024]{1,0:T(8,128)(2,1)S(1)} %get-tuple-element.17.q_ref, bf16[2,8,2,512,128]{4,3,2,1,0:T(8,128)(2,1)S(1)} %gather.1.kv, s32[8]{0:T(128)S(1)} %get-tuple-element.20.lens), custom_call_target="tpu_custom_call" | custom-call | tf_op jit(solution)/shard_map/cond/branch_0_fun/attend/pallas_call | solution.py:694
  113.7 11.9 %merge.1 = bf16[64,1024]{1,0:T(8,128)(2,1)S(1)} custom-call(bf16[4,64,1024]{2,1,0:T(8,128)(2,1)S(1)} %get-tuple-element.21.obuf, f32[8,256]{1,0:T(8,128)S(1)} %get-tuple-element.22.lbuf), custom_call_target="tpu_custom_call" | custom-call | tf_op jit(solution)/shard_map/cond/branch_0_fun/merge/pallas_call | solution.py:712
  125.6 0.7 copy.10
Async XLA Ops:
  0.0 51.0 %copy-start = (bf16[256,1024]{1,0:T(8,128)(2,1)S(1)}, bf16[256,1024]{1,0:T(8,128)(2,1)}, u32[]{:S(2)}) copy-start(bf16[256,1024]{1,0:T(8,128)(2,1)} %q_hbm.1) | copy-start | bytes 1572868
  0.0 51.0 %copy-start.1 = (bf16[64,128]{1,0:T(8,128)(2,1)S(1)}, bf16[64,128]{1,0:T(8,128)(2,1)}, u32[]{:S(2)}) copy-start(bf16[64,128]{1,0:T(8,128)(2,1)} %k_hbm.1) | copy-start | bytes 49156
  0.0 51.0 %copy-start.2 = (bf16[64,128]{1,0:T(8,128)(2,1)S(1)}, bf16[64,128]{1,0:T(8,128)(2,1)}, u32[]{:S(2)}) copy-start(bf16[64,128]{1,0:T(8,128)(2,1)} %v_hbm.1) | copy-start | bytes 49156
  0.0 51.0 %copy-start.3 = (s32[8]{0:T(128)S(1)}, s32[8]{0:T(128)}, u32[]{:S(2)}) copy-start(s32[8]{0:T(128)} %len_hbm.1) | copy-start | bytes 100

commit v7 on v6

--- a/solution.py
+++ b/solution.py
@@ -70,18 +70,19 @@
         move.start()
     moves[0].wait()
     moves[1].wait()
-    stage[p1, :own, :DIM] = k_in[...]
-    stage[p1, :own, DIM:] = v_in[...]
+    stage[p1, :own] = k_in[...]
+    stage[p1, own : 2 * own] = v_in[...]
     wide = k_in[...].astype(jnp.float32)
     longest = jnp.max(jnp.sum(wide * wide, axis=1, keepdims=True), axis=0, keepdims=True)
-    stage[p1, own:, :DIM] = jnp.broadcast_to(longest * 1.01, (EXTRA, DIM)).astype(jnp.bfloat16)
+    k_most = longest
     moves[3].wait()
     longest = jnp.zeros((rows, 1), jnp.float32)
     for h in range(HEADS):
         wide = q_in[:, h * DIM : (h + 1) * DIM].astype(jnp.float32)
         longest = jnp.maximum(longest, jnp.sum(wide * wide, axis=1, keepdims=True))
     longest = jnp.max(longest, axis=0, keepdims=True)
-    stage[p1, own:, DIM:] = jnp.broadcast_to(longest * 1.01, (EXTRA, DIM)).astype(jnp.bfloat16)
+    upper = lax.broadcasted_iota(jnp.int32, (EXTRA, DIM), 0) < EXTRA // 2
+    stage[p1, 2 * own :] = (jnp.where(upper, k_most, longest) * 1.01).astype(jnp.bfloat16)
     pl.semaphore_wait(barrier, len(partners))
 
     def copy(ref, send, recv, where):
@@ -126,7 +127,7 @@
             sib_copy(2 * s - 1, 1 - c, p1 - s, i).wait_recv()
             sib_copy(2 * s, 1 - c, p1 + s, i).wait_recv()
 
-    for d in range(1, ring):
+    for d in sorted(range(1, ring), key=lambda d: abs(d - half)):
         one_copy(d, p1).start()
     moves[2].wait()
 
@@ -195,15 +196,15 @@
     for d in range(1, ring):
         one_copy(d, p1 - d).wait_recv()
     for n in range(ring):
-        kv[c, p2, 0, n * own : (n + 1) * own] = stage[n, :own, :DIM]
-    largest = functools.reduce(jnp.maximum, [stage[n, own:, :] for n in range(ring)])
-    kv[c, p2, 0, chunk:] = largest[:, :DIM]
-    kv[c, p2, 1, chunk:] = largest[:, DIM:]
+        kv[c, p2, 0, n * own : (n + 1) * own] = stage[n, :own]
+    largest = functools.reduce(jnp.maximum, [stage[n, 2 * own :] for n in range(ring)])
+    for i in range(2):
+        kv[c, p2, i, chunk:] = largest
     fwd_copy(1, p2, 0).start()
     bwd_copy(1, p2, 0).start()
     side = LANES // own
     for n in range(ring // side):
-        block = stage[n * side : (n + 1) * side, :own, DIM:].reshape(LANES, DIM)
+        block = stage[n * side : (n + 1) * side, own : 2 * own].reshape(LANES, DIM)
         kv[c, p2, 1, n * LANES : (n + 1) * LANES] = block.T
     fwd_copy(1, p2, 1).start()
     bwd_copy(1, p2, 1).start()
@@ -236,26 +237,30 @@
         def _():
             run([(h, cc, b, chunk) for h in range(HEADS)])
 
-        for step, after in ((1, 1), (2, 3), (3, 6)):
+        for step, after in ((1, 0), (2, 3), (3, 6)):
             if step < half:
                 pl.when(u == after)(functools.partial(pass_on, step))
         return carry
 
     lax.fori_loop(0, 2 + 4 * (half - 2), unit, 0)
-    sib_arrived(half - 1)
-    fwd_copy(half, p2 - half, 0).wait_recv()
-    bwd_copy(half, p2 + half, 1).wait_recv()
-    cross_copy(1 - c, p1 - half, 0).wait_recv()
-    cross_copy(1 - c, p1 + half, 1).wait_recv()
+
+    def last_mine():
+        fwd_copy(half, p2 - half, 0).wait_recv()
+        bwd_copy(half, p2 + half, 1).wait_recv()
+
+    def last_other():
+        sib_arrived(half - 1)
+        cross_copy(1 - c, p1 - half, 0).wait_recv()
+        cross_copy(1 - c, p1 + half, 1).wait_recv()
 
     def peer(d):
         return lax.rem(x + d, lanes)
 
-    def out_copy(d, h):
-        cols = pl.ds(pl.multiple_of(h * DIM, DIM), DIM)
+    def out_copy(d, g):
+        cols = pl.ds(pl.multiple_of(g * 2 * DIM, 2 * DIM), 2 * DIM)
         return pltpu.make_async_remote_copy(
             src_ref=obuf.at[peer(d), :, cols], dst_ref=rbuf.at[d, :, cols],
-            send_sem=s_out.at[d, h], recv_sem=r_out.at[d, h], device_id={"ka": peer(d)}, device_id_type=MESH,
+            send_sem=s_out.at[d, g], recv_sem=r_out.at[d, g], device_id={"ka": peer(d)}, device_id_type=MESH,
         )
 
     def sum_copy(d):
@@ -269,29 +274,40 @@
     late = early_cc + [(c, p2 + half), (1 - c, p1 + half)]
     some = functools.reduce(jnp.logical_or, [seen(wrap(z + d)) for d in shifts])
 
-    def finish(work, h, carry):
-        run([(h, cc, wrap(b), size) for cc, b, size in work])
-        part = acc[h].T.astype(jnp.bfloat16)
-        sums[0, h] = tot[h]
-        cols = pl.ds(pl.multiple_of(h * DIM, DIM), DIM)
-        for j in range(lanes):
-            obuf[j, :, cols] = part[j * own : (j + 1) * own, :]
+    def finish(work, g, carry):
+        pair = [2 * g, 2 * g + 1]
+        run([(h, cc, wrap(b), size) for h in pair for cc, b, size in work])
+        for h in pair:
+            part = acc[h].T.astype(jnp.bfloat16)
+            sums[0, h] = tot[h]
+            cols = pl.ds(pl.multiple_of(h * DIM, DIM), DIM)
+            for j in range(lanes):
+                obuf[j, :, cols] = part[j * own : (j + 1) * own, :]
         for d in range(1, lanes):
-            out_copy(d, h).start()
+            out_copy(d, g).start()
         return carry
 
     @pl.when(some)
     def _():
-        lax.fori_loop(0, HEADS, functools.partial(finish, [(cc, b, chunk) for cc, b in late]), 0)
+        last_other()
+        last_mine()
+        work = [(cc, b, chunk) for cc, b in late]
+        lax.fori_loop(0, HEADS // 2, functools.partial(finish, work), 0)
 
     @pl.when(jnp.logical_not(some))
     def _():
-        lax.fori_loop(0, HEADS, functools.partial(finish, [(1, y + d, chunk // 2) for d in shifts]), 0)
-
+        pl.when(c == 0)(last_other)
+        pl.when(c == 1)(last_mine)
+        work = [(1, y + d, chunk // 2) for d in shifts]
+        lax.fori_loop(0, HEADS // 2, functools.partial(finish, work), 0)
+        pl.when(c == 0)(last_mine)
+        pl.when(c == 1)(last_other)
+
+    met = [kv[cc, b, i, chunk:] for cc in range(2) for b in range(ring) for i in range(2)]
+    met = functools.reduce(jnp.maximum, met).astype(jnp.float32)
     for i in range(2):
-        met = [kv[cc, b, i, chunk:] for cc in range(2) for b in range(ring)]
-        met = functools.reduce(jnp.maximum, met)[:1, :].astype(jnp.float32)
-        sums[0, HEADS + i] = jnp.concatenate([met] * (rows // LANES), axis=1)
+        row = met[i * EXTRA // 2 : i * EXTRA // 2 + 1, :]
+        sums[0, HEADS + i] = jnp.concatenate([row] * (rows // LANES), axis=1)
     for d in range(1, lanes):
         sum_copy(d).start()
     for d in range(1, ring):
@@ -318,14 +334,15 @@
         cols = slice(h * DIM, (h + 1) * DIM)
         mixed = obuf[x, :, cols].astype(jnp.float32)
         for d in range(1, lanes):
-            out_copy(d, h).wait_recv()
+            if h % 2 == 0:
+                out_copy(d, h // 2).wait_recv()
             mixed += rbuf[d, :, cols].astype(jnp.float32)
         out_ref[:, cols] = (mixed * mix[:, h : h + 1]).astype(out_ref.dtype)
 
     for d in range(1, lanes):
         sum_copy(d).wait_send()
-        for h in range(HEADS):
-            out_copy(d, h).wait_send()
+        for g in range(HEADS // 2):
+            out_copy(d, g).wait_send()
 
 
 def swift(ring, lanes, queries, keys, values, doc_lengths):
@@ -348,7 +365,7 @@
             pltpu.VMEM(keys.shape, jnp.bfloat16),
             pltpu.VMEM(values.shape, jnp.bfloat16),
             pltpu.SMEM(doc_lengths.shape, jnp.int32),
-            pltpu.VMEM((ring, own + EXTRA, 2 * DIM), jnp.bfloat16),
+            pltpu.VMEM((ring, 2 * own + EXTRA, DIM), jnp.bfloat16),
             pltpu.VMEM((2, ring, 2, chunk + EXTRA, DIM), jnp.bfloat16),
             pltpu.VMEM((2, ring, chunk, LANES), jnp.bfloat16),
             pltpu.VMEM((HEADS, 2 * DIM, rows), jnp.bfloat16),
@@ -362,7 +379,7 @@
             sems((ring - 1,)), sems((ring - 1,)),
             sems((half, 2)), sems((half, 2)), sems((half, 2)), sems((half, 2)),
             sems((2 * half - 1, 2)), sems((2 * half - 1, 2)), sems((2,)), sems((2,)),
-            sems((lanes, HEADS)), sems((lanes, HEADS)),
+            sems((lanes, HEADS // 2)), sems((lanes, HEADS // 2)),
             sems((lanes,)), sems((lanes,)),
         ],
         compiler_params=pltpu.CompilerParams(
@@ -438,7 +455,7 @@
     def travels(s, p):
         return s < half or (s == half and p < 2), s < half or (s == half and p >= 2)
 
-    for d in range(1, ring):
+    for d in sorted(range(1, ring), key=lambda d: abs(d - half)):
         one_copy(d, p1).start()
     for d in range(1, ring):
         one_copy(d, p1 - d).wait_recv()

time: 127 us -> 121 us (0.953)
  Pallas kernels: 125 us -> 120 us
    pallas_call x1, Pallas kernels: 50.4 us -> 47.6 us  [swift(): pl.pallas_call(functools.partial(swift_kernel, ring, lanes), out_shape=(j...]
    pallas_call x1, Pallas kernels: 31.7 us -> 29.2 us  [steady(): pl.pallas_call(functools.partial(gather_kernel, ring), out_shape=jax.Shap...]
where the time goes in v7:
time: 121 us
  Pallas kernels  120 us (99%)
    pallas_call x1, Pallas kernels, swift(): pl.pallas_call(functools.partial(swift_kernel, ring, lanes), out_shape=(j...  47.6 us
    pallas_call x1, Pallas kernels, steady(): pl.pallas_call(functools.partial(attend_kernel, ring, lanes), out_shape=(...  31 us
    pallas_call x1, Pallas kernels, steady(): pl.pallas_call(functools.partial(gather_kernel, ring), out_shape=jax.Shap...  29.2 us
    pallas_call x1, Pallas kernels, steady(): pl.pallas_call(functools.partial(merge_kernel, lanes), out_shape=jax.Shap...  11.9 us

profile of v7, /device:TPU:448, one launch (start us, length us, event | category | flops | bytes accessed | tf_op | source)
XLA Modules:
  0.0 121.0 jit_solution(16598715819203329594)
XLA Ops:
  0.0 0.0 copy-start
  0.0 0.0 copy-start.1
  0.0 0.0 copy-start.2
  0.0 0.0 copy-start.3
  0.0 47.6 %swift.1 = (bf16[64,1024]{1,0:T(8,128)(2,1)S(1)}, f32[1]{0:T(128)}) custom-call(bf16[256,1024]{1,0:T(8,128)(2,1)} %q_hbm.1, bf16[64,128]{1,0:T(8,128)(2,1)} %k_hbm.1, bf16[64,128]{1,0:T(8,128)(2,1)} %v_hbm.1, s32[8]{0:T(128)} %len_hbm.1), custom_call_target="tpu_custom_call" | custom-call | flops 10000000000 | bytes 10000000 | tf_op jit(solution)/shard_map/swift/pallas_call | solution.py:355
  48.2 0.0 copy-done
  48.2 0.0 copy-done.1
  48.2 0.0 copy-done.2
  48.2 0.0 copy-done.3
  48.2 72.1 %conditional.1 = (bf16[64,1024]{1,0:T(8,128)(2,1)S(1)}) conditional(s32[]{:T(128)} %bitcast, (bf16[64,128]{1,0:T(8,128)(2,1)S(1)}, bf16[64,128]{1,0:T(8,128)(2,1)S(1)}, bf16[256,1024]{1,0:T(8,128)(2,1)S(1)}, s32[8]{0:T(128)S(1)}) %tuple.20, bf16[64,1024]{1,0:T(8,128)(2,1)S(1)} %get-tuple-element.26), branch_computations={%region_0.0_spmd, %region_1.0_spmd} | conditional | bytes 8 | solution.py:752
  48.3 29.2 %gather.1.kv = bf16[2,8,2,512,128]{4,3,2,1,0:T(8,128)(2,1)S(1)} custom-call(bf16[64,128]{1,0:T(8,128)(2,1)S(1)} %get-tuple-element.18.k_ref, bf16[64,128]{1,0:T(8,128)(2,1)S(1)} %get-tuple-element.19.v_ref), custom_call_target="tpu_custom_call" | custom-call | tf_op jit(solution)/shard_map/cond/branch_0_fun/gather/pallas_call | solution.py:697
  77.4 31.0 %attend.1 = (bf16[4,64,1024]{2,1,0:T(8,128)(2,1)S(1)}, f32[8,256]{1,0:T(8,128)S(1)}) custom-call(bf16[256,1024]{1,0:T(8,128)(2,1)S(1)} %get-tuple-element.17.q_ref, bf16[2,8,2,512,128]{4,3,2,1,0:T(8,128)(2,1)S(1)} %gather.1.kv, s32[8]{0:T(128)S(1)} %get-tuple-element.20.lens), custom_call_target="tpu_custom_call" | custom-call | tf_op jit(solution)/shard_map/cond/branch_0_fun/attend/pallas_call | solution.py:711
  108.4 11.9 %merge.1 = bf16[64,1024]{1,0:T(8,128)(2,1)S(1)} custom-call(bf16[4,64,1024]{2,1,0:T(8,128)(2,1)S(1)} %get-tuple-element.21.obuf, f32[8,256]{1,0:T(8,128)S(1)} %get-tuple-element.22.lbuf), custom_call_target="tpu_custom_call" | custom-call | tf_op jit(solution)/shard_map/cond/branch_0_fun/merge/pallas_call | solution.py:729
  120.3 0.7 copy.10
Async XLA Ops:
  0.0 48.2 %copy-start = (bf16[256,1024]{1,0:T(8,128)(2,1)S(1)}, bf16[256,1024]{1,0:T(8,128)(2,1)}, u32[]{:S(2)}) copy-start(bf16[256,1024]{1,0:T(8,128)(2,1)} %q_hbm.1) | copy-start | bytes 1572868
  0.0 48.2 %copy-start.1 = (bf16[64,128]{1,0:T(8,128)(2,1)S(1)}, bf16[64,128]{1,0:T(8,128)(2,1)}, u32[]{:S(2)}) copy-start(bf16[64,128]{1,0:T(8,128)(2,1)} %k_hbm.1) | copy-start | bytes 49156
  0.0 48.2 %copy-start.2 = (bf16[64,128]{1,0:T(8,128)(2,1)S(1)}, bf16[64,128]{1,0:T(8,128)(2,1)}, u32[]{:S(2)}) copy-start(bf16[64,128]{1,0:T(8,128)(2,1)} %v_hbm.1) | copy-start | bytes 49156
  0.0 48.2 %copy-start.3 = (s32[8]{0:T(128)S(1)}, s32[8]{0:T(128)}, u32[]{:S(2)}) copy-start(s32[8]{0:T(128)} %len_hbm.1) | copy-start | bytes 100

commit v8 on v7

--- a/solution.py
+++ b/solution.py
@@ -152,8 +152,9 @@
     later = (first >= 0) & (first < own) & (tok < x * own + first)
     hidden = jnp.where(later, -MASK, hidden).astype(jnp.bfloat16)
     for h in range(HEADS):
-        qcat[h, :DIM, :] = q_in[:, h * DIM : (h + 1) * DIM].T
-        qcat[h, DIM:, :] = hidden
+        at = slice(h % 2 * rows, (h % 2 + 1) * rows)
+        qcat[h // 2, :DIM, at] = q_in[:, h * DIM : (h + 1) * DIM].T
+        qcat[h // 2, DIM:, at] = hidden
     acc[...] = jnp.zeros_like(acc)
     tot[...] = jnp.zeros_like(tot)
 
@@ -175,16 +176,16 @@
 
     ones = jnp.ones((16, chunk), jnp.bfloat16)
 
-    def scores(h, cc, b, size):
+    def scores(g, cc, b, size):
         keys = jnp.concatenate([kv[cc, b, 0, :size], kfeat[cc, b, :size]], axis=1)
-        return jnp.dot(keys, qcat[h], preferred_element_type=jnp.float32)
-
-    def fold(h, cc, b, size, s):
+        return jnp.dot(keys, qcat[g], preferred_element_type=jnp.float32)
+
+    def fold(g, cc, b, size, s):
         p = jnp.exp2(s * FACTOR).astype(jnp.bfloat16)
         vals = jnp.concatenate([kv[cc, b, 1, n : n + LANES] for n in range(0, size, LANES)], axis=1)
         both = jnp.dot(jnp.concatenate([vals, ones[:, :size]], axis=0), p, preferred_element_type=jnp.float32)
-        acc[h] += both[:DIM]
-        tot[h] += both[DIM : DIM + 1]
+        acc[g] += both[:DIM]
+        tot[g] += both[DIM : DIM + 1]
 
     def run(work):
         s = scores(*work[0])
@@ -235,7 +236,7 @@
 
         @pl.when((cc == 1) | seen(b))
         def _():
-            run([(h, cc, b, chunk) for h in range(HEADS)])
+            run([(g, cc, b, chunk) for g in range(HEADS // 2)])
 
         for step, after in ((1, 0), (2, 3), (3, 6)):
             if step < half:
@@ -248,8 +249,10 @@
         fwd_copy(half, p2 - half, 0).wait_recv()
         bwd_copy(half, p2 + half, 1).wait_recv()
 
-    def last_other():
+    def last_sib():
         sib_arrived(half - 1)
+
+    def last_cross():
         cross_copy(1 - c, p1 - half, 0).wait_recv()
         cross_copy(1 - c, p1 + half, 1).wait_recv()
 
@@ -272,14 +275,14 @@
     shifts = (1 - half, half - 1, half)
     early_cc = [(c, p2 + d) for d in shifts[:2]] + [(1 - c, p1 + d) for d in shifts[:2]]
     late = early_cc + [(c, p2 + half), (1 - c, p1 + half)]
-    some = functools.reduce(jnp.logical_or, [seen(wrap(z + d)) for d in shifts])
 
     def finish(work, g, carry):
-        pair = [2 * g, 2 * g + 1]
-        run([(h, cc, wrap(b), size) for h in pair for cc, b, size in work])
-        for h in pair:
-            part = acc[h].T.astype(jnp.bfloat16)
-            sums[0, h] = tot[h]
+        run([(g, cc, wrap(b), size) for cc, b, size in work])
+        for n in range(2):
+            h = 2 * g + n
+            at = slice(n * rows, (n + 1) * rows)
+            part = acc[g, :, at].T.astype(jnp.bfloat16)
+            sums[0, h] = tot[g, :, at]
             cols = pl.ds(pl.multiple_of(h * DIM, DIM), DIM)
             for j in range(lanes):
                 obuf[j, :, cols] = part[j * own : (j + 1) * own, :]
@@ -287,21 +290,42 @@
             out_copy(d, g).start()
         return carry
 
-    @pl.when(some)
+    def finish_all(work):
+        lax.fori_loop(0, HEADS // 2, functools.partial(finish, work), 0)
+
+    @pl.when(z >= half)
     def _():
-        last_other()
+        last_sib()
+        last_cross()
         last_mine()
-        work = [(cc, b, chunk) for cc, b in late]
-        lax.fori_loop(0, HEADS // 2, functools.partial(finish, work), 0)
-
-    @pl.when(jnp.logical_not(some))
+        finish_all([(cc, b, chunk) for cc, b in late])
+
+    halves = [(1, y + d, chunk // 2) for d in shifts]
+
+    @pl.when(z == half - 1)
     def _():
-        pl.when(c == 0)(last_other)
+        last_sib()
+        pl.when(c == 0)(last_cross)
         pl.when(c == 1)(last_mine)
-        work = [(1, y + d, chunk // 2) for d in shifts]
-        lax.fori_loop(0, HEADS // 2, functools.partial(finish, work), 0)
+        finish_all([(0, 0, chunk)] + halves)
         pl.when(c == 0)(last_mine)
-        pl.when(c == 1)(last_other)
+        pl.when(c == 1)(last_cross)
+
+    @pl.when(z < half - 1)
+    def _():
+        @pl.when(c == 0)
+        def _():
+            last_sib()
+            last_cross()
+
+        pl.when(c == 1)(last_mine)
+        finish_all(halves)
+        pl.when(c == 0)(last_mine)
+
+        @pl.when(c == 1)
+        def _():
+            last_sib()
+            last_cross()
 
     met = [kv[cc, b, i, chunk:] for cc in range(2) for b in range(ring) for i in range(2)]
     met = functools.reduce(jnp.maximum, met).astype(jnp.float32)
@@ -368,9 +392,9 @@
             pltpu.VMEM((ring, 2 * own + EXTRA, DIM), jnp.bfloat16),
             pltpu.VMEM((2, ring, 2, chunk + EXTRA, DIM), jnp.bfloat16),
             pltpu.VMEM((2, ring, chunk, LANES), jnp.bfloat16),
-            pltpu.VMEM((HEADS, 2 * DIM, rows), jnp.bfloat16),
-            pltpu.VMEM((HEADS, DIM, rows), jnp.float32),
-            pltpu.VMEM((HEADS, 1, rows), jnp.float32),
+            pltpu.VMEM((HEADS // 2, 2 * DIM, 2 * rows), jnp.bfloat16),
+            pltpu.VMEM((HEADS // 2, DIM, 2 * rows), jnp.float32),
+            pltpu.VMEM((HEADS // 2, 1, 2 * rows), jnp.float32),
             pltpu.VMEM(parts, jnp.bfloat16),
             pltpu.VMEM(parts, jnp.bfloat16),
             pltpu.VMEM((lanes, HEADS + 2, 1, rows), jnp.float32),

time: 121 us -> 119 us (0.983)
  Pallas kernels: 120 us -> 118 us
    pallas_call x1, Pallas kernels: 47.6 us -> 45.8 us  [swift(): pl.pallas_call(functools.partial(swift_kernel, ring, lanes), out_shape=(j...]
where the time goes in v8:
time: 119 us
  Pallas kernels  118 us (99%)
    pallas_call x1, Pallas kernels, swift(): pl.pallas_call(functools.partial(swift_kernel, ring, lanes), out_shape=(j...  45.8 us
    pallas_call x1, Pallas kernels, steady(): pl.pallas_call(functools.partial(attend_kernel, ring, lanes), out_shape=(...  31 us
    pallas_call x1, Pallas kernels, steady(): pl.pallas_call(functools.partial(gather_kernel, ring), out_shape=jax.Shap...  29.2 us
    pallas_call x1, Pallas kernels, steady(): pl.pallas_call(functools.partial(merge_kernel, lanes), out_shape=jax.Shap...  11.9 us

profile of v8, /device:TPU:448, one launch (start us, length us, event | category | flops | bytes accessed | tf_op | source)
XLA Modules:
  0.0 119.2 jit_solution(14944944742121317626)
XLA Ops:
  0.0 0.0 copy-start
  0.0 0.0 copy-start.1
  0.0 0.0 copy-start.2
  0.0 0.0 copy-start.3
  0.0 45.8 %swift.1 = (bf16[64,1024]{1,0:T(8,128)(2,1)S(1)}, f32[1]{0:T(128)}) custom-call(bf16[256,1024]{1,0:T(8,128)(2,1)} %q_hbm.1, bf16[64,128]{1,0:T(8,128)(2,1)} %k_hbm.1, bf16[64,128]{1,0:T(8,128)(2,1)} %v_hbm.1, s32[8]{0:T(128)} %len_hbm.1), custom_call_target="tpu_custom_call" | custom-call | flops 10000000000 | bytes 10000000 | tf_op jit(solution)/shard_map/swift/pallas_call | solution.py:379
  46.4 0.0 copy-done
  46.4 0.0 copy-done.1
  46.4 0.0 copy-done.2
  46.4 0.0 copy-done.3
  46.5 72.0 %conditional.1 = (bf16[64,1024]{1,0:T(8,128)(2,1)S(1)}) conditional(s32[]{:T(128)} %bitcast, (bf16[64,128]{1,0:T(8,128)(2,1)S(1)}, bf16[64,128]{1,0:T(8,128)(2,1)S(1)}, bf16[256,1024]{1,0:T(8,128)(2,1)S(1)}, s32[8]{0:T(128)S(1)}) %tuple.20, bf16[64,1024]{1,0:T(8,128)(2,1)S(1)} %get-tuple-element.26), branch_computations={%region_0.0_spmd, %region_1.0_spmd} | conditional | bytes 8 | solution.py:776
  46.5 29.2 %gather.1.kv = bf16[2,8,2,512,128]{4,3,2,1,0:T(8,128)(2,1)S(1)} custom-call(bf16[64,128]{1,0:T(8,128)(2,1)S(1)} %get-tuple-element.18.k_ref, bf16[64,128]{1,0:T(8,128)(2,1)S(1)} %get-tuple-element.19.v_ref), custom_call_target="tpu_custom_call" | custom-call | tf_op jit(solution)/shard_map/cond/branch_0_fun/gather/pallas_call | solution.py:721
  75.6 31.0 %attend.1 = (bf16[4,64,1024]{2,1,0:T(8,128)(2,1)S(1)}, f32[8,256]{1,0:T(8,128)S(1)}) custom-call(bf16[256,1024]{1,0:T(8,128)(2,1)S(1)} %get-tuple-element.17.q_ref, bf16[2,8,2,512,128]{4,3,2,1,0:T(8,128)(2,1)S(1)} %gather.1.kv, s32[8]{0:T(128)S(1)} %get-tuple-element.20.lens), custom_call_target="tpu_custom_call" | custom-call | tf_op jit(solution)/shard_map/cond/branch_0_fun/attend/pallas_call | solution.py:735
  106.6 11.9 %merge.1 = bf16[64,1024]{1,0:T(8,128)(2,1)S(1)} custom-call(bf16[4,64,1024]{2,1,0:T(8,128)(2,1)S(1)} %get-tuple-element.21.obuf, f32[8,256]{1,0:T(8,128)S(1)} %get-tuple-element.22.lbuf), custom_call_target="tpu_custom_call" | custom-call | tf_op jit(solution)/shard_map/cond/branch_0_fun/merge/pallas_call | solution.py:753
  118.5 0.7 copy.10
Async XLA Ops:
  0.0 46.4 %copy-start = (bf16[256,1024]{1,0:T(8,128)(2,1)S(1)}, bf16[256,1024]{1,0:T(8,128)(2,1)}, u32[]{:S(2)}) copy-start(bf16[256,1024]{1,0:T(8,128)(2,1)} %q_hbm.1) | copy-start | bytes 1572868
  0.0 46.4 %copy-start.1 = (bf16[64,128]{1,0:T(8,128)(2,1)S(1)}, bf16[64,128]{1,0:T(8,128)(2,1)}, u32[]{:S(2)}) copy-start(bf16[64,128]{1,0:T(8,128)(2,1)} %k_hbm.1) | copy-start | bytes 49156
  0.0 46.4 %copy-start.2 = (bf16[64,128]{1,0:T(8,128)(2,1)S(1)}, bf16[64,128]{1,0:T(8,128)(2,1)}, u32[]{:S(2)}) copy-start(bf16[64,128]{1,0:T(8,128)(2,1)} %v_hbm.1) | copy-start | bytes 49156
  0.0 46.4 %copy-start.3 = (s32[8]{0:T(128)S(1)}, s32[8]{0:T(128)}, u32[]{:S(2)}) copy-start(s32[8]{0:T(128)} %len_hbm.1) | copy-start | bytes 100

commit v9 on v8

--- a/solution.py
+++ b/solution.py
@@ -30,8 +30,8 @@
 
 def swift_kernel(
     ring, lanes, q_hbm, k_hbm, v_hbm, len_hbm, out_ref, bound_ref,
-    q_in, k_in, v_in, lens, stage, kv, kfeat, qcat, acc, tot, obuf, rbuf, sums, mixing,
-    s_in, s_one, r_one, s_fwd, r_fwd, s_bwd, r_bwd, s_sib, r_sib, s_cross, r_cross, s_out, r_out, s_sum, r_sum,
+    q_in, k_in, v_in, lens, stage, kv, kfeat, qcat, acc, tot, obuf, rbuf, sums, most, mixing,
+    s_in, s_one, r_one, s_fwd, r_fwd, s_bwd, r_bwd, s_sib, r_sib, s_cross, r_cross, s_out, r_out, s_sum, r_sum, s_most, r_most,
 ):
     half = ring // 2
     rows = q_in.shape[0]
@@ -118,7 +118,6 @@
                 bwd_copy(s + 1, p2 + s, i).start()
             if s + 1 == half:
                 cross_copy(c, p2 - s + 2 * i * s, i).start()
-        for i in range(2):
             sib_copy(2 * s - 1, c, p2 - s, i).start()
             sib_copy(2 * s, c, p2 + s, i).start()
 
@@ -234,7 +233,13 @@
         def _():
             sib_arrived(s)
 
-        @pl.when((cc == 1) | seen(b))
+        short = (cc == 1) & (z < half)
+
+        @pl.when(short)
+        def _():
+            run([(g, 1, b, chunk // 2) for g in range(HEADS // 2)])
+
+        @pl.when(jnp.logical_not(short) & ((cc == 1) | seen(b)))
         def _():
             run([(g, cc, b, chunk) for g in range(HEADS // 2)])
 
@@ -270,6 +275,12 @@
         return pltpu.make_async_remote_copy(
             src_ref=sums.at[0], dst_ref=sums.at[d],
             send_sem=s_sum.at[d], recv_sem=r_sum.at[d], device_id={"ka": peer(d)}, device_id_type=MESH,
+        )
+
+    def most_copy(d):
+        return pltpu.make_async_remote_copy(
+            src_ref=most.at[0], dst_ref=most.at[d],
+            send_sem=s_most.at[d], recv_sem=r_most.at[d], device_id={"ka": peer(d)}, device_id_type=MESH,
         )
 
     shifts = (1 - half, half - 1, half)
@@ -292,6 +303,8 @@
 
     def finish_all(work):
         lax.fori_loop(0, HEADS // 2, functools.partial(finish, work), 0)
+        for d in range(1, lanes):
+            sum_copy(d).start()
 
     @pl.when(z >= half)
     def _():
@@ -331,9 +344,9 @@
     met = functools.reduce(jnp.maximum, met).astype(jnp.float32)
     for i in range(2):
         row = met[i * EXTRA // 2 : i * EXTRA // 2 + 1, :]
-        sums[0, HEADS + i] = jnp.concatenate([row] * (rows // LANES), axis=1)
+        most[0, i] = row
     for d in range(1, lanes):
-        sum_copy(d).start()
+        most_copy(d).start()
     for d in range(1, ring):
         one_copy(d, p1).wait_send()
     for i in range(2):
@@ -351,8 +364,6 @@
     whole = functools.reduce(jnp.add, [sums[d] for d in range(lanes)])
     share = [1.0 / whole[h] for h in range(HEADS)] + [jnp.zeros((LANES - HEADS, rows), jnp.float32)]
     mixing[...] = jnp.concatenate(share, axis=0).T
-    met = functools.reduce(jnp.maximum, [sums[d] for d in range(lanes)])
-    bound_ref[0] = jnp.max(met[HEADS] * met[HEADS + 1])
     mix = mixing[pl.ds(pl.multiple_of(x * own, own), own), :]
     for h in range(HEADS):
         cols = slice(h * DIM, (h + 1) * DIM)
@@ -364,7 +375,12 @@
         out_ref[:, cols] = (mixed * mix[:, h : h + 1]).astype(out_ref.dtype)
 
     for d in range(1, lanes):
+        most_copy(d).wait_recv()
+    met = functools.reduce(jnp.maximum, [most[d] for d in range(lanes)])
+    bound_ref[0] = jnp.max(met[0] * met[1])
+    for d in range(1, lanes):
         sum_copy(d).wait_send()
+        most_copy(d).wait_send()
         for g in range(HEADS // 2):
             out_copy(d, g).wait_send()
 
@@ -397,13 +413,15 @@
             pltpu.VMEM((HEADS // 2, 1, 2 * rows), jnp.float32),
             pltpu.VMEM(parts, jnp.bfloat16),
             pltpu.VMEM(parts, jnp.bfloat16),
-            pltpu.VMEM((lanes, HEADS + 2, 1, rows), jnp.float32),
+            pltpu.VMEM((lanes, HEADS, 1, rows), jnp.float32),
+            pltpu.VMEM((lanes, 2, 1, LANES), jnp.float32),
             pltpu.VMEM((rows, LANES), jnp.float32),
             sems((4,)),
             sems((ring - 1,)), sems((ring - 1,)),
             sems((half, 2)), sems((half, 2)), sems((half, 2)), sems((half, 2)),
             sems((2 * half - 1, 2)), sems((2 * half - 1, 2)), sems((2,)), sems((2,)),
             sems((lanes, HEADS // 2)), sems((lanes, HEADS // 2)),
+            sems((lanes,)), sems((lanes,)),
             sems((lanes,)), sems((lanes,)),
         ],
         compiler_params=pltpu.CompilerParams(

time: 119 us -> 120 us (level)
  no operation moved by 1% of the time
where the time goes in v9:
time: 120 us; the launch traced here: 119 us
  Pallas kernels  118 us (98%)
    pallas_call x1, Pallas kernels, swift(): pl.pallas_call(functools.partial(swift_kernel, ring, lanes), out_shape=(j...  45.9 us
    pallas_call x1, Pallas kernels, steady(): pl.pallas_call(functools.partial(attend_kernel, ring, lanes), out_shape=(...  31 us
    pallas_call x1, Pallas kernels, steady(): pl.pallas_call(functools.partial(gather_kernel, ring), out_shape=jax.Shap...  29.2 us
    pallas_call x1, Pallas kernels, steady(): pl.pallas_call(functools.partial(merge_kernel, lanes), out_shape=jax.Shap...  11.9 us

profile of v9, /device:TPU:448, one launch (start us, length us, event | category | flops | bytes accessed | tf_op | source)
XLA Modules:
  0.0 119.3 jit_solution(1669038180214563361)
XLA Ops:
  0.0 0.0 copy-start
  0.0 0.0 copy-start.1
  0.0 0.0 copy-start.2
  0.0 0.0 copy-start.3
  0.0 45.9 %swift.1 = (bf16[64,1024]{1,0:T(8,128)(2,1)S(1)}, f32[1]{0:T(128)}) custom-call(bf16[256,1024]{1,0:T(8,128)(2,1)} %q_hbm.1, bf16[64,128]{1,0:T(8,128)(2,1)} %k_hbm.1, bf16[64,128]{1,0:T(8,128)(2,1)} %v_hbm.1, s32[8]{0:T(128)} %len_hbm.1), custom_call_target="tpu_custom_call" | custom-call | flops 10000000000 | bytes 10000000 | tf_op jit(solution)/shard_map/swift/pallas_call | solution.py:395
  46.5 0.0 copy-done
  46.5 0.0 copy-done.1
  46.5 0.0 copy-done.2
  46.6 0.0 copy-done.3
  46.6 72.1 %conditional.1 = (bf16[64,1024]{1,0:T(8,128)(2,1)S(1)}) conditional(s32[]{:T(128)} %bitcast, (bf16[64,128]{1,0:T(8,128)(2,1)S(1)}, bf16[64,128]{1,0:T(8,128)(2,1)S(1)}, bf16[256,1024]{1,0:T(8,128)(2,1)S(1)}, s32[8]{0:T(128)S(1)}) %tuple.20, bf16[64,1024]{1,0:T(8,128)(2,1)S(1)} %get-tuple-element.26), branch_computations={%region_0.0_spmd, %region_1.0_spmd} | conditional | bytes 8 | solution.py:794
  46.6 29.2 %gather.1.kv = bf16[2,8,2,512,128]{4,3,2,1,0:T(8,128)(2,1)S(1)} custom-call(bf16[64,128]{1,0:T(8,128)(2,1)S(1)} %get-tuple-element.18.k_ref, bf16[64,128]{1,0:T(8,128)(2,1)S(1)} %get-tuple-element.19.v_ref), custom_call_target="tpu_custom_call" | custom-call | tf_op jit(solution)/shard_map/cond/branch_0_fun/gather/pallas_call | solution.py:739
  75.7 31.0 %attend.1 = (bf16[4,64,1024]{2,1,0:T(8,128)(2,1)S(1)}, f32[8,256]{1,0:T(8,128)S(1)}) custom-call(bf16[256,1024]{1,0:T(8,128)(2,1)S(1)} %get-tuple-element.17.q_ref, bf16[2,8,2,512,128]{4,3,2,1,0:T(8,128)(2,1)S(1)} %gather.1.kv, s32[8]{0:T(128)S(1)} %get-tuple-element.20.lens), custom_call_target="tpu_custom_call" | custom-call | tf_op jit(solution)/shard_map/cond/branch_0_fun/attend/pallas_call | solution.py:753
  106.7 11.9 %merge.1 = bf16[64,1024]{1,0:T(8,128)(2,1)S(1)} custom-call(bf16[4,64,1024]{2,1,0:T(8,128)(2,1)S(1)} %get-tuple-element.21.obuf, f32[8,256]{1,0:T(8,128)S(1)} %get-tuple-element.22.lbuf), custom_call_target="tpu_custom_call" | custom-call | tf_op jit(solution)/shard_map/cond/branch_0_fun/merge/pallas_call | solution.py:771
  118.6 0.7 copy.10
Async XLA Ops:
  0.0 46.5 %copy-start = (bf16[256,1024]{1,0:T(8,128)(2,1)S(1)}, bf16[256,1024]{1,0:T(8,128)(2,1)}, u32[]{:S(2)}) copy-start(bf16[256,1024]{1,0:T(8,128)(2,1)} %q_hbm.1) | copy-start | bytes 1572868
  0.0 46.5 %copy-start.1 = (bf16[64,128]{1,0:T(8,128)(2,1)S(1)}, bf16[64,128]{1,0:T(8,128)(2,1)}, u32[]{:S(2)}) copy-start(bf16[64,128]{1,0:T(8,128)(2,1)} %k_hbm.1) | copy-start | bytes 49156
  0.0 46.5 %copy-start.2 = (bf16[64,128]{1,0:T(8,128)(2,1)S(1)}, bf16[64,128]{1,0:T(8,128)(2,1)}, u32[]{:S(2)}) copy-start(bf16[64,128]{1,0:T(8,128)(2,1)} %v_hbm.1) | copy-start | bytes 49156
  0.0 46.5 %copy-start.3 = (s32[8]{0:T(128)S(1)}, s32[8]{0:T(128)}, u32[]{:S(2)}) copy-start(s32[8]{0:T(128)} %len_hbm.1) | copy-start | bytes 100

commit v10 on v9

--- a/solution.py
+++ b/solution.py
@@ -55,6 +55,13 @@
 
     sibling = {"pb": me + 1 - 2 * c}
 
+    moves = [
+        pltpu.make_async_copy(src, dst, s_in.at[n])
+        for n, (src, dst) in enumerate(((k_hbm, k_in), (v_hbm, v_in), (len_hbm, lens), (q_hbm, q_in)))
+    ]
+    for move in moves:
+        move.start()
+
     barrier = pltpu.get_barrier_semaphore()
     partners = [device(p1 + d, p2) for d in range(1, ring)]
     partners += [device(p1, p2 + d, core) for d in (1, -1) for core in (c, 1 - c)]
@@ -62,12 +69,6 @@
     partners += [sibling] + [{"ka": lax.rem(x + d, lanes)} for d in range(1, lanes)]
     for partner in partners:
         pl.semaphore_signal(barrier, inc=1, device_id=partner, device_id_type=MESH)
-    moves = [
-        pltpu.make_async_copy(src, dst, s_in.at[n])
-        for n, (src, dst) in enumerate(((k_hbm, k_in), (v_hbm, v_in), (len_hbm, lens), (q_hbm, q_in)))
-    ]
-    for move in moves:
-        move.start()
     moves[0].wait()
     moves[1].wait()
     stage[p1, :own] = k_in[...]

time: 120 us -> 120 us (level)
  no operation moved by 1% of the time
where the time goes in v10:
time: 120 us
  Pallas kernels  118 us (98%)
    pallas_call x1, Pallas kernels, swift(): pl.pallas_call(functools.partial(swift_kernel, ring, lanes), out_shape=(j...  46 us
    pallas_call x1, Pallas kernels, steady(): pl.pallas_call(functools.partial(attend_kernel, ring, lanes), out_shape=(...  31 us
    pallas_call x1, Pallas kernels, steady(): pl.pallas_call(functools.partial(gather_kernel, ring), out_shape=jax.Shap...  29.4 us
    pallas_call x1, Pallas kernels, steady(): pl.pallas_call(functools.partial(merge_kernel, lanes), out_shape=jax.Shap...  11.9 us

profile of v10, /device:TPU:448, one launch (start us, length us, event | category | flops | bytes accessed | tf_op | source)
XLA Modules:
  0.0 119.6 jit_solution(251849993430484416)
XLA Ops:
  0.0 0.0 copy-start
  0.0 0.0 copy-start.1
  0.0 0.0 copy-start.2
  0.0 0.0 copy-start.3
  0.0 46.0 %swift.1 = (bf16[64,1024]{1,0:T(8,128)(2,1)S(1)}, f32[1]{0:T(128)}) custom-call(bf16[256,1024]{1,0:T(8,128)(2,1)} %q_hbm.1, bf16[64,128]{1,0:T(8,128)(2,1)} %k_hbm.1, bf16[64,128]{1,0:T(8,128)(2,1)} %v_hbm.1, s32[8]{0:T(128)} %len_hbm.1), custom_call_target="tpu_custom_call" | custom-call | flops 10000000000 | bytes 10000000 | tf_op jit(solution)/shard_map/swift/pallas_call | solution.py:396
  46.6 0.0 copy-done
  46.6 0.0 copy-done.1
  46.6 0.0 copy-done.2
  46.6 0.0 copy-done.3
  46.6 72.3 %conditional.1 = (bf16[64,1024]{1,0:T(8,128)(2,1)S(1)}) conditional(s32[]{:T(128)} %bitcast, (bf16[64,128]{1,0:T(8,128)(2,1)S(1)}, bf16[64,128]{1,0:T(8,128)(2,1)S(1)}, bf16[256,1024]{1,0:T(8,128)(2,1)S(1)}, s32[8]{0:T(128)S(1)}) %tuple.20, bf16[64,1024]{1,0:T(8,128)(2,1)S(1)} %get-tuple-element.26), branch_computations={%region_0.0_spmd, %region_1.0_spmd} | conditional | bytes 8 | solution.py:795
  46.6 29.4 %gather.1.kv = bf16[2,8,2,512,128]{4,3,2,1,0:T(8,128)(2,1)S(1)} custom-call(bf16[64,128]{1,0:T(8,128)(2,1)S(1)} %get-tuple-element.18.k_ref, bf16[64,128]{1,0:T(8,128)(2,1)S(1)} %get-tuple-element.19.v_ref), custom_call_target="tpu_custom_call" | custom-call | tf_op jit(solution)/shard_map/cond/branch_0_fun/gather/pallas_call | solution.py:740
  76.1 31.0 %attend.1 = (bf16[4,64,1024]{2,1,0:T(8,128)(2,1)S(1)}, f32[8,256]{1,0:T(8,128)S(1)}) custom-call(bf16[256,1024]{1,0:T(8,128)(2,1)S(1)} %get-tuple-element.17.q_ref, bf16[2,8,2,512,128]{4,3,2,1,0:T(8,128)(2,1)S(1)} %gather.1.kv, s32[8]{0:T(128)S(1)} %get-tuple-element.20.lens), custom_call_target="tpu_custom_call" | custom-call | tf_op jit(solution)/shard_map/cond/branch_0_fun/attend/pallas_call | solution.py:754
  107.0 11.9 %merge.1 = bf16[64,1024]{1,0:T(8,128)(2,1)S(1)} custom-call(bf16[4,64,1024]{2,1,0:T(8,128)(2,1)S(1)} %get-tuple-element.21.obuf, f32[8,256]{1,0:T(8,128)S(1)} %get-tuple-element.22.lbuf), custom_call_target="tpu_custom_call" | custom-call | tf_op jit(solution)/shard_map/cond/branch_0_fun/merge/pallas_call | solution.py:772
  118.9 0.7 copy.10
Async XLA Ops:
  0.0 46.6 %copy-start = (bf16[256,1024]{1,0:T(8,128)(2,1)S(1)}, bf16[256,1024]{1,0:T(8,128)(2,1)}, u32[]{:S(2)}) copy-start(bf16[256,1024]{1,0:T(8,128)(2,1)} %q_hbm.1) | copy-start | bytes 1572868
  0.0 46.6 %copy-start.1 = (bf16[64,128]{1,0:T(8,128)(2,1)S(1)}, bf16[64,128]{1,0:T(8,128)(2,1)}, u32[]{:S(2)}) copy-start(bf16[64,128]{1,0:T(8,128)(2,1)} %k_hbm.1) | copy-start | bytes 49156
  0.0 46.6 %copy-start.2 = (bf16[64,128]{1,0:T(8,128)(2,1)S(1)}, bf16[64,128]{1,0:T(8,128)(2,1)}, u32[]{:S(2)}) copy-start(bf16[64,128]{1,0:T(8,128)(2,1)} %v_hbm.1) | copy-start | bytes 49156
  0.0 46.6 %copy-start.3 = (s32[8]{0:T(128)S(1)}, s32[8]{0:T(128)}, u32[]{:S(2)}) copy-start(s32[8]{0:T(128)} %len_hbm.1) | copy-start | bytes 100
